TPU v7x, 256 devices: a whole 4x4x8 slice. The times are simulated.
256 devices in a mesh: gx: 8 (over x, core), gy: 8 (over z), gz: 4 (over y).
Axes of the slice: x: 4, y: 4, z: 8, core: 2. Of those that a mesh axis runs over, the one named last changes fastest.
Arguments:
- spectrum: bfloat16 [256, 256, 32, 256], P('gx', 'gy', 'gz'), may hold values from 0.049804688 to 2
- wind_east: float32 [256, 256, 32], P('gx', 'gy', 'gz'), may hold values from -0.45 to 0.45
- wind_north: float32 [256, 256, 32], P('gx', 'gy', 'gz'), may hold values from -0.45 to 0.45
- fall_rate: float32 [32, 256], P('gz'), may hold values from 0.006 to 12
- cloud_cells: int32 [8, 8, 4, 64, 16], P('gx', 'gy', 'gz'), may hold values from 0 to 8191, as said below
- block_target: int32 [8, 8, 4, 64], P(None, None, 'gz'), may hold values from 0 to 64, as said below
- pair_inputs: bfloat16 [256, 2048], replicated, may hold values from -0.375 to 0.375
- pair_outputs: bfloat16 [1024, 256], replicated, may hold values from -0.1875 to 0.1875
- loss_kernel: bfloat16 [256, 256], replicated, may hold values from 0 to 0.00390625
- fragments: bfloat16 [256, 256], replicated, may hold values from 0 to 0.0078125
Outputs:
- settled: bfloat16 [256, 256, 32, 256], P('gx', 'gy', 'gz')
Inputs may be any that keep to these rules, and one draw needn't show every extreme that they name: `cloud_cells`: entry [i, j, k, b, :] lists the local cell numbers (x * 32 + y) * 8 + z of block b of the device at mesh index (i, j, k); the 1024 entries of one device are distinct. `block_target`: entry [i, j, k, b] below 64 is the flat index i2 * (devices along gy) + j2 of the device (i2, j2, k) that works on block b of device (i, j, k); 64 marks a block without cloud. In each gz index the cloudy blocks number 64 * 32 in all, a device holds 1 to 64 of them, every device of the plane is named exactly 32 times, and by at most 1 block of any one device.
All inputs are finite; a program needn't handle non-finite values.
Results may differ from a plain program's by a relative error of at most 0.0032.
Values may be sent and summed in bfloat16 or wider, within the bound.
No kernel may reach another device: no remote copies, remote signals or barrier semaphores. Data moves between devices by JAX's collectives and lax.ppermute only.
A program may use at most 128 MiB of HBM per device.

v0:
```python
import jax
import jax.numpy as jnp
from jax import lax
from jax.sharding import PartitionSpec as P


def padded_2(x, sides, width):
    edges = {}
    for axis, dim in sides:
        size, length = (lax.axis_size(axis), x.shape[dim])
        up = [(i, (i + 1) % size) for i in range(size)]
        last = lax.slice_in_dim(x, length - width, length, axis=dim)
        initial = lax.slice_in_dim(x, 0, width, axis=dim)
        edges[dim] = (
            lax.ppermute(last, axis, up),
            lax.ppermute(initial, axis, [(b, a) for a, b in up]),
        )
    done = []
    for _, dim in sides:
        low, high = edges[dim]
        around = [(width, width) if d in done else (0, 0) for d in range(x.ndim)]
        x = jnp.concatenate([jnp.pad(low, around), x, jnp.pad(high, around)], axis=dim)
        done.append(dim)
    return x


def collide(cloud_rows, pair_inputs, pair_outputs, loss_kernel, fragments):
    pair_count = pair_outputs.shape[0]
    linear = jnp.dot(cloud_rows, pair_inputs, preferred_element_type=jnp.float32)
    products = (linear[:, :pair_count] * linear[:, pair_count:]).astype(jnp.bfloat16)
    decline = jnp.dot(cloud_rows, loss_kernel, preferred_element_type=jnp.float32)
    losses = cloud_rows.astype(jnp.float32) * decline
    gained = jnp.dot(products, pair_outputs, preferred_element_type=jnp.float32)
    gained = gained + jnp.dot(
        losses.astype(jnp.bfloat16), fragments, preferred_element_type=jnp.float32
    )
    return (gained - losses).astype(jnp.bfloat16)


def advect(spectrum, wind_east, wind_north):
    padded = padded_2(spectrum, (("gx", 0), ("gy", 1)), 1)
    centre = spectrum.astype(jnp.float32)
    from_west = padded[:-2, 1:-1].astype(jnp.float32)
    from_east = padded[2:, 1:-1].astype(jnp.float32)
    from_south = padded[1:-1, :-2].astype(jnp.float32)
    from_north = padded[1:-1, 2:].astype(jnp.float32)
    east_rate = wind_east[..., None]
    north_rate = wind_north[..., None]
    return (
        centre
        - jnp.maximum(east_rate, 0.0) * (centre - from_west)
        - jnp.minimum(east_rate, 0.0) * (from_east - centre)
        - jnp.maximum(north_rate, 0.0) * (centre - from_south)
        - jnp.minimum(north_rate, 0.0) * (from_north - centre)
    )


def segment_maps(fall_rate):
    levels, channels = fall_rate.shape
    inverse = 1.0 / (1.0 + fall_rate)
    rows = [None] * levels
    gains = [None] * levels
    above_row = jnp.zeros((levels, channels), jnp.float32)
    above_gain = jnp.ones((channels,), jnp.float32)
    level_ids = jnp.arange(levels)[:, None]
    for level_index in reversed(range(levels)):
        own_row = jnp.where(level_ids == level_index, 1.0, 0.0).astype(jnp.float32)
        row = inverse[level_index][None, :] * (own_row + above_row)
        gain = inverse[level_index] * above_gain
        rows[level_index] = row
        gains[level_index] = gain
        above_row = fall_rate[level_index][None, :] * row
        above_gain = fall_rate[level_index] * gain
    return (jnp.stack(rows, axis=0), jnp.stack(gains, axis=0), above_row, above_gain)


def body(
    spectrum,
    wind_east,
    wind_north,
    fall_rate,
    cloud_cells,
    block_target,
    pair_inputs,
    pair_outputs,
    loss_kernel,
    fragments,
):
    size_x, size_y, size_z, channels = spectrum.shape
    number_of_cells = size_x * size_y * size_z
    advected = advect(spectrum, wind_east, wind_north)
    flat_cells = advected.reshape(number_of_cells, channels)
    blocks_total = cloud_cells.shape[3]
    block_cells = cloud_cells.shape[4]
    cell_ids = cloud_cells.reshape(blocks_total * block_cells)
    blocks = flat_cells[cell_ids].astype(jnp.bfloat16).reshape(blocks_total, block_cells, channels)
    plane_size = lax.axis_size("gx") * lax.axis_size("gy")
    own_index = lax.axis_index("gx") * lax.axis_size("gy") + lax.axis_index("gy")
    routes = block_target.reshape(plane_size, blocks_total)
    own_targets = lax.dynamic_index_in_dim(routes, own_index, 0, keepdims=False)
    active = own_targets < plane_size
    zero_value = jnp.zeros((), jnp.bfloat16)
    computed = collide(
        blocks.reshape(-1, channels), pair_inputs, pair_outputs, loss_kernel, fragments
    )
    tendency = jnp.where(
        active[:, None, None], computed.reshape(blocks_total, block_cells, channels), zero_value
    )
    moist_field = (
        flat_cells.at[cell_ids]
        .add(tendency.reshape(-1, channels).astype(jnp.float32))
        .reshape(size_x, size_y, size_z, channels)
    )
    level_rows, level_gains, out_row, carried_gain = segment_maps(fall_rate)
    local_values = jnp.zeros((size_x, size_y, size_z, channels), jnp.float32)
    inflow = jnp.zeros((size_x, size_y, channels), jnp.float32)
    for source in range(size_z):
        source_level = moist_field[:, :, source : source + 1, :]
        local_values = local_values + source_level * level_rows[:, source, :]
        inflow = inflow + source_level[:, :, 0, :] * out_row[source]
    all_flux, all_gain = (
        lax.all_gather(inflow[None].astype(jnp.bfloat16), "gz", axis=0, tiled=True).astype(
            jnp.float32
        ),
        lax.all_gather(carried_gain[None].astype(jnp.bfloat16), "gz", axis=0, tiled=True).astype(
            jnp.float32
        ),
    )
    height = lax.axis_size("gz")
    own_level = lax.axis_index("gz")
    incoming = jnp.zeros_like(inflow)
    for upper in reversed(range(height)):
        incoming = jnp.where(
            upper > own_level, all_flux[upper] + all_gain[upper] * incoming, incoming
        )
    return (local_values + incoming[:, :, None, :] * level_gains).astype(jnp.bfloat16)


def solution(mesh):
    in_specs = (
        P("gx", "gy", "gz", None),
        P("gx", "gy", "gz"),
        P("gx", "gy", "gz"),
        P("gz", None),
        P("gx", "gy", "gz", None, None),
        P(None, None, "gz", None),
        P(),
        P(),
        P(),
        P(),
    )
    out_specs = P("gx", "gy", "gz", None)
    return jax.shard_map(body, mesh=mesh, in_specs=in_specs, out_specs=out_specs, check_vma=False)
```

profile of v0, /device:TPU:2, one launch (start us, length us, event | category | flops | bytes accessed | tf_op | source)
XLA Modules:
  0.0 160.1 jit_solution(9245047635911674080)
XLA Ops:
  6.5 1.8 %fusion.58 = (bf16[1,32,8,256]{3,2,1,0:T(8,128)(2,1)}, bf16[1,32,8,256]{3,2,1,0:T(8,128)(2,1)}) fusion(bf16[32,32,8,256]{3,2,1,0:T(8,128)(2,1)} %param.10), kind=kLoop, calls=%fused_computation.129 | loop fusion | bytes 524288 | tf_op jit(solution)/shard_map/slice | solution.py:13
  8.3 1.7 %collective-permute-start.1 = (bf16[1,32,8,256]{3,2,1,0:T(8,128)(2,1)}, bf16[1,32,8,256]{3,2,1,0:T(8,128)(2,1)S(1)}, u32[]{:S(2)}, u32[]{:S(2)}) collective-permute-start(bf16[1,32,8,256]{3,2,1,0:T(8,128)(2,1)} %get-tuple-element.23), channel_id=1, source_target_pairs={{32,0},{64,32},{96,64},{128,96},{160,128},{192,160},{224,192},{0,2... | collective-permute-start | bytes 393224 | tf_op jit(solution)/shard_map/ppermute | solution.py:16
  10.0 1.7 %fusion.57 = (bf16[32,1,8,256]{3,2,1,0:T(8,128)(2,1)}, bf16[32,1,8,256]{3,2,1,0:T(8,128)(2,1)}) fusion(bf16[32,32,8,256]{3,2,1,0:T(8,128)(2,1)} %param.10), kind=kLoop, calls=%fused_computation.128 | loop fusion | bytes 524288 | tf_op jit(solution)/shard_map/slice | solution.py:12
  11.7 1.9 %collective-permute-start.2 = (bf16[32,1,8,256]{3,2,1,0:T(8,128)(2,1)}, bf16[32,1,8,256]{3,2,1,0:T(8,128)(2,1)}, u32[]{:S(2)}, u32[]{:S(2)}) collective-permute-start(bf16[32,1,8,256]{3,2,1,0:T(8,128)(2,1)} %get-tuple-element.21), channel_id=1, source_target_pairs={{0,4},{4,8},{8,12},{12,16},{16,20},{20,24},{24,28},{28,0},{1,5},{5... | collective-permute-start | bytes 393224 | tf_op jit(solution)/shard_map/ppermute | solution.py:15
  13.7 3.9 %collective-permute-start.3 = (bf16[32,1,8,256]{3,2,1,0:T(8,128)(2,1)}, bf16[32,1,8,256]{3,2,1,0:T(8,128)(2,1)}, u32[]{:S(2)}, u32[]{:S(2)}) collective-permute-start(bf16[32,1,8,256]{3,2,1,0:T(8,128)(2,1)} %get-tuple-element.22), channel_id=1, source_target_pairs={{4,0},{8,4},{12,8},{16,12},{20,16},{24,20},{28,24},{0,28},{5,1},{9... | collective-permute-start | bytes 393224 | tf_op jit(solution)/shard_map/ppermute | solution.py:16
  17.6 0.7 add_divide_fusion
  18.3 0.6 fusion.62
  18.9 1.6 %convert_bitcast_fusion = (bf16[1,1,256]{2,1,0:T(2,128)(2,1)}, f32[1,256]{1,0:T(1,128)}, f32[1,256]{1,0:T(1,128)}, f32[1,256]{1,0:T(1,128)}, f32[1,256]{1,0:T(1,...) fusion(f32[8,256]{1,0:T(8,128)} %param.13, ...), kind=kLoop, calls=%fused_computation.119 | loop fusion | flops 4096 | bytes 27136
  20.5 1.6 fusion.61
  22.1 0.6 compare_select_fusion.1
  22.7 0.5 compare_select_fusion.3
  23.2 0.6 compare_select_fusion.5
  23.8 0.6 compare_select_fusion.7
  24.4 0.9 broadcast_maximum_fusion.1
  25.3 0.2 copy.39
  25.5 0.2 copy.40
  25.7 0.9 broadcast_maximum_fusion
  26.7 0.2 copy.41
  26.9 0.2 copy.42
  27.1 0.8 copy.43
  27.9 0.1 reshape.2557
  28.0 0.7 compare_bitcast_fusion
  28.7 0.1 broadcast_in_dim.53
  28.8 0.6 broadcast_in_dim.54
  29.4 1.6 constant_dynamic-update-slice_fusion.10
  31.0 0.8 multiply_multiply_fusion.1
  31.8 0.6 fusion.60
  32.5 1.4 constant_dynamic-update-slice_fusion.9
  33.9 0.6 broadcast_clamp_fusion
  34.5 2.5 %constant_dynamic-update-slice_fusion.1 = bf16[34,32,8,256]{3,2,1,0:T(8,128)(2,1)S(1)} fusion(bf16[34,32,8,256]{3,2,1,0:T(8,128)(2,1)S(1)} %constant_dynamic-update-slice_fusion.2, bf16[32,32,8,256]{3,2,1,0:T(8,128)(2,1)} %param.10), kind=kLoop, calls=%fused_computation.76 | loop fusion | bytes 8388608
  37.0 0.0 copy-start.19
  37.0 12.5 %fusion.3 = f32[32,32,8,256]{3,2,1,0:T(8,128)} fusion(bf16[32,32,8,256]{3,2,1,0:T(8,128)(2,1)S(1)} %copy-done.1, bf16[34,32,8,256]{3,2,1,0:T(8,128)(2,1)S(1)} %constant_dynamic-update-slice_fusion, bf16[32,1,8,256]{3,2,1,0:T(8,128)(2,1)} %collective-permute-done.3, bf16[32,1,8,256]{3,2,1,0:T(8,128)(2,1)} %collective-permute-done.2, ...), kind=kLoop, calls=%fused_computation.10 | loop fusion | flops 73400320 | bytes 17694720 | tf_op jit(solution)/shard_map/sub | solution.py:50
  49.5 7.4 %gather_fusion = bf16[1024,256]{1,0:T(8,128)(2,1)S(1)} fusion(f32[8192,256]{1,0:T(8,128)} %bitcast.160, s32[1024]{0:T(1024)} %broadcast_clamp_fusion), kind=kCustom, calls=%fused_computation | custom fusion | bytes 1052672 | tf_op jit(solution)/shard_map/gather | solution.py:96
  56.9 0.3 fusion.65
  57.3 1.3 fusion.64
  58.5 0.3 fusion.46
  58.9 1.0 fusion.26
  59.9 12.7 %scatter_fusion = f32[8192,256]{1,0:T(8,128)} fusion(f32[8192,256]{1,0:T(8,128)} %bitcast.161, s32[1024]{0:T(1024)S(1)} %bitcast.215, f32[1024,256]{1,0:T(8,128)S(1)} %fusion.26), kind=kCustom, calls=%fused_computation.1 | custom fusion | flops 262144 | bytes 3149824 | tf_op jit(solution)/shard_map/scatter-add | solution.py:111
  72.7 30.4 %fusion.56 = (f32[32,32,1,256]{3,2,1,0:T(1,128)S(1)}, f32[32,32,1,256]{3,2,1,0:T(1,128)S(1)}, f32[32,32,1,256]{3,2,1,0:T(1,128)S(1)}, f32[32,32,1,256]{3,2,1,0:T...) fusion(f32[32,32,8,256]{3,2,1,0:T(8,128)} %bitcast.162), kind=kLoop, calls=%fused_computation.127 | loop fusion | bytes 16777216 | tf_op jit(solution)/shard_map/slice | solution.py:118
  103.4 0.7 copy-done.2
  104.0 0.4 copy-done.4
  104.4 0.3 copy-done.6
  104.7 0.4 copy-done.7
  105.1 0.3 copy-done.8
  105.5 0.3 copy-done.9
  105.8 1.9 %fusion.38 = bf16[1,32,32,256]{3,2,1,0:T(8,128)(2,1)} fusion(f32[32,32,1,256]{3,2,1,0:T(1,128)S(1)} %get-tuple-element.20, f32[32,32,1,256]{3,2,1,0:T(1,128)S(1)} %get-tuple-element.14, f32[32,32,1,256]{3,2,1,0:T(1,128)S(1)} %get-tuple-element.15, f32[32,32,1,256]{3,2,1,0:T(1,128)S(1)} %get-tuple-element.16, f32[32,32,1,256]{3,2,1,0:T(1,128)S(1)} %get-tuple-element.17, ...), kind=kLoop, calls=%fused_computation.45 | loop fusion | flops 4194304 | bytes 8921088 | tf_op jit(solution)/shard_map/convert_element_type | solution.py:122
  107.7 0.0 all-gather.3.cloned.1.call-update
  107.9 0.1 constant_dynamic-update-slice_fusion.8
  108.0 10.0 %all-gather = bf16[4,1,256]{2,1,0:T(2,128)(2,1)S(1)} all-gather(bf16[1,1,256]{2,1,0:T(2,128)(2,1)S(1)} %copy-done.53), channel_id=1, replica_groups=mesh['gx'=8,'gy'=8,'gz'=4] {'gz'}, dimensions={0}, use_global_device_ids=true | all-gather | bytes 2560 | tf_op jit(solution)/shard_map/all_gather | solution.py:125
  118.0 0.1 constant_dynamic-update-slice_fusion.7
  118.1 0.1 constant_dynamic-update-slice_fusion.6
  118.2 0.1 constant_dynamic-update-slice_fusion.5
  118.2 0.1 constant_dynamic-update-slice_fusion.4
  118.3 0.1 constant_dynamic-update-slice_fusion.3
  118.7 3.4 %copy_bitcast_fusion.6 = (f32[32,32,256]{2,1,0:T(8,128)}, f32[32,32,256]{2,1,0:T(8,128)}) fusion(f32[32,32,1,256]{3,2,1,0:T(1,128)} %copy-done.9, f32[32,32,1,256]{3,2,1,0:T(1,128)} %copy-done.8), kind=kLoop, calls=%fused_computation.66 | loop fusion | bytes 4194304 | tf_op jit(solution)/shard_map/mul | solution.py:119
  122.1 3.1 %copy_bitcast_fusion.4 = (f32[32,32,256]{2,1,0:T(8,128)}, f32[32,32,256]{2,1,0:T(8,128)}) fusion(f32[32,32,1,256]{3,2,1,0:T(1,128)} %copy-done.6, f32[32,32,1,256]{3,2,1,0:T(1,128)} %copy-done.7), kind=kLoop, calls=%fused_computation.64 | loop fusion | bytes 4194304 | tf_op jit(solution)/shard_map/mul | solution.py:119
  125.2 1.5 copy_bitcast_fusion.2
  126.7 1.5 copy_bitcast_fusion
  128.2 13.4 %all-gather.3.cloned.1.call-done = bf16[4,32,32,256]{3,2,1,0:T(8,128)(2,1)} async-done(((bf16[1,32,32,256]{3,2,1,0:T(8,128)(2,1)}), bf16[4,32,32,256]{3,2,1,0:T(8,128)(2,1)}) %all-gather.3.cloned.1.call-update) | async-done | bytes 2097168 | tf_op jit(solution)/shard_map/all_gather | solution.py:122
  141.7 2.2 %convert_element_type.73 = f32[4,32,32,256]{3,2,1,0:T(8,128)S(1)} convert(bf16[4,32,32,256]{3,2,1,0:T(8,128)(2,1)} %all-gather.3.cloned.1.call-done) | non-fusion elementwise | flops 1048576 | bytes 6291456 | tf_op jit(solution)/shard_map/convert_element_type | solution.py:122
  143.9 0.6 fusion.36
  144.6 0.2 copy-done.16
  144.8 0.3 copy-done.17
  145.1 8.1 %add_convert_fusion = bf16[32,32,8,256]{3,2,1,0:T(8,128)(2,1)} fusion(f32[8,256]{1,0:T(8,128)S(1)} %stack.5, f32[32,32,256]{2,1,0:T(8,128)S(1)} %fusion.36, f32[8,256]{1,0:T(8,128)S(1)} %bitcast.226, f32[32,32,256]{2,1,0:T(8,128)S(1)} %copy-done.16, f32[8,256]{1,0:T(8,128)S(1)} %bitcast.227, f32[32,32,256]{2,1,0:T(8,128)S(1)} %copy-done.17, ...), kind=kLoop, calls=%fused_computation.16 | loop fusion | flops 37748736 | bytes 13705216 | tf_op jit(solution)/shard_map/convert_element_type | solution.py:136
  (121 shorter events, 0.4 us)
Async XLA Ops:
  6.5 50.7 %copy-start = (bf16[256,2048]{1,0:T(8,128)(2,1)S(1)}, bf16[256,2048]{1,0:T(8,128)(2,1)}, u32[]{:S(2)}) copy-start(bf16[256,2048]{1,0:T(8,128)(2,1)} %param.16) | copy-start | bytes 3145732
  6.5 135.1 %all-gather.3.cloned.1.call-start = ((), (), s32[]{:S(2)}) async-start(), calls=%async_computation | async-start | bytes 2621440 | tf_op jit(solution)/shard_map/all_gather | solution.py:122
  8.3 26.2 %collective-permute-start = (bf16[1,32,8,256]{3,2,1,0:T(8,128)(2,1)}, bf16[1,32,8,256]{3,2,1,0:T(8,128)(2,1)S(1)}, u32[]{:S(2)}, u32[]{:S(2)}) collective-permute-start(bf16[1,32,8,256]{3,2,1,0:T(8,128)(2,1)} %get-tuple-element.24), channel_id=1, source_target_pairs={{0,32},{32,64},{64,96},{96,128},{128,160},{160,192},{192,224},{224... | collective-permute-start | bytes 393224 | tf_op jit(solution)/shard_map/ppermute | solution.py:15
  8.3 28.7 %collective-permute-start.1 = (bf16[1,32,8,256]{3,2,1,0:T(8,128)(2,1)}, bf16[1,32,8,256]{3,2,1,0:T(8,128)(2,1)S(1)}, u32[]{:S(2)}, u32[]{:S(2)}) collective-permute-start(bf16[1,32,8,256]{3,2,1,0:T(8,128)(2,1)} %get-tuple-element.23), channel_id=1, source_target_pairs={{32,0},{64,32},{96,64},{128,96},{160,128},{192,160},{224,192},{0,2... | collective-permute-start | bytes 393224 | tf_op jit(solution)/shard_map/ppermute | solution.py:16
  11.7 25.3 %collective-permute-start.2 = (bf16[32,1,8,256]{3,2,1,0:T(8,128)(2,1)}, bf16[32,1,8,256]{3,2,1,0:T(8,128)(2,1)}, u32[]{:S(2)}, u32[]{:S(2)}) collective-permute-start(bf16[32,1,8,256]{3,2,1,0:T(8,128)(2,1)} %get-tuple-element.21), channel_id=1, source_target_pairs={{0,4},{4,8},{8,12},{12,16},{16,20},{20,24},{24,28},{28,0},{1,5},{5... | collective-permute-start | bytes 393224 | tf_op jit(solution)/shard_map/ppermute | solution.py:15
  13.7 23.4 %collective-permute-start.3 = (bf16[32,1,8,256]{3,2,1,0:T(8,128)(2,1)}, bf16[32,1,8,256]{3,2,1,0:T(8,128)(2,1)}, u32[]{:S(2)}, u32[]{:S(2)}) collective-permute-start(bf16[32,1,8,256]{3,2,1,0:T(8,128)(2,1)} %get-tuple-element.22), channel_id=1, source_target_pairs={{4,0},{8,4},{12,8},{16,12},{20,16},{24,20},{28,24},{0,28},{5,1},{9... | collective-permute-start | bytes 393224 | tf_op jit(solution)/shard_map/ppermute | solution.py:16
  28.0 9.0 %copy-start.26 = (s32[1024,1]{0,1:T(1,128)}, s32[1024,1]{0,1:T(1,128)S(1)}, u32[]{:S(2)}) copy-start(s32[1024,1]{0,1:T(1,128)S(1)} %compare_select_fusion) | copy-start | bytes 12292
  29.4 7.6 %copy-start.1 = (bf16[32,32,8,256]{3,2,1,0:T(8,128)(2,1)S(1)}, bf16[32,32,8,256]{3,2,1,0:T(8,128)(2,1)}, u32[]{:S(2)}) copy-start(bf16[32,32,8,256]{3,2,1,0:T(8,128)(2,1)} %param.10) | copy-start | bytes 12582916
  37.0 19.9 %copy-start.19 = (bf16[256,256]{1,0:T(8,128)(2,1)S(1)}, bf16[256,256]{1,0:T(8,128)(2,1)}, u32[]{:S(2)}) copy-start(bf16[256,256]{1,0:T(8,128)(2,1)} %param.18) | copy-start | bytes 393220
  49.5 9.0 %copy-start.20 = (bf16[256,256]{1,0:T(8,128)(2,1)S(1)}, bf16[256,256]{1,0:T(8,128)(2,1)}, u32[]{:S(2)}) copy-start(bf16[256,256]{1,0:T(8,128)(2,1)} %param.19) | copy-start | bytes 393220
  56.9 1.9 %copy-start.18 = (bf16[1024,256]{1,0:T(8,128)(2,1)S(1)}, bf16[1024,256]{1,0:T(8,128)(2,1)}, u32[]{:S(2)}) copy-start(bf16[1024,256]{1,0:T(8,128)(2,1)} %param.17) | copy-start | bytes 1572868
  56.9 1.9 %copy-start.45 = (pred[1024]{0:T(1024)(128)(4,1)S(1)}, pred[1024]{0:T(1024)(128)(4,1)}, u32[]{:S(2)}) copy-start(pred[1024]{0:T(1024)(128)(4,1)} %broadcast_in_dim.54) | copy-start | bytes 3076
  58.5 1.4 copy-start.27
  72.6 33.1 %copy-start.37 = (f32[1,256]{1,0:T(1,128)S(1)}, f32[1,256]{1,0:T(1,128)}, u32[]{:S(2)}) copy-start(f32[1,256]{1,0:T(1,128)} %get-tuple-element.37) | copy-start | bytes 3076
  72.6 33.1 %copy-start.38 = (f32[1,256]{1,0:T(1,128)S(1)}, f32[1,256]{1,0:T(1,128)}, u32[]{:S(2)}) copy-start(f32[1,256]{1,0:T(1,128)} %get-tuple-element.38) | copy-start | bytes 3076
  72.6 33.1 %copy-start.39 = (f32[1,256]{1,0:T(1,128)S(1)}, f32[1,256]{1,0:T(1,128)}, u32[]{:S(2)}) copy-start(f32[1,256]{1,0:T(1,128)} %get-tuple-element.39) | copy-start | bytes 3076
  72.6 33.1 %copy-start.40 = (f32[1,256]{1,0:T(1,128)S(1)}, f32[1,256]{1,0:T(1,128)}, u32[]{:S(2)}) copy-start(f32[1,256]{1,0:T(1,128)} %get-tuple-element.40) | copy-start | bytes 3076
  72.7 33.1 %copy-start.41 = (f32[1,256]{1,0:T(1,128)S(1)}, f32[1,256]{1,0:T(1,128)}, u32[]{:S(2)}) copy-start(f32[1,256]{1,0:T(1,128)} %get-tuple-element.41) | copy-start | bytes 3076
  72.7 33.1 %copy-start.42 = (f32[1,256]{1,0:T(1,128)S(1)}, f32[1,256]{1,0:T(1,128)}, u32[]{:S(2)}) copy-start(f32[1,256]{1,0:T(1,128)} %get-tuple-element.42) | copy-start | bytes 3076
  72.7 33.1 %copy-start.43 = (f32[1,256]{1,0:T(1,128)S(1)}, f32[1,256]{1,0:T(1,128)}, u32[]{:S(2)}) copy-start(f32[1,256]{1,0:T(1,128)} %get-tuple-element.43) | copy-start | bytes 3076
  72.7 33.1 %copy-start.44 = (f32[1,256]{1,0:T(1,128)S(1)}, f32[1,256]{1,0:T(1,128)}, u32[]{:S(2)}) copy-start(f32[1,256]{1,0:T(1,128)} %get-tuple-element.44) | copy-start | bytes 3076
  103.1 1.0 copy-start.2
  103.1 1.3 copy-start.4
  103.1 1.6 %copy-start.6 = (f32[32,32,1,256]{3,2,1,0:T(1,128)}, f32[32,32,1,256]{3,2,1,0:T(1,128)S(1)}, u32[]{:S(2)}) copy-start(f32[32,32,1,256]{3,2,1,0:T(1,128)S(1)} %get-tuple-element.17) | copy-start | bytes 3145732
  103.1 2.0 %copy-start.7 = (f32[32,32,1,256]{3,2,1,0:T(1,128)}, f32[32,32,1,256]{3,2,1,0:T(1,128)S(1)}, u32[]{:S(2)}) copy-start(f32[32,32,1,256]{3,2,1,0:T(1,128)S(1)} %get-tuple-element.18) | copy-start | bytes 3145732
  103.1 2.3 %copy-start.8 = (f32[32,32,1,256]{3,2,1,0:T(1,128)}, f32[32,32,1,256]{3,2,1,0:T(1,128)S(1)}, u32[]{:S(2)}) copy-start(f32[32,32,1,256]{3,2,1,0:T(1,128)S(1)} %get-tuple-element.13) | copy-start | bytes 3145732
  103.1 2.6 %copy-start.9 = (f32[32,32,1,256]{3,2,1,0:T(1,128)}, f32[32,32,1,256]{3,2,1,0:T(1,128)S(1)}, u32[]{:S(2)}) copy-start(f32[32,32,1,256]{3,2,1,0:T(1,128)S(1)} %get-tuple-element.19) | copy-start | bytes 3145732
  103.1 4.6 %copy-start.21 = (f32[8,8,256]{2,1,0:T(8,128)S(1)}, f32[8,8,256]{2,1,0:T(8,128)}, u32[]{:S(2)}) copy-start(f32[8,8,256]{2,1,0:T(8,128)} %constant_dynamic-update-slice_fusion.9) | copy-start | bytes 196612
  103.1 4.6 %copy-start.22 = (f32[1,256]{1,0:T(1,128)S(1)}, f32[1,256]{1,0:T(1,128)}, u32[]{:S(2)}) copy-start(f32[1,256]{1,0:T(1,128)} %get-tuple-element.58) | copy-start | bytes 3076
  103.2 4.6 %copy-start.23 = (f32[1,256]{1,0:T(1,128)S(1)}, f32[1,256]{1,0:T(1,128)}, u32[]{:S(2)}) copy-start(f32[1,256]{1,0:T(1,128)} %get-tuple-element.50) | copy-start | bytes 3076
  103.2 4.6 %copy-start.24 = (f32[1,256]{1,0:T(1,128)S(1)}, f32[1,256]{1,0:T(1,128)}, u32[]{:S(2)}) copy-start(f32[1,256]{1,0:T(1,128)} %get-tuple-element.59) | copy-start | bytes 3076
  103.2 4.6 %copy-start.25 = (f32[8]{0:T(128)S(1)}, f32[8]{0:T(128)}, u32[]{:S(2)}) copy-start(f32[8]{0:T(128)} %get-tuple-element.64) | copy-start | bytes 100
  103.2 4.6 %copy-start.28 = (f32[1,256]{1,0:T(1,128)S(1)}, f32[1,256]{1,0:T(1,128)}, u32[]{:S(2)}) copy-start(f32[1,256]{1,0:T(1,128)} %get-tuple-element.51) | copy-start | bytes 3076
  103.2 4.6 %copy-start.29 = (f32[1,256]{1,0:T(1,128)S(1)}, f32[1,256]{1,0:T(1,128)}, u32[]{:S(2)}) copy-start(f32[1,256]{1,0:T(1,128)} %get-tuple-element.60) | copy-start | bytes 3076
  103.2 4.6 %copy-start.30 = (f32[8]{0:T(128)S(1)}, f32[8]{0:T(128)}, u32[]{:S(2)}) copy-start(f32[8]{0:T(128)} %get-tuple-element.65) | copy-start | bytes 100
  103.2 4.6 %copy-start.31 = (f32[1,256]{1,0:T(1,128)S(1)}, f32[1,256]{1,0:T(1,128)}, u32[]{:S(2)}) copy-start(f32[1,256]{1,0:T(1,128)} %get-tuple-element.52) | copy-start | bytes 3076
  103.2 4.6 %copy-start.32 = (f32[1,256]{1,0:T(1,128)S(1)}, f32[1,256]{1,0:T(1,128)}, u32[]{:S(2)}) copy-start(f32[1,256]{1,0:T(1,128)} %get-tuple-element.55) | copy-start | bytes 3076
  103.2 4.6 %copy-start.33 = (f32[8]{0:T(128)S(1)}, f32[8]{0:T(128)}, u32[]{:S(2)}) copy-start(f32[8]{0:T(128)} %get-tuple-element.66) | copy-start | bytes 100
  103.2 4.6 %copy-start.34 = (f32[8]{0:T(128)S(1)}, f32[8]{0:T(128)}, u32[]{:S(2)}) copy-start(f32[8]{0:T(128)} %get-tuple-element.67) | copy-start | bytes 100
  103.3 4.6 %copy-start.35 = (f32[8]{0:T(128)S(1)}, f32[8]{0:T(128)}, u32[]{:S(2)}) copy-start(f32[8]{0:T(128)} %get-tuple-element.68) | copy-start | bytes 100
  103.3 4.6 %copy-start.36 = (f32[8]{0:T(128)S(1)}, f32[8]{0:T(128)}, u32[]{:S(2)}) copy-start(f32[8]{0:T(128)} %get-tuple-element.69) | copy-start | bytes 100
  103.3 4.7 %copy-start.53 = (bf16[1,1,256]{2,1,0:T(2,128)(2,1)S(1)}, bf16[1,1,256]{2,1,0:T(2,128)(2,1)}, u32[]{:S(2)}) copy-start(bf16[1,1,256]{2,1,0:T(2,128)(2,1)} %get-tuple-element.5) | copy-start | bytes 1540
  103.3 15.2 %copy-start.46 = (f32[1,256]{1,0:T(1,128)S(1)}, f32[1,256]{1,0:T(1,128)}, u32[]{:S(2)}) copy-start(f32[1,256]{1,0:T(1,128)} %get-tuple-element.6) | copy-start | bytes 3076
  103.3 15.2 %copy-start.47 = (f32[1,256]{1,0:T(1,128)S(1)}, f32[1,256]{1,0:T(1,128)}, u32[]{:S(2)}) copy-start(f32[1,256]{1,0:T(1,128)} %get-tuple-element.7) | copy-start | bytes 3076
  103.3 15.2 %copy-start.48 = (f32[1,256]{1,0:T(1,128)S(1)}, f32[1,256]{1,0:T(1,128)}, u32[]{:S(2)}) copy-start(f32[1,256]{1,0:T(1,128)} %get-tuple-element.8) | copy-start | bytes 3076
  103.3 15.2 %copy-start.49 = (f32[1,256]{1,0:T(1,128)S(1)}, f32[1,256]{1,0:T(1,128)}, u32[]{:S(2)}) copy-start(f32[1,256]{1,0:T(1,128)} %get-tuple-element.9) | copy-start | bytes 3076
  103.3 15.2 %copy-start.50 = (f32[1,256]{1,0:T(1,128)S(1)}, f32[1,256]{1,0:T(1,128)}, u32[]{:S(2)}) copy-start(f32[1,256]{1,0:T(1,128)} %get-tuple-element.10) | copy-start | bytes 3076
  103.3 15.2 %copy-start.51 = (f32[1,256]{1,0:T(1,128)S(1)}, f32[1,256]{1,0:T(1,128)}, u32[]{:S(2)}) copy-start(f32[1,256]{1,0:T(1,128)} %get-tuple-element.11) | copy-start | bytes 3076
  103.3 15.2 %copy-start.52 = (f32[1,256]{1,0:T(1,128)S(1)}, f32[1,256]{1,0:T(1,128)}, u32[]{:S(2)}) copy-start(f32[1,256]{1,0:T(1,128)} %get-tuple-element.12) | copy-start | bytes 3076
  118.6 6.6 %copy-start.3 = (f32[32,32,1,256]{3,2,1,0:T(1,128)S(1)}, f32[32,32,1,256]{3,2,1,0:T(1,128)}, u32[]{:S(2)}) copy-start(f32[32,32,1,256]{3,2,1,0:T(1,128)} %copy-done.2) | copy-start | bytes 3145732
  118.6 6.6 %copy-start.5 = (f32[32,32,1,256]{3,2,1,0:T(1,128)S(1)}, f32[32,32,1,256]{3,2,1,0:T(1,128)}, u32[]{:S(2)}) copy-start(f32[32,32,1,256]{3,2,1,0:T(1,128)} %copy-done.4) | copy-start | bytes 3145732
  128.2 16.3 %copy-start.10 = (f32[32,32,256]{2,1,0:T(8,128)S(1)}, f32[32,32,256]{2,1,0:T(8,128)}, u32[]{:S(2)}) copy-start(f32[32,32,256]{2,1,0:T(8,128)} %get-tuple-element.78) | copy-start | bytes 3145732
  128.2 16.3 %copy-start.11 = (f32[32,32,256]{2,1,0:T(8,128)S(1)}, f32[32,32,256]{2,1,0:T(8,128)}, u32[]{:S(2)}) copy-start(f32[32,32,256]{2,1,0:T(8,128)} %get-tuple-element.79) | copy-start | bytes 3145732
  141.7 2.9 %copy-start.12 = (f32[32,32,256]{2,1,0:T(8,128)S(1)}, f32[32,32,256]{2,1,0:T(8,128)}, u32[]{:S(2)}) copy-start(f32[32,32,256]{2,1,0:T(8,128)} %get-tuple-element.76) | copy-start | bytes 3145732
  141.7 2.9 %copy-start.13 = (f32[32,32,256]{2,1,0:T(8,128)S(1)}, f32[32,32,256]{2,1,0:T(8,128)}, u32[]{:S(2)}) copy-start(f32[32,32,256]{2,1,0:T(8,128)} %get-tuple-element.77) | copy-start | bytes 3145732
  141.7 2.9 %copy-start.14 = (f32[32,32,256]{2,1,0:T(8,128)S(1)}, f32[32,32,256]{2,1,0:T(8,128)}, u32[]{:S(2)}) copy-start(f32[32,32,256]{2,1,0:T(8,128)} %get-tuple-element.74) | copy-start | bytes 3145732
  141.7 2.9 %copy-start.15 = (f32[32,32,256]{2,1,0:T(8,128)S(1)}, f32[32,32,256]{2,1,0:T(8,128)}, u32[]{:S(2)}) copy-start(f32[32,32,256]{2,1,0:T(8,128)} %get-tuple-element.75) | copy-start | bytes 3145732
  141.7 3.1 %copy-start.16 = (f32[32,32,256]{2,1,0:T(8,128)S(1)}, f32[32,32,256]{2,1,0:T(8,128)}, u32[]{:S(2)}) copy-start(f32[32,32,256]{2,1,0:T(8,128)} %get-tuple-element.72) | copy-start | bytes 3145732
  141.7 3.4 %copy-start.17 = (f32[32,32,256]{2,1,0:T(8,128)S(1)}, f32[32,32,256]{2,1,0:T(8,128)}, u32[]{:S(2)}) copy-start(f32[32,32,256]{2,1,0:T(8,128)} %get-tuple-element.73) | copy-start | bytes 3145732
Sparse Core Ops, SparseCore 0:
  107.9 33.7 all-gather.2
where the time goes:
time: 162 us; the launch traced here: 160 us
  local copies, waits for them, and re-layouts  61.7 us (38%)
  other arithmetic  50.1 us (31%)
  between operations  14.3 us (9%)
  waiting for transfers between devices  13.5 us (8%)
  blocking collectives  9.98 us (6%)
  starting transfers between devices  7.61 us (5%)
  matrix products  2.91 us (2%)
    slice x1, local copies, waits for them, and re-layouts, body(): source_level = moist_field[:, :, source:source + 1, :]  30.4 us
    all_gather x1, waiting for transfers between devices, body(): lax.all_gather(inflow[None].astype(jnp.bfloat16), 'gz', axis=0, tiled=True)  13.4 us
    scatter-add x1, other arithmetic, body(): moist_field = flat_cells.at[cell_ids].add(tendency.reshape(-1, channels)....  12.7 us
    sub x1, other arithmetic, advect(): centre - jnp.maximum(east_rate, 0.0) * (centre - from_west)  12.5 us
    all_gather x1, blocking collectives, body(): lax.all_gather(carried_gain[None].astype(jnp.bfloat16), 'gz', axis=0, til...  9.98 us
    mul x4, local copies, waits for them, and re-layouts, body(): local_values = local_values + source_level * level_rows[:, source, :]  9.56 us
    convert_element_type x1, other arithmetic, body(): (local_values + incoming[:, :, None, :] * level_gains).astype(jnp.bfloat16)  8.12 us
    gather x1, local copies, waits for them, and re-layouts, body(): flat_cells[cell_ids].astype(jnp.bfloat16)  7.36 us
  transfers between devices with their start and end apart: 5, of which 1 were waited for; matrix products, arithmetic and copies ran while one was open for 19% of the time, Pallas kernels for 0%

commit v1 on v0

v1 whole, which is shorter than its diff:
```python
import jax
import jax.numpy as jnp
from jax import lax
from jax.experimental import pallas as pl
from jax.experimental.pallas import tpu as pltpu
from jax.sharding import PartitionSpec as P

F32 = jnp.float32
BF16 = jnp.bfloat16
GAIN_ROWS = 16
HALVES = 2


def edges_kernel(s_ref, west_ref, east_ref, south_ref, north_ref, sems):
    nx, ny = s_ref.shape[:2]
    pieces = (
        (s_ref.at[0:1], west_ref),
        (s_ref.at[nx - 1 : nx], east_ref),
        (s_ref.at[:, 0:1], south_ref),
        (s_ref.at[:, ny - 1 : ny], north_ref),
    )
    copies = [
        pltpu.make_async_copy(src, dst, sems.at[i]) for i, (src, dst) in enumerate(pieces)
    ]
    for copy in copies:
        copy.start()
    for copy in copies:
        copy.wait()


def edges(spectrum):
    nx, ny, nz, nb = spectrum.shape
    any_spec = pl.BlockSpec(memory_space=pl.ANY)
    row = jax.ShapeDtypeStruct((1, ny, nz, nb), BF16)
    column = jax.ShapeDtypeStruct((nx, 1, nz, nb), BF16)
    return pl.pallas_call(
        edges_kernel,
        out_shape=(row, row, column, column),
        in_specs=[any_spec],
        out_specs=[any_spec] * 4,
        scratch_shapes=[pltpu.SemaphoreType.DMA((4,))],
        compiler_params=pltpu.CompilerParams(vmem_limit_bytes=2**20),
        name="edges",
    )(spectrum)


def cell_kernel(
    cells_ref,
    active_ref,
    s_any,
    west_any,
    east_any,
    south_any,
    north_any,
    we_ref,
    wn_ref,
    fall_ref,
    pi_ref,
    po_ref,
    lk_ref,
    fr_ref,
    local_any,
    flux_ref,
    pad,
    south,
    north,
    adv,
    rows,
    stage,
    sems,
):
    nx, ny, nz, nb = s_any.shape
    blk, blocks = cells_ref.shape
    pairs = po_ref.shape[0]
    tiles = nb // 128
    parts = 4
    per = nx // parts
    ins = [
        pltpu.make_async_copy(west_any, pad.at[0:1], sems.at[0]),
        pltpu.make_async_copy(east_any, pad.at[nx + 1 : nx + 2], sems.at[1]),
        pltpu.make_async_copy(south_any, south, sems.at[2]),
        pltpu.make_async_copy(north_any, north, sems.at[3]),
    ]
    for i in range(parts):
        ins.append(
            pltpu.make_async_copy(
                s_any.at[i * per : (i + 1) * per],
                pad.at[1 + i * per : 1 + (i + 1) * per],
                sems.at[4 + i],
            )
        )
    for copy in ins:
        copy.start()
    for copy in ins:
        copy.wait()

    def advect(x, carry):
        u = we_ref[x]
        v = wn_ref[x]
        c_w = jnp.maximum(u, 0.0)
        c_e = jnp.maximum(-u, 0.0)
        c_s = jnp.maximum(v, 0.0)
        c_n = jnp.maximum(-v, 0.0)
        c_0 = 1.0 - c_w - c_e - c_s - c_n

        def wide(c, y):
            return jnp.broadcast_to(c[:, y : y + 1], (nz, nb))

        behind = south[x, 0].astype(F32)
        here = pad[x + 1, 0].astype(F32)
        for y in range(ny):
            ahead = (north[x, 0] if y == ny - 1 else pad[x + 1, y + 1]).astype(F32)
            value = (
                wide(c_0, y) * here
                + wide(c_w, y) * pad[x, y].astype(F32)
                + wide(c_e, y) * pad[x + 2, y].astype(F32)
                + wide(c_s, y) * behind
                + wide(c_n, y) * ahead
            )
            at = pl.ds(pl.multiple_of(x * (ny * nz) + y * nz, 8), nz)
            for t in range(tiles):
                adv[t, at, :] = value[:, t * 128 : (t + 1) * 128]
            behind, here = here, ahead
        return carry

    lax.fori_loop(0, nx, advect, 0)

    def gather(b, carry):
        base = pl.multiple_of(b * blk, blk)
        for j in range(blk):
            for t in range(tiles):
                rows[t, pl.ds(base + j, 1), :] = adv[t, pl.ds(cells_ref[j, b], 1), :]
        return carry

    lax.fori_loop(0, blocks, gather, 0)

    step = 512
    tile = 256

    def collide(i, carry):
        here = pl.ds(pl.multiple_of(i * step, step), step)
        cloud = jnp.concatenate([rows[t, here, :] for t in range(tiles)], 1).astype(BF16)
        decline = jnp.dot(cloud, lk_ref[...], preferred_element_type=F32)
        losses = cloud.astype(F32) * decline
        total = jnp.dot(losses.astype(BF16), fr_ref[...], preferred_element_type=F32) - losses
        for n in range(pairs // tile):
            left = jnp.dot(
                cloud, pi_ref[:, n * tile : (n + 1) * tile], preferred_element_type=F32
            )
            right = jnp.dot(
                cloud,
                pi_ref[:, pairs + n * tile : pairs + (n + 1) * tile],
                preferred_element_type=F32,
            )
            total = total + jnp.dot(
                (left * right).astype(BF16),
                po_ref[n * tile : (n + 1) * tile, :],
                preferred_element_type=F32,
            )
        total = total.astype(BF16).astype(F32)
        for t in range(tiles):
            rows[t, here, :] = total[:, t * 128 : (t + 1) * 128]
        return carry

    lax.fori_loop(0, blocks * blk // step, collide, 0)

    def scatter(b, carry):
        base = pl.multiple_of(b * blk, blk)

        @pl.when(active_ref[b] != 0)
        def _():
            ids = [cells_ref[j, b] for j in range(blk)]
            sums = [
                adv[t, pl.ds(ids[j], 1), :] + rows[t, pl.ds(base + j, 1), :]
                for j in range(blk)
                for t in range(tiles)
            ]
            for j in range(blk):
                for t in range(tiles):
                    adv[t, pl.ds(ids[j], 1), :] = sums[j * tiles + t]

        return carry

    lax.fori_loop(0, blocks, scatter, 0)

    fall = fall_ref[...]
    inverse = 1.0 / (1.0 + fall)
    through = fall * inverse
    cut = 2 * 8 * nz

    def settle(g, carry):
        base = pl.multiple_of(g * cut, cut)
        flows = []
        for t in range(tiles):
            lanes = slice(t * 128, (t + 1) * 128)
            for half in range(2):
                inflow = jnp.zeros((8, 128), F32)
                for z in reversed(range(nz)):
                    at = pl.ds(base + half * 8 * nz + z, 8, stride=nz)
                    total = adv[t, at, :] + inflow
                    adv[t, at, :] = total * inverse[z : z + 1, lanes]
                    inflow = total * through[z : z + 1, lanes]
                flows.append(inflow)
            flux_ref[pl.ds(pl.multiple_of(g * 16, 16), 16), lanes] = jnp.concatenate(
                flows[-2:], 0
            ).astype(BF16)
        for c in range(16):
            column = pl.ds(pl.multiple_of(base + c * nz, 8), nz)
            stage[g // 2, (g % 2) * 16 + c] = jnp.concatenate(
                [adv[t, column, :] for t in range(tiles)], 1
            ).astype(BF16)
        return carry

    for i in range(parts):
        lax.fori_loop(i * per * 2, (i + 1) * per * 2, settle, 0)
        pltpu.make_async_copy(
            stage.at[i * per : (i + 1) * per],
            local_any.at[i * per : (i + 1) * per],
            sems.at[4 + i],
        ).start()

    gain = jnp.ones((1, nb), F32)
    for z in reversed(range(nz)):
        gain = gain * through[z : z + 1, :]
    flux_ref[pl.ds(nx * ny, GAIN_ROWS), :] = jnp.broadcast_to(gain, (GAIN_ROWS, nb)).astype(BF16)
    for i in range(parts):
        pltpu.make_async_copy(
            stage.at[i * per : (i + 1) * per],
            local_any.at[i * per : (i + 1) * per],
            sems.at[4 + i],
        ).wait()


def combine_kernel(zid_ref, own_ref, a_ref, b_ref, out_ref):
    n = own_ref.shape[0] - GAIN_ROWS
    z = zid_ref[0]

    @pl.when(z == 0)
    def _():
        out_ref[...] = b_ref[...]

    @pl.when(z != 0)
    def _():
        gain = own_ref[n : n + GAIN_ROWS, :].astype(F32)

        def some(i, carry):
            at = pl.ds(pl.multiple_of(i * 16, 16), 16)
            out_ref[at, :] = (
                own_ref[at, :].astype(F32) + gain * a_ref[at, :].astype(F32)
            ).astype(BF16)
            return carry

        lax.fori_loop(0, n // 16, some, 0, unroll=4)
        out_ref[n : n + GAIN_ROWS, :] = (
            gain * a_ref[n : n + GAIN_ROWS, :].astype(F32)
        ).astype(BF16)


def combine(zid, own, a, b):
    vmem = pl.BlockSpec(memory_space=pltpu.VMEM)
    return pl.pallas_call(
        combine_kernel,
        out_shape=jax.ShapeDtypeStruct(own.shape, BF16),
        in_specs=[pl.BlockSpec(memory_space=pltpu.SMEM), vmem, vmem, vmem],
        out_specs=vmem,
        compiler_params=pltpu.CompilerParams(vmem_limit_bytes=4 * 2**20),
        name="combine",
    )(zid, own, a, b)


def finish_kernel(zid_ref, fall_ref, a_ref, b_ref, d_ref, local_ref, out_ref, inflow):
    nxs, ny, nz, nb = local_ref.shape
    n = a_ref.shape[0] - GAIN_ROWS
    rows = nxs * ny
    z = zid_ref[0]
    fall = fall_ref[...]
    through = fall / (1.0 + fall)
    inverse = 1.0 / (1.0 + fall)
    carried = jnp.ones((1, nb), F32)
    gains = [None] * nz
    for level in reversed(range(nz)):
        gains[level] = carried * inverse[level : level + 1, :]
        carried = carried * through[level : level + 1, :]
    gain = jnp.concatenate(gains, 0)
    start = pl.program_id(0) * rows
    bottom = z == 0
    mix = jnp.where(bottom, d_ref[n : n + GAIN_ROWS, :], a_ref[n : n + GAIN_ROWS, :]).astype(F32)
    for i in range(rows // 16):
        at = pl.ds(pl.multiple_of(start + i * 16, 16), 16)
        a, b, d = a_ref[at, :].astype(F32), b_ref[at, :].astype(F32), d_ref[at, :].astype(F32)
        inflow[i * 16 : (i + 1) * 16, :] = jnp.where(bottom, d, a) + mix * jnp.where(bottom, b, d)

    def column(x, carry):
        for y in range(ny):
            m = jnp.broadcast_to(inflow[pl.ds(x * ny + y, 1), :], (nz, nb))
            out_ref[x, y] = (local_ref[x, y].astype(F32) + m * gain).astype(BF16)
        return carry

    lax.fori_loop(0, nxs, column, 0)


def finish(zid, fall, a, b, d, local, half):
    nx, ny, nz, nb = local.shape
    nxs = 4
    steps = nx // HALVES // nxs
    vmem = pl.BlockSpec(memory_space=pltpu.VMEM)
    block = pl.BlockSpec((nxs, ny, nz, nb), lambda i: (i + half * steps, 0, 0, 0))
    return pl.pallas_call(
        finish_kernel,
        out_shape=jax.ShapeDtypeStruct(local.shape, BF16),
        grid=(steps,),
        in_specs=[
            pl.BlockSpec(memory_space=pltpu.SMEM),
            vmem,
            vmem,
            vmem,
            vmem,
            block,
        ],
        out_specs=block,
        scratch_shapes=[pltpu.VMEM((nxs * ny, nb), F32)],
        input_output_aliases={5: 0},
        compiler_params=pltpu.CompilerParams(vmem_limit_bytes=12 * 2**20),
        name="finish",
    )(zid, fall, a, b, d, local)


def cell_work(cells, active, spectrum, halo, we, wn, fall, pi, po, lk, fr):
    nx, ny, nz, nb = spectrum.shape
    vmem = pl.BlockSpec(memory_space=pltpu.VMEM)
    smem = pl.BlockSpec(memory_space=pltpu.SMEM)
    any_spec = pl.BlockSpec(memory_space=pl.ANY)
    blk, blocks = cells.shape
    return pl.pallas_call(
        cell_kernel,
        out_shape=(
            jax.ShapeDtypeStruct(spectrum.shape, BF16),
            jax.ShapeDtypeStruct((nx * ny + GAIN_ROWS, nb), BF16),
        ),
        in_specs=[smem, smem] + [any_spec] * 5 + [vmem] * 7,
        out_specs=(any_spec, vmem),
        scratch_shapes=[
            pltpu.VMEM((nx + 2, ny, nz, nb), BF16),
            pltpu.VMEM((nx, 1, nz, nb), BF16),
            pltpu.VMEM((nx, 1, nz, nb), BF16),
            pltpu.VMEM((nb // 128, nx * ny * nz, 128), F32),
            pltpu.VMEM((nb // 128, blk * blocks, 128), F32),
            pltpu.VMEM((nx, ny, nz, nb), BF16),
            pltpu.SemaphoreType.DMA((8,)),
        ],
        compiler_params=pltpu.CompilerParams(vmem_limit_bytes=40 * 2**20),
        name="cells",
    )(cells, active, spectrum, *halo, we, wn, fall, pi, po, lk, fr)


def body(
    spectrum,
    wind_east,
    wind_north,
    fall_rate,
    cloud_cells,
    block_target,
    pair_inputs,
    pair_outputs,
    loss_kernel,
    fragments,
):
    nx, ny, nz, nb = spectrum.shape
    n_gx, n_gy = (lax.axis_size(a) for a in ("gx", "gy"))
    up_x = [(i, (i + 1) % n_gx) for i in range(n_gx)]
    up_y = [(i, (i + 1) % n_gy) for i in range(n_gy)]
    low_x, high_x, low_y, high_y = edges(spectrum)
    south = lax.ppermute(high_y, "gy", up_y)
    north = lax.ppermute(low_y, "gy", [(b, a) for a, b in up_y])
    west = lax.ppermute(high_x, "gx", up_x)
    east = lax.ppermute(low_x, "gx", [(b, a) for a, b in up_x])

    blocks, blk = cloud_cells.shape[3:]
    cells = cloud_cells.reshape(blocks, blk).T
    plane = n_gx * n_gy
    own = lax.axis_index("gx") * n_gy + lax.axis_index("gy")
    targets = lax.dynamic_index_in_dim(block_target.reshape(plane, blocks), own, 0, keepdims=False)
    active = (targets < plane).astype(jnp.int32)
    local, flux = cell_work(
        cells,
        active,
        spectrum,
        (west, east, south, north),
        wind_east.transpose(0, 2, 1),
        wind_north.transpose(0, 2, 1),
        fall_rate,
        pair_inputs,
        pair_outputs,
        loss_kernel,
        fragments,
    )
    zid = lax.axis_index("gz").reshape(1)
    count = nx * ny // HALVES
    firsts = []
    for h in range(HALVES):
        piece = jnp.concatenate([flux[h * count : (h + 1) * count], flux[nx * ny :]], 0)
        a = lax.ppermute(piece, "gz", [(3, 2), (2, 1)])
        b = lax.ppermute(piece, "gz", [(3, 0)])
        firsts.append((piece, a, b))
    seconds = []
    for piece, a, b in firsts:
        c = combine(zid, piece, a, b)
        d = lax.ppermute(c, "gz", [(1, 0), (0, 1)])
        seconds.append((a, b, d))
    out = local
    for h, (a, b, d) in enumerate(seconds):
        out = finish(zid, fall_rate, a, b, d, out, h)
    return out


def solution(mesh):
    in_specs = (
        P("gx", "gy", "gz", None),
        P("gx", "gy", "gz"),
        P("gx", "gy", "gz"),
        P("gz", None),
        P("gx", "gy", "gz", None, None),
        P(None, None, "gz", None),
        P(),
        P(),
        P(),
        P(),
    )
    out_specs = P("gx", "gy", "gz", None)
    return jax.shard_map(body, mesh=mesh, in_specs=in_specs, out_specs=out_specs, check_vma=False)
```

time: 162 us -> 70.8 us (0.44)
  the two profiles are of different devices: /device:TPU:2 before, /device:TPU:98 now
where the time goes in v1:
time: 70.8 us; the launch traced here: 70.1 us
  Pallas kernels  31 us (44%)
  waiting for transfers between devices  18.8 us (27%)
  starting transfers between devices  14.9 us (21%)
  local copies, waits for them, and re-layouts  4.44 us (6%)
  other arithmetic  0.71 us (1%)
    pallas_call x1, Pallas kernels, cell_work(): pl.pallas_call(cell_kernel, out_shape=(jax.ShapeDtypeStruct(spectrum.shap...  22 us
    ppermute x2, waiting for transfers between devices, body(): b = lax.ppermute(piece, 'gz', [(3, 0)])  8.6 us
    pallas_call x2, Pallas kernels, finish(): pl.pallas_call(finish_kernel, out_shape=jax.ShapeDtypeStruct(local.shape,...  8.48 us
    ppermute x2, starting transfers between devices, body(): d = lax.ppermute(c, 'gz', [(1, 0), (0, 1)])  6.1 us
    ppermute x2, waiting for transfers between devices, body(): d = lax.ppermute(c, 'gz', [(1, 0), (0, 1)])  4.72 us
    unnamed x20, local copies, waits for them, and re-layouts  4.4 us
    ppermute x1, waiting for transfers between devices, body(): north = lax.ppermute(low_y, 'gy', [(b, a) for a, b in up_y])  3.41 us
    ppermute x1, starting transfers between devices, body(): south = lax.ppermute(high_y, 'gy', up_y)  3.13 us
  transfers between devices with their start and end apart: 10, of which 5 were waited for; matrix products, arithmetic and copies ran while one was open for 1% of the time, Pallas kernels for 6%

profile of v1, /device:TPU:98, one launch (start us, length us, event | category | flops | bytes accessed | tf_op | source)
XLA Modules:
  0.0 70.1 jit_solution(9564763043685705475)
XLA Ops:
  0.0 0.0 copy-start
  0.0 2.2 %copy-done = bf16[32,32,8,256]{3,2,1,0:T(8,128)(2,1)S(1)} copy-done((bf16[32,32,8,256]{3,2,1,0:T(8,128)(2,1)S(1)}, bf16[32,32,8,256]{3,2,1,0:T(8,128)(2,1)}, u32[]{:S(2)}) %copy-start) | copy-done | bytes 4194328
  2.2 0.0 copy-start.2
  2.2 0.0 copy-start.3
  2.2 0.0 copy-start.4
  2.2 0.0 copy-start.5
  2.2 0.0 copy-start.6
  2.2 0.0 copy-start.7
  2.2 0.0 copy-start.8
  2.2 0.0 copy-start.9
  2.2 0.4 edges.1
  2.7 0.0 collective-permute-start
  2.7 1.7 %collective-permute-start.1 = (bf16[1,32,8,256]{3,2,1,0:T(8,128)(2,1)S(1)}, bf16[1,32,8,256]{3,2,1,0:T(8,128)(2,1)S(1)}, u32[]{:S(2)}, u32[]{:S(2)}) collective-permute-start(bf16[1,32,8,256]{3,2,1,0:T(8,128)(2,1)S(1)} %get-tuple-element.12), channel_id=1, source_target_pairs={{32,0},{64,32},{96,64},{128,96},{160,128},{192,160},{224,192},{0,2... | collective-permute-start | bytes 393224 | tf_op jit(solution)/shard_map/ppermute | solution.py:376
  4.4 3.1 %collective-permute-start.2 = (bf16[32,1,8,256]{3,2,1,0:T(8,128)(2,1)S(1)}, bf16[32,1,8,256]{3,2,1,0:T(8,128)(2,1)S(1)}, u32[]{:S(2)}, u32[]{:S(2)}) collective-permute-start(bf16[32,1,8,256]{3,2,1,0:T(8,128)(2,1)S(1)} %get-tuple-element.13), channel_id=1, source_target_pairs={{0,4},{4,8},{8,12},{12,16},{16,20},{20,24},{24,28},{28,0},{1,5},{5... | collective-permute-start | bytes 393224 | tf_op jit(solution)/shard_map/ppermute | solution.py:373
  7.6 0.0 collective-permute-start.3
  7.6 0.7 fusion.active_ref
  8.2 0.0 collective-permute-done.west_any
  8.3 0.0 collective-permute-done.1.east_any
  8.3 2.1 %collective-permute-done.2.south_any = bf16[32,1,8,256]{3,2,1,0:T(8,128)(2,1)S(1)} collective-permute-done((bf16[32,1,8,256]{3,2,1,0:T(8,128)(2,1)S(1)}, bf16[32,1,8,256]{3,2,1,0:T(8,128)(2,1)S(1)}, u32[]{:S(2)}, u32[]{:S(2)}) %collective-permute-start.2) | collective-permute-done | bytes 131104 | tf_op jit(solution)/shard_map/ppermute | solution.py:373
  10.3 3.4 %collective-permute-done.3.north_any = bf16[32,1,8,256]{3,2,1,0:T(8,128)(2,1)S(1)} collective-permute-done((bf16[32,1,8,256]{3,2,1,0:T(8,128)(2,1)S(1)}, bf16[32,1,8,256]{3,2,1,0:T(8,128)(2,1)S(1)}, u32[]{:S(2)}, u32[]{:S(2)}) %collective-permute-start.3) | collective-permute-done | bytes 131104 | tf_op jit(solution)/shard_map/ppermute | solution.py:374
  13.7 0.0 copy-done.2
  13.8 0.0 copy-done.3
  13.8 0.0 copy-done.4
  13.8 0.0 copy-done.5
  13.8 0.0 copy-done.6
  13.8 0.0 copy-done.7
  13.8 0.0 copy-done.8
  13.8 0.0 copy-done.9
  13.8 0.0 copy-start.1
  13.8 2.2 %copy-done.1 = bf16[32,32,8,256]{3,2,1,0:T(8,128)(2,1)S(1)} copy-done((bf16[32,32,8,256]{3,2,1,0:T(8,128)(2,1)S(1)}, bf16[32,32,8,256]{3,2,1,0:T(8,128)(2,1)}, u32[]{:S(2)}) %copy-start.1) | copy-done | bytes 4194328
  16.0 22.0 %cells.1 = (bf16[32,32,8,256]{3,2,1,0:T(8,128)(2,1)}, bf16[1040,256]{1,0:T(8,128)(2,1)S(1)}) custom-call(s32[16,64]{1,0:T(8,128)S(1)} %bitcast.11, s32[64]{0:T(128)S(1)} %fusion.active_ref, bf16[32,32,8,256]{3,2,1,0:T(8,128)(2,1)S(1)} %copy-done.1, bf16[1,32,8,256]{3,2,1,0:T(8,128)(2,1)S(1)} %collective-permute-done.west_any, ...), custom_call_target="tpu_custom_call" | custom-call | tf_op jit(solution)/shard_map/cells/pallas_call | solution.py:334
  38.1 1.3 %collective-permute-start.8 = (bf16[528,256]{1,0:T(8,128)(2,1)S(1)}, bf16[528,256]{1,0:T(8,128)(2,1)S(1)}, u32[]{:S(2)}, u32[]{:S(2)}) collective-permute-start(bf16[528,256]{1,0:T(8,128)(2,1)S(1)} %pad_maximum_fusion.own_ref), channel_id=1, source_target_pairs={{3,0},{7,4},{11,8},{15,12},{19,16},{23,20},{27,24},{31,28},{35,32}... | collective-permute-start | bytes 811016 | tf_op jit(solution)/shard_map/ppermute | solution.py:403
  39.4 0.7 collective-permute-start.7
  40.1 1.3 %collective-permute-start.5 = (bf16[528,256]{1,0:T(8,128)(2,1)S(1)}, bf16[528,256]{1,0:T(8,128)(2,1)S(1)}, u32[]{:S(2)}, u32[]{:S(2)}) collective-permute-start(bf16[528,256]{1,0:T(8,128)(2,1)S(1)} %concatenate.6.own_ref), channel_id=1, source_target_pairs={{3,0},{7,4},{11,8},{15,12},{19,16},{23,20},{27,24},{31,28},{35,32}... | collective-permute-start | bytes 811016 | tf_op jit(solution)/shard_map/ppermute | solution.py:403
  41.4 0.7 collective-permute-start.4
  42.1 8.5 %collective-permute-done.8.b_ref = bf16[528,256]{1,0:T(8,128)(2,1)S(1)} collective-permute-done((bf16[528,256]{1,0:T(8,128)(2,1)S(1)}, bf16[528,256]{1,0:T(8,128)(2,1)S(1)}, u32[]{:S(2)}, u32[]{:S(2)}) %collective-permute-start.8) | collective-permute-done | bytes 270368 | tf_op jit(solution)/shard_map/ppermute | solution.py:403
  50.6 0.0 collective-permute-done.7.a_ref
  50.7 3.1 %collective-permute-start.9 = (bf16[528,256]{1,0:T(8,128)(2,1)S(1)}, bf16[528,256]{1,0:T(8,128)(2,1)S(1)}, u32[]{:S(2)}, u32[]{:S(2)}) collective-permute-start(bf16[528,256]{1,0:T(8,128)(2,1)S(1)} %combine.3), channel_id=1, source_target_pairs={{1,0},{0,1},{5,4},{4,5},{9,8},{8,9},{13,12},{12,13},{17,16},{16,17... | collective-permute-start | bytes 811016 | tf_op jit(solution)/shard_map/ppermute | solution.py:408
  53.7 0.1 collective-permute-done.5.b_ref
  53.8 0.0 collective-permute-done.4.a_ref
  53.8 3.1 %collective-permute-start.6 = (bf16[528,256]{1,0:T(8,128)(2,1)S(1)}, bf16[528,256]{1,0:T(8,128)(2,1)S(1)}, u32[]{:S(2)}, u32[]{:S(2)}) collective-permute-start(bf16[528,256]{1,0:T(8,128)(2,1)S(1)} %combine.2), channel_id=1, source_target_pairs={{1,0},{0,1},{5,4},{4,5},{9,8},{8,9},{13,12},{12,13},{17,16},{16,17... | collective-permute-start | bytes 811016 | tf_op jit(solution)/shard_map/ppermute | solution.py:408
  56.9 4.7 %collective-permute-done.9.d_ref = bf16[528,256]{1,0:T(8,128)(2,1)S(1)} collective-permute-done((bf16[528,256]{1,0:T(8,128)(2,1)S(1)}, bf16[528,256]{1,0:T(8,128)(2,1)S(1)}, u32[]{:S(2)}, u32[]{:S(2)}) %collective-permute-start.9) | collective-permute-done | bytes 270368 | tf_op jit(solution)/shard_map/ppermute | solution.py:408
  61.6 4.2 %finish.2.local_ref = bf16[32,32,8,256]{3,2,1,0:T(8,128)(2,1)} custom-call(s32[1]{0:T(128)} %bitcast.zid_ref, f32[8,256]{1,0:T(8,128)S(1)} %copy-done.8, bf16[528,256]{1,0:T(8,128)(2,1)S(1)} %collective-permute-done.7.a_ref, bf16[528,256]{1,0:T(8,128)(2,1)S(1)} %collective-permute-done.8.b_ref, ...), custom_call_target="tpu_custom_call", output_to_operand_aliasing={{}: (5, {})} | custom-call | tf_op jit(solution)/shard_map/finish/pallas_call | solution.py:308
  65.9 0.0 collective-permute-done.6.d_ref
  65.9 4.2 %finish.3 = bf16[32,32,8,256]{3,2,1,0:T(8,128)(2,1)} custom-call(s32[1]{0:T(128)} %bitcast.zid_ref, f32[8,256]{1,0:T(8,128)S(1)} %copy-done.8, bf16[528,256]{1,0:T(8,128)(2,1)S(1)} %collective-permute-done.4.a_ref, bf16[528,256]{1,0:T(8,128)(2,1)S(1)} %collective-permute-done.5.b_ref, ...), custom_call_target="tpu_custom_call", output_to_operand_aliasing={{}: (5, {})} | custom-call | tf_op jit(solution)/shard_map/finish/pallas_call | solution.py:308
  (6 shorter events, 0.1 us)
Async XLA Ops:
  0.0 2.2 %copy-start = (bf16[32,32,8,256]{3,2,1,0:T(8,128)(2,1)S(1)}, bf16[32,32,8,256]{3,2,1,0:T(8,128)(2,1)}, u32[]{:S(2)}) copy-start(bf16[32,32,8,256]{3,2,1,0:T(8,128)(2,1)} %s_any.1) | copy-start | bytes 12582916
  2.2 11.6 %copy-start.2 = (bf16[256,2048]{1,0:T(8,128)(2,1)S(1)}, bf16[256,2048]{1,0:T(8,128)(2,1)}, u32[]{:S(2)}) copy-start(bf16[256,2048]{1,0:T(8,128)(2,1)} %pi_ref.1) | copy-start | bytes 3145732
  2.2 11.6 %copy-start.3 = (bf16[1024,256]{1,0:T(8,128)(2,1)S(1)}, bf16[1024,256]{1,0:T(8,128)(2,1)}, u32[]{:S(2)}) copy-start(bf16[1024,256]{1,0:T(8,128)(2,1)} %po_ref.1) | copy-start | bytes 1572868
  2.2 11.6 %copy-start.4 = (f32[32,32,8]{1,2,0:T(8,128)S(1)}, f32[32,32,8]{1,2,0:T(8,128)}, u32[]{:S(2)}) copy-start(f32[32,32,8]{1,2,0:T(8,128)} %param.11) | copy-start | bytes 98308
  2.2 11.6 %copy-start.5 = (f32[32,32,8]{1,2,0:T(8,128)S(1)}, f32[32,32,8]{1,2,0:T(8,128)}, u32[]{:S(2)}) copy-start(f32[32,32,8]{1,2,0:T(8,128)} %param.12) | copy-start | bytes 98308
  2.2 11.6 %copy-start.6 = (bf16[256,256]{1,0:T(8,128)(2,1)S(1)}, bf16[256,256]{1,0:T(8,128)(2,1)}, u32[]{:S(2)}) copy-start(bf16[256,256]{1,0:T(8,128)(2,1)} %lk_ref.1) | copy-start | bytes 393220
  2.2 11.6 %copy-start.7 = (bf16[256,256]{1,0:T(8,128)(2,1)S(1)}, bf16[256,256]{1,0:T(8,128)(2,1)}, u32[]{:S(2)}) copy-start(bf16[256,256]{1,0:T(8,128)(2,1)} %fr_ref.1) | copy-start | bytes 393220
  2.2 11.6 %copy-start.8 = (f32[8,256]{1,0:T(8,128)S(1)}, f32[8,256]{1,0:T(8,128)}, u32[]{:S(2)}) copy-start(f32[8,256]{1,0:T(8,128)} %fall_ref.5) | copy-start | bytes 24580
  2.2 11.6 %copy-start.9 = (s32[1,1,1,64,16]{3,4,2,1,0:T(8,128)S(1)}, s32[1,1,1,64,16]{3,4,2,1,0:T(8,128)}, u32[]{:S(2)}) copy-start(s32[1,1,1,64,16]{3,4,2,1,0:T(8,128)} %param.14) | copy-start | bytes 12292
  2.7 5.6 %collective-permute-start = (bf16[1,32,8,256]{3,2,1,0:T(8,128)(2,1)S(1)}, bf16[1,32,8,256]{3,2,1,0:T(8,128)(2,1)S(1)}, u32[]{:S(2)}, u32[]{:S(2)}) collective-permute-start(bf16[1,32,8,256]{3,2,1,0:T(8,128)(2,1)S(1)} %get-tuple-element.11), channel_id=1, source_target_pairs={{0,32},{32,64},{64,96},{96,128},{128,160},{160,192},{192,224},{224... | collective-permute-start | bytes 393224 | tf_op jit(solution)/shard_map/ppermute | solution.py:375
  2.7 5.6 %collective-permute-start.1 = (bf16[1,32,8,256]{3,2,1,0:T(8,128)(2,1)S(1)}, bf16[1,32,8,256]{3,2,1,0:T(8,128)(2,1)S(1)}, u32[]{:S(2)}, u32[]{:S(2)}) collective-permute-start(bf16[1,32,8,256]{3,2,1,0:T(8,128)(2,1)S(1)} %get-tuple-element.12), channel_id=1, source_target_pairs={{32,0},{64,32},{96,64},{128,96},{160,128},{192,160},{224,192},{0,2... | collective-permute-start | bytes 393224 | tf_op jit(solution)/shard_map/ppermute | solution.py:376
  4.4 5.9 %collective-permute-start.2 = (bf16[32,1,8,256]{3,2,1,0:T(8,128)(2,1)S(1)}, bf16[32,1,8,256]{3,2,1,0:T(8,128)(2,1)S(1)}, u32[]{:S(2)}, u32[]{:S(2)}) collective-permute-start(bf16[32,1,8,256]{3,2,1,0:T(8,128)(2,1)S(1)} %get-tuple-element.13), channel_id=1, source_target_pairs={{0,4},{4,8},{8,12},{12,16},{16,20},{20,24},{24,28},{28,0},{1,5},{5... | collective-permute-start | bytes 393224 | tf_op jit(solution)/shard_map/ppermute | solution.py:373
  7.6 6.2 %collective-permute-start.3 = (bf16[32,1,8,256]{3,2,1,0:T(8,128)(2,1)S(1)}, bf16[32,1,8,256]{3,2,1,0:T(8,128)(2,1)S(1)}, u32[]{:S(2)}, u32[]{:S(2)}) collective-permute-start(bf16[32,1,8,256]{3,2,1,0:T(8,128)(2,1)S(1)} %get-tuple-element.14), channel_id=1, source_target_pairs={{4,0},{8,4},{12,8},{16,12},{20,16},{24,20},{28,24},{0,28},{5,1},{9... | collective-permute-start | bytes 393224 | tf_op jit(solution)/shard_map/ppermute | solution.py:374
  13.8 2.2 %copy-start.1 = (bf16[32,32,8,256]{3,2,1,0:T(8,128)(2,1)S(1)}, bf16[32,32,8,256]{3,2,1,0:T(8,128)(2,1)}, u32[]{:S(2)}) copy-start(bf16[32,32,8,256]{3,2,1,0:T(8,128)(2,1)} %s_any.1) | copy-start | bytes 12582916
  38.1 12.5 %collective-permute-start.8 = (bf16[528,256]{1,0:T(8,128)(2,1)S(1)}, bf16[528,256]{1,0:T(8,128)(2,1)S(1)}, u32[]{:S(2)}, u32[]{:S(2)}) collective-permute-start(bf16[528,256]{1,0:T(8,128)(2,1)S(1)} %pad_maximum_fusion.own_ref), channel_id=1, source_target_pairs={{3,0},{7,4},{11,8},{15,12},{19,16},{23,20},{27,24},{31,28},{35,32}... | collective-permute-start | bytes 811016 | tf_op jit(solution)/shard_map/ppermute | solution.py:403
  39.4 11.2 %collective-permute-start.7 = (bf16[528,256]{1,0:T(8,128)(2,1)S(1)}, bf16[528,256]{1,0:T(8,128)(2,1)S(1)}, u32[]{:S(2)}, u32[]{:S(2)}) collective-permute-start(bf16[528,256]{1,0:T(8,128)(2,1)S(1)} %pad_maximum_fusion.own_ref), channel_id=1, source_target_pairs={{3,2},{2,1},{7,6},{6,5},{11,10},{10,9},{15,14},{14,13},{19,18},{18... | collective-permute-start | bytes 811016 | tf_op jit(solution)/shard_map/ppermute | solution.py:402
  40.1 13.7 %collective-permute-start.5 = (bf16[528,256]{1,0:T(8,128)(2,1)S(1)}, bf16[528,256]{1,0:T(8,128)(2,1)S(1)}, u32[]{:S(2)}, u32[]{:S(2)}) collective-permute-start(bf16[528,256]{1,0:T(8,128)(2,1)S(1)} %concatenate.6.own_ref), channel_id=1, source_target_pairs={{3,0},{7,4},{11,8},{15,12},{19,16},{23,20},{27,24},{31,28},{35,32}... | collective-permute-start | bytes 811016 | tf_op jit(solution)/shard_map/ppermute | solution.py:403
  41.4 12.4 %collective-permute-start.4 = (bf16[528,256]{1,0:T(8,128)(2,1)S(1)}, bf16[528,256]{1,0:T(8,128)(2,1)S(1)}, u32[]{:S(2)}, u32[]{:S(2)}) collective-permute-start(bf16[528,256]{1,0:T(8,128)(2,1)S(1)} %concatenate.6.own_ref), channel_id=1, source_target_pairs={{3,2},{2,1},{7,6},{6,5},{11,10},{10,9},{15,14},{14,13},{19,18},{18... | collective-permute-start | bytes 811016 | tf_op jit(solution)/shard_map/ppermute | solution.py:402
  50.7 10.9 %collective-permute-start.9 = (bf16[528,256]{1,0:T(8,128)(2,1)S(1)}, bf16[528,256]{1,0:T(8,128)(2,1)S(1)}, u32[]{:S(2)}, u32[]{:S(2)}) collective-permute-start(bf16[528,256]{1,0:T(8,128)(2,1)S(1)} %combine.3), channel_id=1, source_target_pairs={{1,0},{0,1},{5,4},{4,5},{9,8},{8,9},{13,12},{12,13},{17,16},{16,17... | collective-permute-start | bytes 811016 | tf_op jit(solution)/shard_map/ppermute | solution.py:408
  53.8 12.0 %collective-permute-start.6 = (bf16[528,256]{1,0:T(8,128)(2,1)S(1)}, bf16[528,256]{1,0:T(8,128)(2,1)S(1)}, u32[]{:S(2)}, u32[]{:S(2)}) collective-permute-start(bf16[528,256]{1,0:T(8,128)(2,1)S(1)} %combine.2), channel_id=1, source_target_pairs={{1,0},{0,1},{5,4},{4,5},{9,8},{8,9},{13,12},{12,13},{17,16},{16,17... | collective-permute-start | bytes 811016 | tf_op jit(solution)/shard_map/ppermute | solution.py:408

commit v2 on v1

v2 whole, which is shorter than its diff:
```python
import functools

import jax
import jax.numpy as jnp
from jax import lax
from jax.experimental import pallas as pl
from jax.experimental.pallas import tpu as pltpu
from jax.sharding import PartitionSpec as P

F32 = jnp.float32
BF16 = jnp.bfloat16
LANES = 128
GROUP = 4
GAIN_ROWS = 16
MIB = 2**20
VMEM = pl.BlockSpec(memory_space=pltpu.VMEM)
SMEM = pl.BlockSpec(memory_space=pltpu.SMEM)
ANY = pl.BlockSpec(memory_space=pl.ANY)
HBM = pl.BlockSpec(memory_space=pltpu.HBM)
in_hbm = functools.partial(pltpu.with_memory_space_constraint, memory_space=pltpu.HBM)
in_vmem = functools.partial(pltpu.with_memory_space_constraint, memory_space=pltpu.VMEM)


def edges_kernel(s_ref, west_ref, east_ref, south_ref, north_ref, sems):
    nx, ny = s_ref.shape[:2]
    pieces = (
        (s_ref.at[0:1], west_ref),
        (s_ref.at[nx - 1 : nx], east_ref),
        (s_ref.at[:, 0:1], south_ref),
        (s_ref.at[:, ny - 1 : ny], north_ref),
    )
    copies = [
        pltpu.make_async_copy(src, dst, sems.at[i]) for i, (src, dst) in enumerate(pieces)
    ]
    for copy in copies:
        copy.start()
    for copy in copies:
        copy.wait()


def edges(spectrum):
    nx, ny, nz, nb = spectrum.shape
    row = jax.ShapeDtypeStruct((1, ny, nz, nb), BF16)
    column = jax.ShapeDtypeStruct((nx, 1, nz, nb), BF16)
    return pl.pallas_call(
        edges_kernel,
        out_shape=(row, row, column, column),
        in_specs=[HBM],
        out_specs=[ANY] * 4,
        scratch_shapes=[pltpu.SemaphoreType.DMA((4,))],
        compiler_params=pltpu.CompilerParams(vmem_limit_bytes=MIB),
        name="edges",
    )(in_hbm(spectrum))


def wide(c, y, shape):
    return jnp.broadcast_to(c[:, y : y + 1], shape)


def inner_kernel(s_any, we_any, wn_any, adv, s_ref, we_ref, wn_ref, sems):
    nx, ny, nz, nb = s_ref.shape
    winds = [
        pltpu.make_async_copy(we_any, we_ref, sems.at[0]),
        pltpu.make_async_copy(wn_any, wn_ref, sems.at[1]),
    ]
    cuts = (0, GROUP + 1, nx // 2 + 1, nx)
    loads = [
        pltpu.make_async_copy(s_any.at[lo:hi], s_ref.at[lo:hi], sems.at[2 + i])
        for i, (lo, hi) in enumerate(zip(cuts, cuts[1:]))
    ]
    for copy in winds + loads:
        copy.start()
    for copy in winds:
        copy.wait()

    half = (nz, LANES)
    none = jnp.zeros((nz, nb), F32)

    def advect(g, carry):
        x = g * GROUP
        before, after = jnp.maximum(x - 1, 0), jnp.minimum(x + GROUP, nx - 1)
        has_before = jnp.where(x > 0, 1.0, 0.0)
        has_after = jnp.where(x + GROUP < nx, 1.0, 0.0)
        us = [we_ref[x + r] for r in range(GROUP)]
        vs = [wn_ref[x + r] for r in range(GROUP)]
        behind = [none] * GROUP
        here = [s_ref[x + r, 0].astype(F32) for r in range(GROUP)]
        for y in range(ny):
            if y < ny - 1:
                ahead = [s_ref[x + r, y + 1].astype(F32) for r in range(GROUP)]
            else:
                ahead = [none] * GROUP
            line = [
                s_ref[before, y].astype(F32) * has_before,
                *here,
                s_ref[after, y].astype(F32) * has_after,
            ]
            for r in range(GROUP):
                u, v = wide(us[r], y, half), wide(vs[r], y, half)
                from_low, from_south = u > 0.0, v > 0.0
                u, v = jnp.abs(u), jnp.abs(v)
                at = pl.ds(pl.multiple_of(((x + r) * ny + y) * nz, 8), nz)
                for t in range(nb // LANES):
                    lanes = slice(t * LANES, (t + 1) * LANES)
                    own = here[r][:, lanes]
                    side = jnp.where(from_low, line[r][:, lanes], line[r + 2][:, lanes])
                    other = jnp.where(from_south, behind[r][:, lanes], ahead[r][:, lanes])
                    adv[t, at, :] = own + u * (side - own) + v * (other - own)
            behind, here = here, ahead
        return carry

    done = 0
    for hi, copy in zip(cuts[1:], loads):
        copy.wait()
        ready = (nx if hi == nx else hi - 1) // GROUP
        lax.fori_loop(done, ready, advect, 0)
        done = ready


def settle_columns(adv, flux_ref, fall, first, count):
    nz, nb = fall.shape
    inverse = 1.0 / (1.0 + fall)
    through = fall * inverse
    tiles = adv.shape[0]

    def settle(g, carry):
        base = pl.multiple_of((first + g * 16) * nz, 128)
        for t in range(tiles):
            lanes = slice(t * LANES, (t + 1) * LANES)
            flows = []
            for half in range(2):
                inflow = jnp.zeros((8, LANES), F32)
                for z in reversed(range(nz)):
                    at = pl.ds(base + half * 8 * nz + z, 8, stride=nz)
                    total = adv[t, at, :] + inflow
                    adv[t, at, :] = total * inverse[z : z + 1, lanes]
                    inflow = total * through[z : z + 1, lanes]
                flows.append(inflow)
            flux_ref[pl.ds(pl.multiple_of(g * 16, 16), 16), lanes] = jnp.concatenate(
                flows, 0
            ).astype(BF16)
        return carry

    lax.fori_loop(0, count // 16, settle, 0)
    gain = jnp.ones((1, nb), F32)
    for z in reversed(range(nz)):
        gain = gain * through[z : z + 1, :]
    flux_ref[pl.ds(count, GAIN_ROWS), :] = jnp.broadcast_to(gain, (GAIN_ROWS, nb)).astype(BF16)


def cloud_kernel(
    place_ref,
    cells_any,
    target_any,
    adv_in,
    west_ref,
    east_ref,
    south_ref,
    north_ref,
    we_ref,
    wn_ref,
    fall_ref,
    pi_ref,
    po_ref,
    lk_ref,
    fr_ref,
    adv,
    flux_ref,
    cells,
    target,
    rows,
    sems,
):
    del adv_in
    nx, nz, ny = we_ref.shape
    nb = fall_ref.shape[1]
    blk, blocks = cells.shape
    pairs = po_ref.shape[0]
    tiles = nb // LANES
    plane = target_any.shape[0] * target_any.shape[1]
    lists = pltpu.make_async_copy(cells_any, cells, sems.at[0])
    routes = pltpu.make_async_copy(target_any.at[place_ref[0], place_ref[1]], target, sems.at[1])
    lists.start()
    routes.start()

    def add(cell, value):
        at = pl.ds(pl.multiple_of(cell, 8), nz)
        for t in range(tiles):
            adv[t, at, :] += value[:, t * LANES : (t + 1) * LANES]

    shape = (nz, nb)
    c_w = jnp.maximum(we_ref[0], 0.0)
    c_e = jnp.maximum(-we_ref[nx - 1], 0.0)
    for y in range(ny):
        add(y * nz, wide(c_w, y, shape) * west_ref[0, y].astype(F32))
        add(((nx - 1) * ny + y) * nz, wide(c_e, y, shape) * east_ref[0, y].astype(F32))

    def sides(i, carry):
        for k in range(4):
            x = i * 4 + k
            v = wn_ref[x]
            c_s = jnp.maximum(v, 0.0)
            c_n = jnp.maximum(-v, 0.0)
            add(x * ny * nz, wide(c_s, 0, shape) * south_ref[x, 0].astype(F32))
            add((x * ny + ny - 1) * nz, wide(c_n, ny - 1, shape) * north_ref[x, 0].astype(F32))
        return carry

    lax.fori_loop(0, nx // 4, sides, 0)
    lists.wait()

    def gather(b, carry):
        base = pl.multiple_of(b * blk, blk)
        for j in range(blk):
            for t in range(tiles):
                rows[t, pl.ds(base + j, 1), :] = adv[t, pl.ds(cells[j, b], 1), :]
        return carry

    lax.fori_loop(0, blocks, gather, 0)

    step = 512
    tile = 256

    def collide(i, carry):
        here = pl.ds(pl.multiple_of(i * step, step), step)
        cloud = jnp.concatenate([rows[t, here, :] for t in range(tiles)], 1).astype(BF16)
        decline = jnp.dot(cloud, lk_ref[...], preferred_element_type=F32)
        losses = cloud.astype(F32) * decline
        total = jnp.dot(losses.astype(BF16), fr_ref[...], preferred_element_type=F32) - losses
        for n in range(pairs // tile):
            left = jnp.dot(
                cloud, pi_ref[:, n * tile : (n + 1) * tile], preferred_element_type=F32
            )
            right = jnp.dot(
                cloud,
                pi_ref[:, pairs + n * tile : pairs + (n + 1) * tile],
                preferred_element_type=F32,
            )
            total = total + jnp.dot(
                (left * right).astype(BF16),
                po_ref[n * tile : (n + 1) * tile, :],
                preferred_element_type=F32,
            )
        total = total.astype(BF16).astype(F32)
        for t in range(tiles):
            rows[t, here, :] += total[:, t * LANES : (t + 1) * LANES]
        return carry

    lax.fori_loop(0, blocks * blk // step, collide, 0)
    routes.wait()

    def scatter(b, carry):
        base = pl.multiple_of(b * blk, blk)

        @pl.when(target[0, b] < plane)
        def _():
            for j in range(blk):
                for t in range(tiles):
                    adv[t, pl.ds(cells[j, b], 1), :] = rows[t, pl.ds(base + j, 1), :]

        return carry

    lax.fori_loop(0, blocks, scatter, 0)
    count = flux_ref.shape[0] - GAIN_ROWS
    settle_columns(adv, flux_ref, fall_ref[...], 0, count)


def settle_kernel(adv, fall_ref, local_any, flux_ref, sems):
    nz = fall_ref.shape[0]
    count = flux_ref.shape[0] - GAIN_ROWS
    first = adv.shape[1] // nz - count
    cut = first * nz
    front = pltpu.make_async_copy(adv.at[:, :cut], local_any.at[:, :cut], sems.at[0])
    back = pltpu.make_async_copy(adv.at[:, cut:], local_any.at[:, cut:], sems.at[1])
    front.start()
    settle_columns(adv, flux_ref, fall_ref[...], first, count)
    back.start()
    front.wait()
    back.wait()


def combine_kernel(zid_ref, own_ref, a_ref, b_ref, out_ref):
    n = own_ref.shape[0] - GAIN_ROWS
    z = zid_ref[0]

    @pl.when(z == 0)
    def _():
        out_ref[...] = b_ref[...]

    @pl.when(z != 0)
    def _():
        gain = own_ref[n : n + GAIN_ROWS, :].astype(F32)

        def some(i, carry):
            at = pl.ds(pl.multiple_of(i * 16, 16), 16)
            out_ref[at, :] = (
                own_ref[at, :].astype(F32) + gain * a_ref[at, :].astype(F32)
            ).astype(BF16)
            return carry

        lax.fori_loop(0, n // 16, some, 0, unroll=4)
        out_ref[n : n + GAIN_ROWS, :] = (
            gain * a_ref[n : n + GAIN_ROWS, :].astype(F32)
        ).astype(BF16)


def combine(zid, own, a, b):
    return pl.pallas_call(
        combine_kernel,
        out_shape=pltpu.VMEM(own.shape, BF16),
        in_specs=[SMEM] + [VMEM] * 3,
        out_specs=VMEM,
        compiler_params=pltpu.CompilerParams(vmem_limit_bytes=4 * MIB),
        name="combine",
    )(zid, own, a, b)


def finish_kernel(
    zid_ref,
    fall_ref,
    a_ref,
    b_ref,
    d_ref,
    local_any,
    prev_ref,
    out_any,
    local,
    inflow,
    stage,
    sems,
    *,
    first,
):
    del prev_ref
    ny, nz, nb = out_any.shape[1:]
    parts, per = stage.shape[:2]
    tiles = nb // LANES
    n = a_ref.shape[0] - GAIN_ROWS
    span = per * ny * nz
    loads = []
    for p in range(parts):
        start = first * ny * nz + p * span
        loads.append(
            pltpu.make_async_copy(
                local_any.at[:, start : start + span],
                local.at[:, p * span : (p + 1) * span],
                sems.at[p],
            )
        )
        loads[-1].start()
    fall = fall_ref[...]
    inverse = 1.0 / (1.0 + fall)
    through = fall * inverse
    carried = jnp.ones((1, nb), F32)
    gains = [None] * nz
    for level in reversed(range(nz)):
        gains[level] = carried * inverse[level : level + 1, :]
        carried = carried * through[level : level + 1, :]
    gain = jnp.concatenate(gains, 0)
    bottom = zid_ref[0] == 0
    mix = jnp.where(bottom, d_ref[n : n + GAIN_ROWS, :], a_ref[n : n + GAIN_ROWS, :]).astype(F32)

    def enter(i, carry):
        at = pl.ds(pl.multiple_of(i * 16, 16), 16)
        a, b, d = a_ref[at, :].astype(F32), b_ref[at, :].astype(F32), d_ref[at, :].astype(F32)
        inflow[at, :] = jnp.where(bottom, d, a) + mix * jnp.where(bottom, b, d)
        return carry

    lax.fori_loop(0, n // 16, enter, 0, unroll=4)
    copies = []
    for p in range(parts):

        def column(x, carry, p=p):
            base = (p * per + x) * ny
            for y in range(ny):
                at = pl.ds(pl.multiple_of((base + y) * nz, 8), nz)
                m = jnp.broadcast_to(inflow[pl.ds(base + y, 1), :], (nz, nb))
                own = jnp.concatenate([local[t, at, :] for t in range(tiles)], 1)
                stage[p, x, y] = (own + m * gain).astype(BF16)
            return carry

        loads[p].wait()
        lax.fori_loop(0, per, column, 0)
        copy = pltpu.make_async_copy(
            stage.at[p], out_any.at[first + p * per : first + (p + 1) * per], sems.at[p]
        )
        copy.start()
        copies.append(copy)
    for copy in copies:
        copy.wait()


def finish(zid, fall, a, b, d, local, prev, shape, first, parts):
    nx, ny, nz, nb = shape
    n = a.shape[0] - GAIN_ROWS
    given = (zid, fall, a, b, d, in_hbm(local)) + (() if prev is None else (prev,))
    kernel = functools.partial(finish_kernel, first=first)
    if prev is None:
        inner = kernel

        def kernel(*refs):
            return inner(*refs[:6], None, *refs[6:])

    return pl.pallas_call(
        kernel,
        out_shape=jax.ShapeDtypeStruct(shape, BF16),
        in_specs=[SMEM] + [VMEM] * 4 + [HBM] + [ANY] * (prev is not None),
        out_specs=ANY,
        scratch_shapes=[
            pltpu.VMEM((nb // LANES, n * nz, LANES), F32),
            pltpu.VMEM((n, nb), F32),
            pltpu.VMEM((parts, n // ny // parts, ny, nz, nb), BF16),
            pltpu.SemaphoreType.DMA((parts,)),
        ],
        input_output_aliases={} if prev is None else {6: 0},
        compiler_params=pltpu.CompilerParams(vmem_limit_bytes=16 * MIB),
        name="finish",
    )(*given)


def inner(spectrum, we, wn):
    nx, ny, nz, nb = spectrum.shape
    return pl.pallas_call(
        inner_kernel,
        out_shape=pltpu.VMEM((nb // LANES, nx * ny * nz, LANES), F32),
        in_specs=[HBM] * 3,
        out_specs=VMEM,
        scratch_shapes=[
            pltpu.VMEM(spectrum.shape, BF16),
            pltpu.VMEM(we.shape, F32),
            pltpu.VMEM(wn.shape, F32),
            pltpu.SemaphoreType.DMA((5,)),
        ],
        compiler_params=pltpu.CompilerParams(vmem_limit_bytes=8 * MIB),
        cost_estimate=pl.CostEstimate(flops=10**7, bytes_accessed=16 * MIB, transcendentals=0),
        name="inner",
    )(in_hbm(spectrum), in_hbm(we), in_hbm(wn))


def cloud(place, cells, target, adv, halo, we, wn, fall, pi, po, lk, fr, count):
    blk, blocks = cells.shape
    nb = fall.shape[1]
    return pl.pallas_call(
        cloud_kernel,
        out_shape=(
            pltpu.VMEM(adv.shape, F32),
            pltpu.VMEM((count + GAIN_ROWS, nb), BF16),
        ),
        in_specs=[SMEM, ANY, ANY] + [VMEM] * 12,
        out_specs=(VMEM, VMEM),
        scratch_shapes=[
            pltpu.SMEM((blk, blocks), jnp.int32),
            pltpu.SMEM((1, blocks), jnp.int32),
            pltpu.VMEM((nb // LANES, blk * blocks, LANES), F32),
            pltpu.SemaphoreType.DMA((2,)),
        ],
        input_output_aliases={3: 0},
        compiler_params=pltpu.CompilerParams(vmem_limit_bytes=16 * MIB),
        name="cloud",
    )(place, cells, target, in_vmem(adv), *halo, we, wn, fall, pi, po, lk, fr)


def settle(adv, fall, count):
    nb = fall.shape[1]
    return pl.pallas_call(
        settle_kernel,
        out_shape=(
            pltpu.HBM(adv.shape, F32),
            pltpu.VMEM((count + GAIN_ROWS, nb), BF16),
        ),
        in_specs=[VMEM, VMEM],
        out_specs=(HBM, VMEM),
        scratch_shapes=[pltpu.SemaphoreType.DMA((2,))],
        compiler_params=pltpu.CompilerParams(vmem_limit_bytes=4 * MIB),
        name="settle",
    )(in_vmem(adv), fall)


def body(
    spectrum,
    wind_east,
    wind_north,
    fall_rate,
    cloud_cells,
    block_target,
    pair_inputs,
    pair_outputs,
    loss_kernel,
    fragments,
):
    nx, ny, nz, nb = spectrum.shape
    n_gx, n_gy = (lax.axis_size(a) for a in ("gx", "gy"))
    up_x = [(i, (i + 1) % n_gx) for i in range(n_gx)]
    up_y = [(i, (i + 1) % n_gy) for i in range(n_gy)]
    low_x, high_x, low_y, high_y = edges(spectrum)
    south = lax.ppermute(high_y, "gy", up_y)
    north = lax.ppermute(low_y, "gy", [(b, a) for a, b in up_y])
    west = lax.ppermute(high_x, "gx", up_x)
    east = lax.ppermute(low_x, "gx", [(b, a) for a, b in up_x])

    we, wn = wind_east.transpose(0, 2, 1), wind_north.transpose(0, 2, 1)
    adv = inner(spectrum, we, wn)
    blocks, blk = cloud_cells.shape[3:]
    cells = cloud_cells.reshape(blocks, blk).T
    place = jnp.stack([lax.axis_index("gx"), lax.axis_index("gy")])
    zid = lax.axis_index("gz").reshape(1)
    columns = nx * ny
    first = columns // 2
    adv, flux = cloud(
        place,
        cells,
        block_target,
        adv,
        (west, east, south, north),
        we,
        wn,
        fall_rate,
        pair_inputs,
        pair_outputs,
        loss_kernel,
        fragments,
        first,
    )

    def begin(flux):
        a = lax.ppermute(flux, "gz", [(3, 2), (2, 1)])
        b = lax.ppermute(flux, "gz", [(3, 0)])
        return flux, a, b

    front = begin(flux)
    local, flux = settle(adv, fall_rate, columns - first)
    back = begin(flux)
    ready = []
    for flux, a, b in (front, back):
        ready.append((a, b, lax.ppermute(combine(zid, flux, a, b), "gz", [(1, 0), (0, 1)])))
    front, back = ready
    shape = spectrum.shape
    out = finish(zid, fall_rate, *front, local, None, shape, 0, 4)
    out = finish(zid, fall_rate, *back, local, out, shape, first // ny, 4)
    return out


def solution(mesh):
    in_specs = (
        P("gx", "gy", "gz", None),
        P("gx", "gy", "gz"),
        P("gx", "gy", "gz"),
        P("gz", None),
        P("gx", "gy", "gz", None, None),
        P(None, None, "gz", None),
        P(),
        P(),
        P(),
        P(),
    )
    out_specs = P("gx", "gy", "gz", None)
    return jax.shard_map(body, mesh=mesh, in_specs=in_specs, out_specs=out_specs, check_vma=False)
```

time: 70.8 us -> 53.2 us (0.75)
  the two profiles are of different devices: /device:TPU:98 before, /device:TPU:2 now
where the time goes in v2:
time: 53.2 us; the launch traced here: 53 us
  Pallas kernels  25.7 us (48%)
  starting transfers between devices  17.6 us (33%)
  waiting for transfers between devices  9.33 us (18%)
    pallas_call x1, Pallas kernels, cloud(): pl.pallas_call(cloud_kernel, out_shape=(pltpu.VMEM(adv.shape, F32), pltpu...  9.31 us
    ppermute x2, waiting for transfers between devices, begin(): b = lax.ppermute(flux, 'gz', [(3, 0)])  6.64 us
    pallas_call x2, Pallas kernels, finish(): pl.pallas_call(kernel, out_shape=jax.ShapeDtypeStruct(shape, BF16), in_sp...  6.44 us
    ppermute x2, starting transfers between devices, body(): lax.ppermute(combine(zid, flux, a, b), 'gz', [(1, 0), (0, 1)])  6.09 us
    pallas_call x1, Pallas kernels, inner(): pl.pallas_call(inner_kernel, out_shape=pltpu.VMEM((nb // LANES, nx * ny *...  5.06 us
    ppermute x1, starting transfers between devices, body(): north = lax.ppermute(low_y, 'gy', [(b, a) for a, b in up_y])  3.94 us
    pallas_call x1, Pallas kernels, settle(): pl.pallas_call(settle_kernel, out_shape=(pltpu.HBM(adv.shape, F32), pltpu...  3.55 us
    ppermute x2, waiting for transfers between devices, body(): lax.ppermute(combine(zid, flux, a, b), 'gz', [(1, 0), (0, 1)])  2.68 us
  transfers between devices with their start and end apart: 10, of which 3 were waited for; matrix products, arithmetic and copies ran while one was open for 0% of the time, Pallas kernels for 22%

profile of v2, /device:TPU:2, one launch (start us, length us, event | category | flops | bytes accessed | tf_op | source)
XLA Modules:
  0.0 53.0 jit_solution(15485581623141106105)
XLA Ops:
  0.0 0.0 copy-start.2
  0.0 0.0 copy-start.1
  0.0 0.0 copy-start.6
  0.0 0.0 copy-start.5
  0.0 0.0 copy-start.4
  0.0 0.0 copy-start.3
  0.0 0.0 copy-start
  0.0 0.0 copy-start.7
  0.1 0.0 copy-start.8
  0.1 1.3 %edges.1 = (bf16[1,32,8,256]{3,2,1,0:T(8,128)(2,1)S(1)}, bf16[1,32,8,256]{3,2,1,0:T(8,128)(2,1)S(1)}, bf16[32,1,8,256]{3,2,1,0:T(8,128)(2,1)S(1)}, bf16[32,1,8,256]{3,2,1,0:T(8,128)(2,1)S(1)}) custom-call(bf16[32,32,8,256]{3,2,1,0:T(8,128)(2,1)} %s_ref.1), custom_call_target="tpu_custom_call" | custom-call | tf_op jit(solution)/shard_map/edges/pallas_call | solution.py:45
  1.4 0.0 collective-permute-start
  1.4 1.7 %collective-permute-start.1 = (bf16[1,32,8,256]{3,2,1,0:T(8,128)(2,1)S(1)}, bf16[1,32,8,256]{3,2,1,0:T(8,128)(2,1)S(1)}, u32[]{:S(2)}, u32[]{:S(2)}) collective-permute-start(bf16[1,32,8,256]{3,2,1,0:T(8,128)(2,1)S(1)} %get-tuple-element.14), channel_id=1, source_target_pairs={{32,0},{64,32},{96,64},{128,96},{160,128},{192,160},{224,192},{0,2... | collective-permute-start | bytes 393224 | tf_op jit(solution)/shard_map/ppermute | solution.py:498
  3.1 1.9 %collective-permute-start.2 = (bf16[32,1,8,256]{3,2,1,0:T(8,128)(2,1)S(1)}, bf16[32,1,8,256]{3,2,1,0:T(8,128)(2,1)S(1)}, u32[]{:S(2)}, u32[]{:S(2)}) collective-permute-start(bf16[32,1,8,256]{3,2,1,0:T(8,128)(2,1)S(1)} %get-tuple-element.15), channel_id=1, source_target_pairs={{0,4},{4,8},{8,12},{12,16},{16,20},{20,24},{24,28},{28,0},{1,5},{5... | collective-permute-start | bytes 393224 | tf_op jit(solution)/shard_map/ppermute | solution.py:495
  5.0 3.9 %collective-permute-start.3 = (bf16[32,1,8,256]{3,2,1,0:T(8,128)(2,1)S(1)}, bf16[32,1,8,256]{3,2,1,0:T(8,128)(2,1)S(1)}, u32[]{:S(2)}, u32[]{:S(2)}) collective-permute-start(bf16[32,1,8,256]{3,2,1,0:T(8,128)(2,1)S(1)} %get-tuple-element.16), channel_id=1, source_target_pairs={{4,0},{8,4},{12,8},{16,12},{20,16},{24,20},{28,24},{0,28},{5,1},{9... | collective-permute-start | bytes 393224 | tf_op jit(solution)/shard_map/ppermute | solution.py:496
  9.0 5.1 %inner.1.adv_in = f32[2,8192,128]{2,1,0:T(8,128)S(1)} custom-call(bf16[32,32,8,256]{3,2,1,0:T(8,128)(2,1)} %s_ref.1, f32[32,8,32]{2,1,0:T(8,128)} %bitcast.8, f32[32,8,32]{2,1,0:T(8,128)} %bitcast.10), custom_call_target="tpu_custom_call" | custom-call | flops 10000000 | bytes 16777216 | tf_op jit(solution)/shard_map/inner/pallas_call | solution.py:422
  14.0 0.1 pad_add_fusion.place_ref
  14.1 0.0 collective-permute-done.west_ref
  14.1 0.0 collective-permute-done.1.east_ref
  14.1 0.0 collective-permute-done.2.south_ref
  14.1 0.0 collective-permute-done.3.north_ref
  14.1 0.0 copy-done.2
  14.1 0.0 copy-done.1
  14.2 0.0 copy-done.6
  14.2 0.0 copy-done.5
  14.2 0.0 copy-done.4
  14.2 0.0 copy-done.3
  14.2 0.0 copy-done
  14.2 0.0 copy-done.7
  14.2 0.0 copy-done.8
  14.2 9.3 %cloud.1 = (f32[2,8192,128]{2,1,0:T(8,128)S(1)}, bf16[528,256]{1,0:T(8,128)(2,1)S(1)}) custom-call(s32[2]{0:T(128)S(1)} %pad_add_fusion.place_ref, s32[16,64]{1,0:T(8,128)S(1)} %bitcast.12, s32[8,8,1,64]{3,2,1,0:T(1,128)S(1)} %copy-done.7, f32[2,8192,128]{2,1,0:T(8,128)S(1)} %inner.1.adv_in, ...), custom_call_target="tpu_custom_call", output_to_operand_aliasing={{0}: (3, {})} | custom-call | tf_op jit(solution)/shard_map/cloud/pallas_call | solution.py:442
  23.5 1.3 %collective-permute-start.8 = (bf16[528,256]{1,0:T(8,128)(2,1)S(1)}, bf16[528,256]{1,0:T(8,128)(2,1)S(1)}, u32[]{:S(2)}, u32[]{:S(2)}) collective-permute-start(bf16[528,256]{1,0:T(8,128)(2,1)S(1)} %get-tuple-element.20.own_ref), channel_id=1, source_target_pairs={{3,0},{7,4},{11,8},{15,12},{19,16},{23,20},{27,24},{31,28},{35,32}... | collective-permute-start | bytes 811016 | tf_op jit(solution)/shard_map/ppermute | solution.py:526
  24.8 0.7 %collective-permute-start.7 = (bf16[528,256]{1,0:T(8,128)(2,1)S(1)}, bf16[528,256]{1,0:T(8,128)(2,1)S(1)}, u32[]{:S(2)}, u32[]{:S(2)}) collective-permute-start(bf16[528,256]{1,0:T(8,128)(2,1)S(1)} %get-tuple-element.20.own_ref), channel_id=1, source_target_pairs={{3,2},{2,1},{7,6},{6,5},{11,10},{10,9},{15,14},{14,13},{19,18},{18... | collective-permute-start | bytes 811016 | tf_op jit(solution)/shard_map/ppermute | solution.py:525
  25.5 3.5 %settle.1 = (f32[2,8192,128]{2,1,0:T(8,128)}, bf16[528,256]{1,0:T(8,128)(2,1)S(1)}) custom-call(f32[2,8192,128]{2,1,0:T(8,128)S(1)} %get-tuple-element.17.adv, f32[8,256]{1,0:T(8,128)S(1)} %copy-done.6), custom_call_target="tpu_custom_call" | custom-call | tf_op jit(solution)/shard_map/settle/pallas_call | solution.py:464
  29.1 1.3 %collective-permute-start.5 = (bf16[528,256]{1,0:T(8,128)(2,1)S(1)}, bf16[528,256]{1,0:T(8,128)(2,1)S(1)}, u32[]{:S(2)}, u32[]{:S(2)}) collective-permute-start(bf16[528,256]{1,0:T(8,128)(2,1)S(1)} %get-tuple-element.18.own_ref), channel_id=1, source_target_pairs={{3,0},{7,4},{11,8},{15,12},{19,16},{23,20},{27,24},{31,28},{35,32}... | collective-permute-start | bytes 811016 | tf_op jit(solution)/shard_map/ppermute | solution.py:526
  30.4 0.7 %collective-permute-start.4 = (bf16[528,256]{1,0:T(8,128)(2,1)S(1)}, bf16[528,256]{1,0:T(8,128)(2,1)S(1)}, u32[]{:S(2)}, u32[]{:S(2)}) collective-permute-start(bf16[528,256]{1,0:T(8,128)(2,1)S(1)} %get-tuple-element.18.own_ref), channel_id=1, source_target_pairs={{3,2},{2,1},{7,6},{6,5},{11,10},{10,9},{15,14},{14,13},{19,18},{18... | collective-permute-start | bytes 811016 | tf_op jit(solution)/shard_map/ppermute | solution.py:525
  31.1 3.5 %collective-permute-done.8.b_ref.refs_3_ = bf16[528,256]{1,0:T(8,128)(2,1)S(1)} collective-permute-done((bf16[528,256]{1,0:T(8,128)(2,1)S(1)}, bf16[528,256]{1,0:T(8,128)(2,1)S(1)}, u32[]{:S(2)}, u32[]{:S(2)}) %collective-permute-start.8) | collective-permute-done | bytes 270368 | tf_op jit(solution)/shard_map/ppermute | solution.py:526
  34.6 0.0 collective-permute-done.7.a_ref.refs_2_
  34.7 3.1 %collective-permute-start.9 = (bf16[528,256]{1,0:T(8,128)(2,1)S(1)}, bf16[528,256]{1,0:T(8,128)(2,1)S(1)}, u32[]{:S(2)}, u32[]{:S(2)}) collective-permute-start(bf16[528,256]{1,0:T(8,128)(2,1)S(1)} %combine.3), channel_id=1, source_target_pairs={{1,0},{0,1},{5,4},{4,5},{9,8},{8,9},{13,12},{12,13},{17,16},{16,17... | collective-permute-start | bytes 811016 | tf_op jit(solution)/shard_map/ppermute | solution.py:534
  37.7 3.1 %collective-permute-done.5.b_ref = bf16[528,256]{1,0:T(8,128)(2,1)S(1)} collective-permute-done((bf16[528,256]{1,0:T(8,128)(2,1)S(1)}, bf16[528,256]{1,0:T(8,128)(2,1)S(1)}, u32[]{:S(2)}, u32[]{:S(2)}) %collective-permute-start.5) | collective-permute-done | bytes 270368 | tf_op jit(solution)/shard_map/ppermute | solution.py:526
  40.8 0.0 collective-permute-done.4.a_ref
  40.8 3.0 %collective-permute-start.6 = (bf16[528,256]{1,0:T(8,128)(2,1)S(1)}, bf16[528,256]{1,0:T(8,128)(2,1)S(1)}, u32[]{:S(2)}, u32[]{:S(2)}) collective-permute-start(bf16[528,256]{1,0:T(8,128)(2,1)S(1)} %combine.2), channel_id=1, source_target_pairs={{1,0},{0,1},{5,4},{4,5},{9,8},{8,9},{13,12},{12,13},{17,16},{16,17... | collective-permute-start | bytes 811016 | tf_op jit(solution)/shard_map/ppermute | solution.py:534
  43.9 0.0 collective-permute-done.9.refs_4_
  43.9 3.2 %finish.2.prev_ref = bf16[32,32,8,256]{3,2,1,0:T(8,128)(2,1)} custom-call(s32[1]{0:T(128)} %bitcast.zid_ref.refs_0_, f32[8,256]{1,0:T(8,128)S(1)} %copy-done.6, bf16[528,256]{1,0:T(8,128)(2,1)S(1)} %collective-permute-done.7.a_ref.refs_2_, bf16[528,256]{1,0:T(8,128)(2,1)S(1)} %collective-permute-done.8.b_ref.refs_3_, ...), custom_call_target="tpu_custom_call" | custom-call | tf_op jit(solution)/shard_map/finish/pallas_call | solution.py:403
  47.1 2.7 %collective-permute-done.6.d_ref = bf16[528,256]{1,0:T(8,128)(2,1)S(1)} collective-permute-done((bf16[528,256]{1,0:T(8,128)(2,1)S(1)}, bf16[528,256]{1,0:T(8,128)(2,1)S(1)}, u32[]{:S(2)}, u32[]{:S(2)}) %collective-permute-start.6) | collective-permute-done | bytes 270368 | tf_op jit(solution)/shard_map/ppermute | solution.py:534
  49.8 3.2 %finish.3 = bf16[32,32,8,256]{3,2,1,0:T(8,128)(2,1)} custom-call(s32[1]{0:T(128)} %bitcast.zid_ref.refs_0_, f32[8,256]{1,0:T(8,128)S(1)} %copy-done.6, bf16[528,256]{1,0:T(8,128)(2,1)S(1)} %collective-permute-done.4.a_ref, bf16[528,256]{1,0:T(8,128)(2,1)S(1)} %collective-permute-done.5.b_ref, ...), custom_call_target="tpu_custom_call", output_to_operand_aliasing={{}: (6, {})} | custom-call | tf_op jit(solution)/shard_map/finish/pallas_call | solution.py:403
  (2 shorter events, 0.0 us)
Async XLA Ops:
  0.0 14.1 %copy-start.2 = (f32[32,32,8]{1,2,0:T(8,128)S(1)}, f32[32,32,8]{1,2,0:T(8,128)}, u32[]{:S(2)}) copy-start(f32[32,32,8]{1,2,0:T(8,128)} %param.12) | copy-start | bytes 98308
  0.0 14.1 %copy-start.1 = (f32[32,32,8]{1,2,0:T(8,128)S(1)}, f32[32,32,8]{1,2,0:T(8,128)}, u32[]{:S(2)}) copy-start(f32[32,32,8]{1,2,0:T(8,128)} %param.11) | copy-start | bytes 98308
  0.0 14.2 %copy-start.6 = (f32[8,256]{1,0:T(8,128)S(1)}, f32[8,256]{1,0:T(8,128)}, u32[]{:S(2)}) copy-start(f32[8,256]{1,0:T(8,128)} %fall_ref.5) | copy-start | bytes 24580
  0.0 14.2 %copy-start.5 = (bf16[256,256]{1,0:T(8,128)(2,1)S(1)}, bf16[256,256]{1,0:T(8,128)(2,1)}, u32[]{:S(2)}) copy-start(bf16[256,256]{1,0:T(8,128)(2,1)} %fr_ref.1) | copy-start | bytes 393220
  0.0 14.2 %copy-start.4 = (bf16[256,256]{1,0:T(8,128)(2,1)S(1)}, bf16[256,256]{1,0:T(8,128)(2,1)}, u32[]{:S(2)}) copy-start(bf16[256,256]{1,0:T(8,128)(2,1)} %lk_ref.1) | copy-start | bytes 393220
  0.0 14.2 %copy-start.3 = (bf16[1024,256]{1,0:T(8,128)(2,1)S(1)}, bf16[1024,256]{1,0:T(8,128)(2,1)}, u32[]{:S(2)}) copy-start(bf16[1024,256]{1,0:T(8,128)(2,1)} %po_ref.1) | copy-start | bytes 1572868
  0.0 14.2 %copy-start = (bf16[256,2048]{1,0:T(8,128)(2,1)S(1)}, bf16[256,2048]{1,0:T(8,128)(2,1)}, u32[]{:S(2)}) copy-start(bf16[256,2048]{1,0:T(8,128)(2,1)} %pi_ref.1) | copy-start | bytes 3145732
  0.0 14.2 %copy-start.7 = (s32[8,8,1,64]{3,2,1,0:T(1,128)S(1)}, s32[8,8,1,64]{3,2,1,0:T(1,128)}, u32[]{:S(2)}) copy-start(s32[8,8,1,64]{3,2,1,0:T(1,128)} %target_any.1) | copy-start | bytes 49156
  0.1 14.2 %copy-start.8 = (s32[1,1,1,64,16]{3,4,2,1,0:T(8,128)S(1)}, s32[1,1,1,64,16]{3,4,2,1,0:T(8,128)}, u32[]{:S(2)}) copy-start(s32[1,1,1,64,16]{3,4,2,1,0:T(8,128)} %param.14) | copy-start | bytes 12292
  1.4 12.8 %collective-permute-start = (bf16[1,32,8,256]{3,2,1,0:T(8,128)(2,1)S(1)}, bf16[1,32,8,256]{3,2,1,0:T(8,128)(2,1)S(1)}, u32[]{:S(2)}, u32[]{:S(2)}) collective-permute-start(bf16[1,32,8,256]{3,2,1,0:T(8,128)(2,1)S(1)} %get-tuple-element.13), channel_id=1, source_target_pairs={{0,32},{32,64},{64,96},{96,128},{128,160},{160,192},{192,224},{224... | collective-permute-start | bytes 393224 | tf_op jit(solution)/shard_map/ppermute | solution.py:497
  1.4 12.7 %collective-permute-start.1 = (bf16[1,32,8,256]{3,2,1,0:T(8,128)(2,1)S(1)}, bf16[1,32,8,256]{3,2,1,0:T(8,128)(2,1)S(1)}, u32[]{:S(2)}, u32[]{:S(2)}) collective-permute-start(bf16[1,32,8,256]{3,2,1,0:T(8,128)(2,1)S(1)} %get-tuple-element.14), channel_id=1, source_target_pairs={{32,0},{64,32},{96,64},{128,96},{160,128},{192,160},{224,192},{0,2... | collective-permute-start | bytes 393224 | tf_op jit(solution)/shard_map/ppermute | solution.py:498
  3.1 11.0 %collective-permute-start.2 = (bf16[32,1,8,256]{3,2,1,0:T(8,128)(2,1)S(1)}, bf16[32,1,8,256]{3,2,1,0:T(8,128)(2,1)S(1)}, u32[]{:S(2)}, u32[]{:S(2)}) collective-permute-start(bf16[32,1,8,256]{3,2,1,0:T(8,128)(2,1)S(1)} %get-tuple-element.15), channel_id=1, source_target_pairs={{0,4},{4,8},{8,12},{12,16},{16,20},{20,24},{24,28},{28,0},{1,5},{5... | collective-permute-start | bytes 393224 | tf_op jit(solution)/shard_map/ppermute | solution.py:495
  5.0 9.1 %collective-permute-start.3 = (bf16[32,1,8,256]{3,2,1,0:T(8,128)(2,1)S(1)}, bf16[32,1,8,256]{3,2,1,0:T(8,128)(2,1)S(1)}, u32[]{:S(2)}, u32[]{:S(2)}) collective-permute-start(bf16[32,1,8,256]{3,2,1,0:T(8,128)(2,1)S(1)} %get-tuple-element.16), channel_id=1, source_target_pairs={{4,0},{8,4},{12,8},{16,12},{20,16},{24,20},{28,24},{0,28},{5,1},{9... | collective-permute-start | bytes 393224 | tf_op jit(solution)/shard_map/ppermute | solution.py:496
  23.5 11.1 %collective-permute-start.8 = (bf16[528,256]{1,0:T(8,128)(2,1)S(1)}, bf16[528,256]{1,0:T(8,128)(2,1)S(1)}, u32[]{:S(2)}, u32[]{:S(2)}) collective-permute-start(bf16[528,256]{1,0:T(8,128)(2,1)S(1)} %get-tuple-element.20.own_ref), channel_id=1, source_target_pairs={{3,0},{7,4},{11,8},{15,12},{19,16},{23,20},{27,24},{31,28},{35,32}... | collective-permute-start | bytes 811016 | tf_op jit(solution)/shard_map/ppermute | solution.py:526
  24.8 9.8 %collective-permute-start.7 = (bf16[528,256]{1,0:T(8,128)(2,1)S(1)}, bf16[528,256]{1,0:T(8,128)(2,1)S(1)}, u32[]{:S(2)}, u32[]{:S(2)}) collective-permute-start(bf16[528,256]{1,0:T(8,128)(2,1)S(1)} %get-tuple-element.20.own_ref), channel_id=1, source_target_pairs={{3,2},{2,1},{7,6},{6,5},{11,10},{10,9},{15,14},{14,13},{19,18},{18... | collective-permute-start | bytes 811016 | tf_op jit(solution)/shard_map/ppermute | solution.py:525
  29.1 11.7 %collective-permute-start.5 = (bf16[528,256]{1,0:T(8,128)(2,1)S(1)}, bf16[528,256]{1,0:T(8,128)(2,1)S(1)}, u32[]{:S(2)}, u32[]{:S(2)}) collective-permute-start(bf16[528,256]{1,0:T(8,128)(2,1)S(1)} %get-tuple-element.18.own_ref), channel_id=1, source_target_pairs={{3,0},{7,4},{11,8},{15,12},{19,16},{23,20},{27,24},{31,28},{35,32}... | collective-permute-start | bytes 811016 | tf_op jit(solution)/shard_map/ppermute | solution.py:526
  30.4 10.4 %collective-permute-start.4 = (bf16[528,256]{1,0:T(8,128)(2,1)S(1)}, bf16[528,256]{1,0:T(8,128)(2,1)S(1)}, u32[]{:S(2)}, u32[]{:S(2)}) collective-permute-start(bf16[528,256]{1,0:T(8,128)(2,1)S(1)} %get-tuple-element.18.own_ref), channel_id=1, source_target_pairs={{3,2},{2,1},{7,6},{6,5},{11,10},{10,9},{15,14},{14,13},{19,18},{18... | collective-permute-start | bytes 811016 | tf_op jit(solution)/shard_map/ppermute | solution.py:525
  34.7 9.2 %collective-permute-start.9 = (bf16[528,256]{1,0:T(8,128)(2,1)S(1)}, bf16[528,256]{1,0:T(8,128)(2,1)S(1)}, u32[]{:S(2)}, u32[]{:S(2)}) collective-permute-start(bf16[528,256]{1,0:T(8,128)(2,1)S(1)} %combine.3), channel_id=1, source_target_pairs={{1,0},{0,1},{5,4},{4,5},{9,8},{8,9},{13,12},{12,13},{17,16},{16,17... | collective-permute-start | bytes 811016 | tf_op jit(solution)/shard_map/ppermute | solution.py:534
  40.8 9.0 %collective-permute-start.6 = (bf16[528,256]{1,0:T(8,128)(2,1)S(1)}, bf16[528,256]{1,0:T(8,128)(2,1)S(1)}, u32[]{:S(2)}, u32[]{:S(2)}) collective-permute-start(bf16[528,256]{1,0:T(8,128)(2,1)S(1)} %combine.2), channel_id=1, source_target_pairs={{1,0},{0,1},{5,4},{4,5},{9,8},{8,9},{13,12},{12,13},{17,16},{16,17... | collective-permute-start | bytes 811016 | tf_op jit(solution)/shard_map/ppermute | solution.py:534

commit v3 on v2

--- a/solution.py
+++ b/solution.py
@@ -141,7 +141,7 @@
             ).astype(BF16)
         return carry
 
-    lax.fori_loop(0, count // 16, settle, 0)
+    lax.fori_loop(0, count // 16, settle, 0, unroll=2)
     gain = jnp.ones((1, nb), F32)
     for z in reversed(range(nz)):
         gain = gain * through[z : z + 1, :]
@@ -215,10 +215,10 @@
                 rows[t, pl.ds(base + j, 1), :] = adv[t, pl.ds(cells[j, b], 1), :]
         return carry
 
-    lax.fori_loop(0, blocks, gather, 0)
-
-    step = 512
-    tile = 256
+    lax.fori_loop(0, blocks, gather, 0, unroll=2)
+
+    step = 1024
+    tile = 512
 
     def collide(i, carry):
         here = pl.ds(pl.multiple_of(i * step, step), step)
@@ -259,7 +259,7 @@
 
         return carry
 
-    lax.fori_loop(0, blocks, scatter, 0)
+    lax.fori_loop(0, blocks, scatter, 0, unroll=4)
     count = flux_ref.shape[0] - GAIN_ROWS
     settle_columns(adv, flux_ref, fall_ref[...], 0, count)
 
@@ -504,7 +504,7 @@
     place = jnp.stack([lax.axis_index("gx"), lax.axis_index("gy")])
     zid = lax.axis_index("gz").reshape(1)
     columns = nx * ny
-    first = columns // 2
+    first = 16 * ny
     adv, flux = cloud(
         place,
         cells,

time: 53.2 us -> 51.9 us (0.976)
  Pallas kernels: 25.7 us -> 24.3 us
    pallas_call x1, Pallas kernels: 9.31 us -> 8.19 us  [cloud(): pl.pallas_call(cloud_kernel, out_shape=(pltpu.VMEM(adv.shape, F32), pltpu...]
  transfers between devices with their start and end apart: 10 -> 10, of which waited for: 3 -> 3; matrix products, arithmetic and copies ran while one was open for 0% -> 0% of each run, Pallas kernels for 22% -> 23%
where the time goes in v3:
time: 51.9 us; the launch traced here: 51.7 us
  Pallas kernels  24.3 us (47%)
  starting transfers between devices  17.6 us (34%)
  waiting for transfers between devices  9.33 us (18%)
    pallas_call x1, Pallas kernels, cloud(): pl.pallas_call(cloud_kernel, out_shape=(pltpu.VMEM(adv.shape, F32), pltpu...  8.19 us
    ppermute x2, waiting for transfers between devices, begin(): b = lax.ppermute(flux, 'gz', [(3, 0)])  6.63 us
    pallas_call x2, Pallas kernels, finish(): pl.pallas_call(kernel, out_shape=jax.ShapeDtypeStruct(shape, BF16), in_sp...  6.44 us
    ppermute x2, starting transfers between devices, body(): lax.ppermute(combine(zid, flux, a, b), 'gz', [(1, 0), (0, 1)])  6.09 us
    pallas_call x1, Pallas kernels, inner(): pl.pallas_call(inner_kernel, out_shape=pltpu.VMEM((nb // LANES, nx * ny *...  5.06 us
    ppermute x1, starting transfers between devices, body(): north = lax.ppermute(low_y, 'gy', [(b, a) for a, b in up_y])  3.94 us
    pallas_call x1, Pallas kernels, settle(): pl.pallas_call(settle_kernel, out_shape=(pltpu.HBM(adv.shape, F32), pltpu...  3.33 us
    ppermute x2, waiting for transfers between devices, body(): lax.ppermute(combine(zid, flux, a, b), 'gz', [(1, 0), (0, 1)])  2.68 us
  transfers between devices with their start and end apart: 10, of which 3 were waited for; matrix products, arithmetic and copies ran while one was open for 0% of the time, Pallas kernels for 23%

profile of v3, /device:TPU:2, one launch (start us, length us, event | category | flops | bytes accessed | tf_op | source)
XLA Modules:
  0.0 51.7 jit_solution(4233819023405932255)
XLA Ops:
  0.0 0.0 copy-start.2
  0.0 0.0 copy-start.1
  0.0 0.0 copy-start.6
  0.0 0.0 copy-start.5
  0.0 0.0 copy-start.4
  0.0 0.0 copy-start.3
  0.0 0.0 copy-start
  0.0 0.0 copy-start.7
  0.1 0.0 copy-start.8
  0.1 1.3 %edges.1 = (bf16[1,32,8,256]{3,2,1,0:T(8,128)(2,1)S(1)}, bf16[1,32,8,256]{3,2,1,0:T(8,128)(2,1)S(1)}, bf16[32,1,8,256]{3,2,1,0:T(8,128)(2,1)S(1)}, bf16[32,1,8,256]{3,2,1,0:T(8,128)(2,1)S(1)}) custom-call(bf16[32,32,8,256]{3,2,1,0:T(8,128)(2,1)} %s_ref.1), custom_call_target="tpu_custom_call" | custom-call | tf_op jit(solution)/shard_map/edges/pallas_call | solution.py:45
  1.4 0.0 collective-permute-start
  1.4 1.7 %collective-permute-start.1 = (bf16[1,32,8,256]{3,2,1,0:T(8,128)(2,1)S(1)}, bf16[1,32,8,256]{3,2,1,0:T(8,128)(2,1)S(1)}, u32[]{:S(2)}, u32[]{:S(2)}) collective-permute-start(bf16[1,32,8,256]{3,2,1,0:T(8,128)(2,1)S(1)} %get-tuple-element.14), channel_id=1, source_target_pairs={{32,0},{64,32},{96,64},{128,96},{160,128},{192,160},{224,192},{0,2... | collective-permute-start | bytes 393224 | tf_op jit(solution)/shard_map/ppermute | solution.py:498
  3.1 1.9 %collective-permute-start.2 = (bf16[32,1,8,256]{3,2,1,0:T(8,128)(2,1)S(1)}, bf16[32,1,8,256]{3,2,1,0:T(8,128)(2,1)S(1)}, u32[]{:S(2)}, u32[]{:S(2)}) collective-permute-start(bf16[32,1,8,256]{3,2,1,0:T(8,128)(2,1)S(1)} %get-tuple-element.15), channel_id=1, source_target_pairs={{0,4},{4,8},{8,12},{12,16},{16,20},{20,24},{24,28},{28,0},{1,5},{5... | collective-permute-start | bytes 393224 | tf_op jit(solution)/shard_map/ppermute | solution.py:495
  5.0 3.9 %collective-permute-start.3 = (bf16[32,1,8,256]{3,2,1,0:T(8,128)(2,1)S(1)}, bf16[32,1,8,256]{3,2,1,0:T(8,128)(2,1)S(1)}, u32[]{:S(2)}, u32[]{:S(2)}) collective-permute-start(bf16[32,1,8,256]{3,2,1,0:T(8,128)(2,1)S(1)} %get-tuple-element.16), channel_id=1, source_target_pairs={{4,0},{8,4},{12,8},{16,12},{20,16},{24,20},{28,24},{0,28},{5,1},{9... | collective-permute-start | bytes 393224 | tf_op jit(solution)/shard_map/ppermute | solution.py:496
  9.0 5.1 %inner.1.adv_in = f32[2,8192,128]{2,1,0:T(8,128)S(1)} custom-call(bf16[32,32,8,256]{3,2,1,0:T(8,128)(2,1)} %s_ref.1, f32[32,8,32]{2,1,0:T(8,128)} %bitcast.8, f32[32,8,32]{2,1,0:T(8,128)} %bitcast.10), custom_call_target="tpu_custom_call" | custom-call | flops 10000000 | bytes 16777216 | tf_op jit(solution)/shard_map/inner/pallas_call | solution.py:422
  14.0 0.1 pad_add_fusion.place_ref
  14.1 0.0 collective-permute-done.west_ref
  14.1 0.0 collective-permute-done.1.east_ref
  14.1 0.0 collective-permute-done.2.south_ref
  14.1 0.0 collective-permute-done.3.north_ref
  14.1 0.0 copy-done.2
  14.1 0.0 copy-done.1
  14.2 0.0 copy-done.6
  14.2 0.0 copy-done.5
  14.2 0.0 copy-done.4
  14.2 0.0 copy-done.3
  14.2 0.0 copy-done
  14.2 0.0 copy-done.7
  14.2 0.0 copy-done.8
  14.2 8.2 %cloud.1 = (f32[2,8192,128]{2,1,0:T(8,128)S(1)}, bf16[528,256]{1,0:T(8,128)(2,1)S(1)}) custom-call(s32[2]{0:T(128)S(1)} %pad_add_fusion.place_ref, s32[16,64]{1,0:T(8,128)S(1)} %bitcast.12, s32[8,8,1,64]{3,2,1,0:T(1,128)S(1)} %copy-done.7, f32[2,8192,128]{2,1,0:T(8,128)S(1)} %inner.1.adv_in, ...), custom_call_target="tpu_custom_call", output_to_operand_aliasing={{0}: (3, {})} | custom-call | tf_op jit(solution)/shard_map/cloud/pallas_call | solution.py:442
  22.4 1.3 %collective-permute-start.8 = (bf16[528,256]{1,0:T(8,128)(2,1)S(1)}, bf16[528,256]{1,0:T(8,128)(2,1)S(1)}, u32[]{:S(2)}, u32[]{:S(2)}) collective-permute-start(bf16[528,256]{1,0:T(8,128)(2,1)S(1)} %get-tuple-element.20.own_ref), channel_id=1, source_target_pairs={{3,0},{7,4},{11,8},{15,12},{19,16},{23,20},{27,24},{31,28},{35,32}... | collective-permute-start | bytes 811016 | tf_op jit(solution)/shard_map/ppermute | solution.py:526
  23.7 0.7 %collective-permute-start.7 = (bf16[528,256]{1,0:T(8,128)(2,1)S(1)}, bf16[528,256]{1,0:T(8,128)(2,1)S(1)}, u32[]{:S(2)}, u32[]{:S(2)}) collective-permute-start(bf16[528,256]{1,0:T(8,128)(2,1)S(1)} %get-tuple-element.20.own_ref), channel_id=1, source_target_pairs={{3,2},{2,1},{7,6},{6,5},{11,10},{10,9},{15,14},{14,13},{19,18},{18... | collective-permute-start | bytes 811016 | tf_op jit(solution)/shard_map/ppermute | solution.py:525
  24.4 3.3 %settle.1 = (f32[2,8192,128]{2,1,0:T(8,128)}, bf16[528,256]{1,0:T(8,128)(2,1)S(1)}) custom-call(f32[2,8192,128]{2,1,0:T(8,128)S(1)} %get-tuple-element.17.adv, f32[8,256]{1,0:T(8,128)S(1)} %copy-done.6), custom_call_target="tpu_custom_call" | custom-call | tf_op jit(solution)/shard_map/settle/pallas_call | solution.py:464
  27.7 1.3 %collective-permute-start.5 = (bf16[528,256]{1,0:T(8,128)(2,1)S(1)}, bf16[528,256]{1,0:T(8,128)(2,1)S(1)}, u32[]{:S(2)}, u32[]{:S(2)}) collective-permute-start(bf16[528,256]{1,0:T(8,128)(2,1)S(1)} %get-tuple-element.18.own_ref), channel_id=1, source_target_pairs={{3,0},{7,4},{11,8},{15,12},{19,16},{23,20},{27,24},{31,28},{35,32}... | collective-permute-start | bytes 811016 | tf_op jit(solution)/shard_map/ppermute | solution.py:526
  29.0 0.7 %collective-permute-start.4 = (bf16[528,256]{1,0:T(8,128)(2,1)S(1)}, bf16[528,256]{1,0:T(8,128)(2,1)S(1)}, u32[]{:S(2)}, u32[]{:S(2)}) collective-permute-start(bf16[528,256]{1,0:T(8,128)(2,1)S(1)} %get-tuple-element.18.own_ref), channel_id=1, source_target_pairs={{3,2},{2,1},{7,6},{6,5},{11,10},{10,9},{15,14},{14,13},{19,18},{18... | collective-permute-start | bytes 811016 | tf_op jit(solution)/shard_map/ppermute | solution.py:525
  29.7 3.8 %collective-permute-done.8.b_ref.refs_3_ = bf16[528,256]{1,0:T(8,128)(2,1)S(1)} collective-permute-done((bf16[528,256]{1,0:T(8,128)(2,1)S(1)}, bf16[528,256]{1,0:T(8,128)(2,1)S(1)}, u32[]{:S(2)}, u32[]{:S(2)}) %collective-permute-start.8) | collective-permute-done | bytes 270368 | tf_op jit(solution)/shard_map/ppermute | solution.py:526
  33.5 0.0 collective-permute-done.7.a_ref.refs_2_
  33.5 3.1 %collective-permute-start.9 = (bf16[528,256]{1,0:T(8,128)(2,1)S(1)}, bf16[528,256]{1,0:T(8,128)(2,1)S(1)}, u32[]{:S(2)}, u32[]{:S(2)}) collective-permute-start(bf16[528,256]{1,0:T(8,128)(2,1)S(1)} %combine.3), channel_id=1, source_target_pairs={{1,0},{0,1},{5,4},{4,5},{9,8},{8,9},{13,12},{12,13},{17,16},{16,17... | collective-permute-start | bytes 811016 | tf_op jit(solution)/shard_map/ppermute | solution.py:534
  36.6 2.9 %collective-permute-done.5.b_ref = bf16[528,256]{1,0:T(8,128)(2,1)S(1)} collective-permute-done((bf16[528,256]{1,0:T(8,128)(2,1)S(1)}, bf16[528,256]{1,0:T(8,128)(2,1)S(1)}, u32[]{:S(2)}, u32[]{:S(2)}) %collective-permute-start.5) | collective-permute-done | bytes 270368 | tf_op jit(solution)/shard_map/ppermute | solution.py:526
  39.5 0.0 collective-permute-done.4.a_ref
  39.5 3.0 %collective-permute-start.6 = (bf16[528,256]{1,0:T(8,128)(2,1)S(1)}, bf16[528,256]{1,0:T(8,128)(2,1)S(1)}, u32[]{:S(2)}, u32[]{:S(2)}) collective-permute-start(bf16[528,256]{1,0:T(8,128)(2,1)S(1)} %combine.2), channel_id=1, source_target_pairs={{1,0},{0,1},{5,4},{4,5},{9,8},{8,9},{13,12},{12,13},{17,16},{16,17... | collective-permute-start | bytes 811016 | tf_op jit(solution)/shard_map/ppermute | solution.py:534
  42.5 0.0 collective-permute-done.9.refs_4_
  42.6 3.2 %finish.2.prev_ref = bf16[32,32,8,256]{3,2,1,0:T(8,128)(2,1)} custom-call(s32[1]{0:T(128)} %bitcast.zid_ref.refs_0_, f32[8,256]{1,0:T(8,128)S(1)} %copy-done.6, bf16[528,256]{1,0:T(8,128)(2,1)S(1)} %collective-permute-done.7.a_ref.refs_2_, bf16[528,256]{1,0:T(8,128)(2,1)S(1)} %collective-permute-done.8.b_ref.refs_3_, ...), custom_call_target="tpu_custom_call" | custom-call | tf_op jit(solution)/shard_map/finish/pallas_call | solution.py:403
  45.8 2.7 %collective-permute-done.6.d_ref = bf16[528,256]{1,0:T(8,128)(2,1)S(1)} collective-permute-done((bf16[528,256]{1,0:T(8,128)(2,1)S(1)}, bf16[528,256]{1,0:T(8,128)(2,1)S(1)}, u32[]{:S(2)}, u32[]{:S(2)}) %collective-permute-start.6) | collective-permute-done | bytes 270368 | tf_op jit(solution)/shard_map/ppermute | solution.py:534
  48.5 3.2 %finish.3 = bf16[32,32,8,256]{3,2,1,0:T(8,128)(2,1)} custom-call(s32[1]{0:T(128)} %bitcast.zid_ref.refs_0_, f32[8,256]{1,0:T(8,128)S(1)} %copy-done.6, bf16[528,256]{1,0:T(8,128)(2,1)S(1)} %collective-permute-done.4.a_ref, bf16[528,256]{1,0:T(8,128)(2,1)S(1)} %collective-permute-done.5.b_ref, ...), custom_call_target="tpu_custom_call", output_to_operand_aliasing={{}: (6, {})} | custom-call | tf_op jit(solution)/shard_map/finish/pallas_call | solution.py:403
  (2 shorter events, 0.0 us)
Async XLA Ops:
  0.0 14.1 %copy-start.2 = (f32[32,32,8]{1,2,0:T(8,128)S(1)}, f32[32,32,8]{1,2,0:T(8,128)}, u32[]{:S(2)}) copy-start(f32[32,32,8]{1,2,0:T(8,128)} %param.12) | copy-start | bytes 98308
  0.0 14.1 %copy-start.1 = (f32[32,32,8]{1,2,0:T(8,128)S(1)}, f32[32,32,8]{1,2,0:T(8,128)}, u32[]{:S(2)}) copy-start(f32[32,32,8]{1,2,0:T(8,128)} %param.11) | copy-start | bytes 98308
  0.0 14.2 %copy-start.6 = (f32[8,256]{1,0:T(8,128)S(1)}, f32[8,256]{1,0:T(8,128)}, u32[]{:S(2)}) copy-start(f32[8,256]{1,0:T(8,128)} %fall_ref.5) | copy-start | bytes 24580
  0.0 14.2 %copy-start.5 = (bf16[256,256]{1,0:T(8,128)(2,1)S(1)}, bf16[256,256]{1,0:T(8,128)(2,1)}, u32[]{:S(2)}) copy-start(bf16[256,256]{1,0:T(8,128)(2,1)} %fr_ref.1) | copy-start | bytes 393220
  0.0 14.2 %copy-start.4 = (bf16[256,256]{1,0:T(8,128)(2,1)S(1)}, bf16[256,256]{1,0:T(8,128)(2,1)}, u32[]{:S(2)}) copy-start(bf16[256,256]{1,0:T(8,128)(2,1)} %lk_ref.1) | copy-start | bytes 393220
  0.0 14.2 %copy-start.3 = (bf16[1024,256]{1,0:T(8,128)(2,1)S(1)}, bf16[1024,256]{1,0:T(8,128)(2,1)}, u32[]{:S(2)}) copy-start(bf16[1024,256]{1,0:T(8,128)(2,1)} %po_ref.1) | copy-start | bytes 1572868
  0.0 14.2 %copy-start = (bf16[256,2048]{1,0:T(8,128)(2,1)S(1)}, bf16[256,2048]{1,0:T(8,128)(2,1)}, u32[]{:S(2)}) copy-start(bf16[256,2048]{1,0:T(8,128)(2,1)} %pi_ref.1) | copy-start | bytes 3145732
  0.0 14.2 %copy-start.7 = (s32[8,8,1,64]{3,2,1,0:T(1,128)S(1)}, s32[8,8,1,64]{3,2,1,0:T(1,128)}, u32[]{:S(2)}) copy-start(s32[8,8,1,64]{3,2,1,0:T(1,128)} %target_any.1) | copy-start | bytes 49156
  0.1 14.2 %copy-start.8 = (s32[1,1,1,64,16]{3,4,2,1,0:T(8,128)S(1)}, s32[1,1,1,64,16]{3,4,2,1,0:T(8,128)}, u32[]{:S(2)}) copy-start(s32[1,1,1,64,16]{3,4,2,1,0:T(8,128)} %param.14) | copy-start | bytes 12292
  1.4 12.8 %collective-permute-start = (bf16[1,32,8,256]{3,2,1,0:T(8,128)(2,1)S(1)}, bf16[1,32,8,256]{3,2,1,0:T(8,128)(2,1)S(1)}, u32[]{:S(2)}, u32[]{:S(2)}) collective-permute-start(bf16[1,32,8,256]{3,2,1,0:T(8,128)(2,1)S(1)} %get-tuple-element.13), channel_id=1, source_target_pairs={{0,32},{32,64},{64,96},{96,128},{128,160},{160,192},{192,224},{224... | collective-permute-start | bytes 393224 | tf_op jit(solution)/shard_map/ppermute | solution.py:497
  1.4 12.7 %collective-permute-start.1 = (bf16[1,32,8,256]{3,2,1,0:T(8,128)(2,1)S(1)}, bf16[1,32,8,256]{3,2,1,0:T(8,128)(2,1)S(1)}, u32[]{:S(2)}, u32[]{:S(2)}) collective-permute-start(bf16[1,32,8,256]{3,2,1,0:T(8,128)(2,1)S(1)} %get-tuple-element.14), channel_id=1, source_target_pairs={{32,0},{64,32},{96,64},{128,96},{160,128},{192,160},{224,192},{0,2... | collective-permute-start | bytes 393224 | tf_op jit(solution)/shard_map/ppermute | solution.py:498
  3.1 11.0 %collective-permute-start.2 = (bf16[32,1,8,256]{3,2,1,0:T(8,128)(2,1)S(1)}, bf16[32,1,8,256]{3,2,1,0:T(8,128)(2,1)S(1)}, u32[]{:S(2)}, u32[]{:S(2)}) collective-permute-start(bf16[32,1,8,256]{3,2,1,0:T(8,128)(2,1)S(1)} %get-tuple-element.15), channel_id=1, source_target_pairs={{0,4},{4,8},{8,12},{12,16},{16,20},{20,24},{24,28},{28,0},{1,5},{5... | collective-permute-start | bytes 393224 | tf_op jit(solution)/shard_map/ppermute | solution.py:495
  5.0 9.1 %collective-permute-start.3 = (bf16[32,1,8,256]{3,2,1,0:T(8,128)(2,1)S(1)}, bf16[32,1,8,256]{3,2,1,0:T(8,128)(2,1)S(1)}, u32[]{:S(2)}, u32[]{:S(2)}) collective-permute-start(bf16[32,1,8,256]{3,2,1,0:T(8,128)(2,1)S(1)} %get-tuple-element.16), channel_id=1, source_target_pairs={{4,0},{8,4},{12,8},{16,12},{20,16},{24,20},{28,24},{0,28},{5,1},{9... | collective-permute-start | bytes 393224 | tf_op jit(solution)/shard_map/ppermute | solution.py:496
  22.4 11.1 %collective-permute-start.8 = (bf16[528,256]{1,0:T(8,128)(2,1)S(1)}, bf16[528,256]{1,0:T(8,128)(2,1)S(1)}, u32[]{:S(2)}, u32[]{:S(2)}) collective-permute-start(bf16[528,256]{1,0:T(8,128)(2,1)S(1)} %get-tuple-element.20.own_ref), channel_id=1, source_target_pairs={{3,0},{7,4},{11,8},{15,12},{19,16},{23,20},{27,24},{31,28},{35,32}... | collective-permute-start | bytes 811016 | tf_op jit(solution)/shard_map/ppermute | solution.py:526
  23.7 9.8 %collective-permute-start.7 = (bf16[528,256]{1,0:T(8,128)(2,1)S(1)}, bf16[528,256]{1,0:T(8,128)(2,1)S(1)}, u32[]{:S(2)}, u32[]{:S(2)}) collective-permute-start(bf16[528,256]{1,0:T(8,128)(2,1)S(1)} %get-tuple-element.20.own_ref), channel_id=1, source_target_pairs={{3,2},{2,1},{7,6},{6,5},{11,10},{10,9},{15,14},{14,13},{19,18},{18... | collective-permute-start | bytes 811016 | tf_op jit(solution)/shard_map/ppermute | solution.py:525
  27.7 11.7 %collective-permute-start.5 = (bf16[528,256]{1,0:T(8,128)(2,1)S(1)}, bf16[528,256]{1,0:T(8,128)(2,1)S(1)}, u32[]{:S(2)}, u32[]{:S(2)}) collective-permute-start(bf16[528,256]{1,0:T(8,128)(2,1)S(1)} %get-tuple-element.18.own_ref), channel_id=1, source_target_pairs={{3,0},{7,4},{11,8},{15,12},{19,16},{23,20},{27,24},{31,28},{35,32}... | collective-permute-start | bytes 811016 | tf_op jit(solution)/shard_map/ppermute | solution.py:526
  29.0 10.4 %collective-permute-start.4 = (bf16[528,256]{1,0:T(8,128)(2,1)S(1)}, bf16[528,256]{1,0:T(8,128)(2,1)S(1)}, u32[]{:S(2)}, u32[]{:S(2)}) collective-permute-start(bf16[528,256]{1,0:T(8,128)(2,1)S(1)} %get-tuple-element.18.own_ref), channel_id=1, source_target_pairs={{3,2},{2,1},{7,6},{6,5},{11,10},{10,9},{15,14},{14,13},{19,18},{18... | collective-permute-start | bytes 811016 | tf_op jit(solution)/shard_map/ppermute | solution.py:525
  33.5 9.0 %collective-permute-start.9 = (bf16[528,256]{1,0:T(8,128)(2,1)S(1)}, bf16[528,256]{1,0:T(8,128)(2,1)S(1)}, u32[]{:S(2)}, u32[]{:S(2)}) collective-permute-start(bf16[528,256]{1,0:T(8,128)(2,1)S(1)} %combine.3), channel_id=1, source_target_pairs={{1,0},{0,1},{5,4},{4,5},{9,8},{8,9},{13,12},{12,13},{17,16},{16,17... | collective-permute-start | bytes 811016 | tf_op jit(solution)/shard_map/ppermute | solution.py:534
  39.5 9.0 %collective-permute-start.6 = (bf16[528,256]{1,0:T(8,128)(2,1)S(1)}, bf16[528,256]{1,0:T(8,128)(2,1)S(1)}, u32[]{:S(2)}, u32[]{:S(2)}) collective-permute-start(bf16[528,256]{1,0:T(8,128)(2,1)S(1)} %combine.2), channel_id=1, source_target_pairs={{1,0},{0,1},{5,4},{4,5},{9,8},{8,9},{13,12},{12,13},{17,16},{16,17... | collective-permute-start | bytes 811016 | tf_op jit(solution)/shard_map/ppermute | solution.py:534

commit v4 on v3

--- a/solution.py
+++ b/solution.py
@@ -145,7 +145,8 @@
     gain = jnp.ones((1, nb), F32)
     for z in reversed(range(nz)):
         gain = gain * through[z : z + 1, :]
-    flux_ref[pl.ds(count, GAIN_ROWS), :] = jnp.broadcast_to(gain, (GAIN_ROWS, nb)).astype(BF16)
+    rest = flux_ref.shape[0] - count
+    flux_ref[pl.ds(count, rest), :] = jnp.broadcast_to(gain, (rest, nb)).astype(BF16)
 
 
 def cloud_kernel(
@@ -260,13 +261,13 @@
         return carry
 
     lax.fori_loop(0, blocks, scatter, 0, unroll=4)
-    count = flux_ref.shape[0] - GAIN_ROWS
+    count = flux_ref.shape[0] - 4 * GAIN_ROWS
     settle_columns(adv, flux_ref, fall_ref[...], 0, count)
 
 
 def settle_kernel(adv, fall_ref, local_any, flux_ref, sems):
     nz = fall_ref.shape[0]
-    count = flux_ref.shape[0] - GAIN_ROWS
+    count = flux_ref.shape[0] - 2 * GAIN_ROWS
     first = adv.shape[1] // nz - count
     cut = first * nz
     front = pltpu.make_async_copy(adv.at[:, :cut], local_any.at[:, :cut], sems.at[0])
@@ -278,13 +279,12 @@
     back.wait()
 
 
-def combine_kernel(zid_ref, own_ref, a_ref, b_ref, out_ref):
-    n = own_ref.shape[0] - GAIN_ROWS
+def combine_kernel(zid_ref, own_ref, a_ref, b_ref, out_ref, *, n):
     z = zid_ref[0]
 
     @pl.when(z == 0)
     def _():
-        out_ref[...] = b_ref[...]
+        out_ref[...] = b_ref[0 : own_ref.shape[0], :]
 
     @pl.when(z != 0)
     def _():
@@ -298,14 +298,14 @@
             return carry
 
         lax.fori_loop(0, n // 16, some, 0, unroll=4)
-        out_ref[n : n + GAIN_ROWS, :] = (
-            gain * a_ref[n : n + GAIN_ROWS, :].astype(F32)
-        ).astype(BF16)
-
-
-def combine(zid, own, a, b):
-    return pl.pallas_call(
-        combine_kernel,
+        for row in range(n, own_ref.shape[0], GAIN_ROWS):
+            at = slice(row, row + GAIN_ROWS)
+            out_ref[at, :] = (gain * a_ref[at, :].astype(F32)).astype(BF16)
+
+
+def combine(zid, own, a, b, n):
+    return pl.pallas_call(
+        functools.partial(combine_kernel, n=n),
         out_shape=pltpu.VMEM(own.shape, BF16),
         in_specs=[SMEM] + [VMEM] * 3,
         out_specs=VMEM,
@@ -314,39 +314,13 @@
     )(zid, own, a, b)
 
 
-def finish_kernel(
-    zid_ref,
-    fall_ref,
-    a_ref,
-    b_ref,
-    d_ref,
-    local_any,
-    prev_ref,
-    out_any,
-    local,
-    inflow,
-    stage,
-    sems,
-    *,
-    first,
+def finish_columns(
+    zid_ref, fall_ref, a_ref, b_ref, d_ref, out_any, local, inflow, stage, sems, first, loads, later
 ):
-    del prev_ref
     ny, nz, nb = out_any.shape[1:]
     parts, per = stage.shape[:2]
     tiles = nb // LANES
-    n = a_ref.shape[0] - GAIN_ROWS
-    span = per * ny * nz
-    loads = []
-    for p in range(parts):
-        start = first * ny * nz + p * span
-        loads.append(
-            pltpu.make_async_copy(
-                local_any.at[:, start : start + span],
-                local.at[:, p * span : (p + 1) * span],
-                sems.at[p],
-            )
-        )
-        loads[-1].start()
+    n = inflow.shape[0]
     fall = fall_ref[...]
     inverse = 1.0 / (1.0 + fall)
     through = fall * inverse
@@ -378,7 +352,10 @@
                 stage[p, x, y] = (own + m * gain).astype(BF16)
             return carry
 
-        loads[p].wait()
+        if loads:
+            loads[p].wait()
+        if later is not None and p == 1:
+            later.start()
         lax.fori_loop(0, per, column, 0)
         copy = pltpu.make_async_copy(
             stage.at[p], out_any.at[first + p * per : first + (p + 1) * per], sems.at[p]
@@ -387,34 +364,77 @@
         copies.append(copy)
     for copy in copies:
         copy.wait()
-
-
-def finish(zid, fall, a, b, d, local, prev, shape, first, parts):
-    nx, ny, nz, nb = shape
-    n = a.shape[0] - GAIN_ROWS
-    given = (zid, fall, a, b, d, in_hbm(local)) + (() if prev is None else (prev,))
-    kernel = functools.partial(finish_kernel, first=first)
-    if prev is None:
-        inner = kernel
-
-        def kernel(*refs):
-            return inner(*refs[:6], None, *refs[6:])
-
-    return pl.pallas_call(
-        kernel,
-        out_shape=jax.ShapeDtypeStruct(shape, BF16),
-        in_specs=[SMEM] + [VMEM] * 4 + [HBM] + [ANY] * (prev is not None),
+    if later is not None:
+        later.wait()
+
+
+def finish_front_kernel(
+    zid_ref, fall_ref, a_ref, b_ref, d_ref, local_any, out_any, back, front, inflow, stage, sems
+):
+    parts = stage.shape[0]
+    cut = front.shape[1]
+    span = cut // parts
+    loads = [
+        pltpu.make_async_copy(
+            local_any.at[:, p * span : (p + 1) * span],
+            front.at[:, p * span : (p + 1) * span],
+            sems.at[p],
+        )
+        for p in range(parts)
+    ]
+    for copy in loads:
+        copy.start()
+    later = pltpu.make_async_copy(local_any.at[:, cut:], back, sems.at[parts])
+    given = (zid_ref, fall_ref, a_ref, b_ref, d_ref, out_any, front, inflow, stage, sems)
+    finish_columns(*given, 0, loads, later)
+
+
+def finish_back_kernel(
+    zid_ref, fall_ref, a_ref, b_ref, d_ref, back, prev_ref, out_any, inflow, stage, sems
+):
+    del prev_ref
+    first = out_any.shape[0] - stage.shape[0] * stage.shape[1]
+    given = (zid_ref, fall_ref, a_ref, b_ref, d_ref, out_any, back, inflow, stage, sems)
+    finish_columns(*given, first, [], None)
+
+
+def finish_scratch(n, parts, shape):
+    ny, nz, nb = shape[1:]
+    return [
+        pltpu.VMEM((n, nb), F32),
+        pltpu.VMEM((parts, n // ny // parts, ny, nz, nb), BF16),
+        pltpu.SemaphoreType.DMA((parts + 1,)),
+    ]
+
+
+def finish_front(zid, fall, a, b, d, local, shape, n, parts):
+    nz, nb = shape[2:]
+    tiles, cells, lanes = local.shape
+    return pl.pallas_call(
+        finish_front_kernel,
+        out_shape=(
+            jax.ShapeDtypeStruct(shape, BF16),
+            pltpu.VMEM((tiles, cells - n * nz, lanes), F32),
+        ),
+        in_specs=[SMEM] + [VMEM] * 4 + [HBM],
+        out_specs=(ANY, VMEM),
+        scratch_shapes=[pltpu.VMEM((tiles, n * nz, lanes), F32), *finish_scratch(n, parts, shape)],
+        compiler_params=pltpu.CompilerParams(vmem_limit_bytes=16 * MIB),
+        name="finish_front",
+    )(zid, fall, a, b, d, in_hbm(local))
+
+
+def finish_back(zid, fall, a, b, d, back, prev, n, parts):
+    return pl.pallas_call(
+        finish_back_kernel,
+        out_shape=jax.ShapeDtypeStruct(prev.shape, BF16),
+        in_specs=[SMEM] + [VMEM] * 5 + [ANY],
         out_specs=ANY,
-        scratch_shapes=[
-            pltpu.VMEM((nb // LANES, n * nz, LANES), F32),
-            pltpu.VMEM((n, nb), F32),
-            pltpu.VMEM((parts, n // ny // parts, ny, nz, nb), BF16),
-            pltpu.SemaphoreType.DMA((parts,)),
-        ],
-        input_output_aliases={} if prev is None else {6: 0},
+        scratch_shapes=finish_scratch(n, parts, prev.shape),
+        input_output_aliases={6: 0},
         compiler_params=pltpu.CompilerParams(vmem_limit_bytes=16 * MIB),
-        name="finish",
-    )(*given)
+        name="finish_back",
+    )(zid, fall, a, b, d, in_vmem(back), prev)
 
 
 def inner(spectrum, we, wn):
@@ -443,7 +463,7 @@
         cloud_kernel,
         out_shape=(
             pltpu.VMEM(adv.shape, F32),
-            pltpu.VMEM((count + GAIN_ROWS, nb), BF16),
+            pltpu.VMEM((count + 4 * GAIN_ROWS, nb), BF16),
         ),
         in_specs=[SMEM, ANY, ANY] + [VMEM] * 12,
         out_specs=(VMEM, VMEM),
@@ -465,7 +485,7 @@
         settle_kernel,
         out_shape=(
             pltpu.HBM(adv.shape, F32),
-            pltpu.VMEM((count + GAIN_ROWS, nb), BF16),
+            pltpu.VMEM((count + 2 * GAIN_ROWS, nb), BF16),
         ),
         in_specs=[VMEM, VMEM],
         out_specs=(HBM, VMEM),
@@ -522,20 +542,21 @@
     )
 
     def begin(flux):
-        a = lax.ppermute(flux, "gz", [(3, 2), (2, 1)])
+        own = flux[:-GAIN_ROWS]
+        a = lax.ppermute(own, "gz", [(3, 2), (2, 1)])
         b = lax.ppermute(flux, "gz", [(3, 0)])
-        return flux, a, b
+        return own, a, b
 
     front = begin(flux)
     local, flux = settle(adv, fall_rate, columns - first)
     back = begin(flux)
     ready = []
-    for flux, a, b in (front, back):
-        ready.append((a, b, lax.ppermute(combine(zid, flux, a, b), "gz", [(1, 0), (0, 1)])))
+    for n, (flux, a, b) in ((first, front), (columns - first, back)):
+        ready.append((a, b, lax.ppermute(combine(zid, flux, a, b, n), "gz", [(1, 0), (0, 1)])))
     front, back = ready
     shape = spectrum.shape
-    out = finish(zid, fall_rate, *front, local, None, shape, 0, 4)
-    out = finish(zid, fall_rate, *back, local, out, shape, first // ny, 4)
+    out, rest = finish_front(zid, fall_rate, *front, local, shape, first, 4)
+    out = finish_back(zid, fall_rate, *back, rest, out, columns - first, 4)
     return out
 
 

time: 51.9 us -> 51.4 us (level)
  starting transfers between devices: 17.6 us -> 17 us
    ppermute x4, waiting for transfers between devices: 2.68 us -> 1.92 us  [the longest x2 1.92 us: body(): lax.ppermute(combine(zid, flux, a, b, n), 'gz', [(1, 0), (0, 1)])]
    ppermute x2, waiting for transfers between devices: 6.63 us -> 7.38 us  [begin(): b = lax.ppermute(flux, 'gz', [(3, 0)])]
    ppermute x4, starting transfers between devices: 7.44 us -> 6.85 us  [the longest x2 5.5 us: body(): lax.ppermute(combine(zid, flux, a, b, n), 'gz', [(1, 0), (0, 1)])]
  transfers between devices with their start and end apart: 10 -> 10, of which waited for: 3 -> 4; matrix products, arithmetic and copies ran while one was open for 0% -> 0% of each run, Pallas kernels for 23% -> 26%
where the time goes in v4:
time: 51.4 us; the launch traced here: 51.2 us
  Pallas kernels  24.4 us (47%)
  starting transfers between devices  17 us (33%)
  waiting for transfers between devices  9.31 us (18%)
    pallas_call x1, Pallas kernels, cloud(): pl.pallas_call(cloud_kernel, out_shape=(pltpu.VMEM(adv.shape, F32), pltpu...  8.19 us
    ppermute x2, waiting for transfers between devices, begin(): b = lax.ppermute(flux, 'gz', [(3, 0)])  7.38 us
    ppermute x2, starting transfers between devices, body(): lax.ppermute(combine(zid, flux, a, b, n), 'gz', [(1, 0), (0, 1)])  5.5 us
    pallas_call x1, Pallas kernels, inner(): pl.pallas_call(inner_kernel, out_shape=pltpu.VMEM((nb // LANES, nx * ny *...  5.17 us
    pallas_call x1, Pallas kernels, finish_front(): pl.pallas_call(finish_front_kernel, out_shape=(jax.ShapeDtypeStruct(shape...  4.6 us
    ppermute x1, starting transfers between devices, body(): north = lax.ppermute(low_y, 'gy', [(b, a) for a, b in up_y])  3.94 us
    pallas_call x1, Pallas kernels, settle(): pl.pallas_call(settle_kernel, out_shape=(pltpu.HBM(adv.shape, F32), pltpu...  3.34 us
    ppermute x2, starting transfers between devices, begin(): b = lax.ppermute(flux, 'gz', [(3, 0)])  2.58 us
  transfers between devices with their start and end apart: 10, of which 4 were waited for; matrix products, arithmetic and copies ran while one was open for 0% of the time, Pallas kernels for 26%

profile of v4, /device:TPU:2, one launch (start us, length us, event | category | flops | bytes accessed | tf_op | source)
XLA Modules:
  0.0 51.2 jit_solution(17714980838558815394)
XLA Ops:
  0.0 1.1 %edges.1 = (bf16[1,32,8,256]{3,2,1,0:T(8,128)(2,1)S(1)}, bf16[1,32,8,256]{3,2,1,0:T(8,128)(2,1)S(1)}, bf16[32,1,8,256]{3,2,1,0:T(8,128)(2,1)S(1)}, bf16[32,1,8,256]{3,2,1,0:T(8,128)(2,1)S(1)}) custom-call(bf16[32,32,8,256]{3,2,1,0:T(8,128)(2,1)} %s_ref.1), custom_call_target="tpu_custom_call" | custom-call | tf_op jit(solution)/shard_map/edges/pallas_call | solution.py:45
  1.1 0.0 collective-permute-start
  1.2 1.7 %collective-permute-start.1 = (bf16[1,32,8,256]{3,2,1,0:T(8,128)(2,1)S(1)}, bf16[1,32,8,256]{3,2,1,0:T(8,128)(2,1)S(1)}, u32[]{:S(2)}, u32[]{:S(2)}) collective-permute-start(bf16[1,32,8,256]{3,2,1,0:T(8,128)(2,1)S(1)} %get-tuple-element.16), channel_id=1, source_target_pairs={{32,0},{64,32},{96,64},{128,96},{160,128},{192,160},{224,192},{0,2... | collective-permute-start | bytes 393224 | tf_op jit(solution)/shard_map/ppermute | solution.py:518
  2.9 1.9 %collective-permute-start.2 = (bf16[32,1,8,256]{3,2,1,0:T(8,128)(2,1)S(1)}, bf16[32,1,8,256]{3,2,1,0:T(8,128)(2,1)S(1)}, u32[]{:S(2)}, u32[]{:S(2)}) collective-permute-start(bf16[32,1,8,256]{3,2,1,0:T(8,128)(2,1)S(1)} %get-tuple-element.17), channel_id=1, source_target_pairs={{0,4},{4,8},{8,12},{12,16},{16,20},{20,24},{24,28},{28,0},{1,5},{5... | collective-permute-start | bytes 393224 | tf_op jit(solution)/shard_map/ppermute | solution.py:515
  4.8 3.9 %collective-permute-start.3 = (bf16[32,1,8,256]{3,2,1,0:T(8,128)(2,1)S(1)}, bf16[32,1,8,256]{3,2,1,0:T(8,128)(2,1)S(1)}, u32[]{:S(2)}, u32[]{:S(2)}) collective-permute-start(bf16[32,1,8,256]{3,2,1,0:T(8,128)(2,1)S(1)} %get-tuple-element.18), channel_id=1, source_target_pairs={{4,0},{8,4},{12,8},{16,12},{20,16},{24,20},{28,24},{0,28},{5,1},{9... | collective-permute-start | bytes 393224 | tf_op jit(solution)/shard_map/ppermute | solution.py:516
  8.8 0.0 copy-start
  8.8 0.0 copy-start.1
  8.8 0.0 copy-start.2
  8.8 0.0 copy-start.3
  8.8 0.0 copy-start.4
  8.8 0.0 copy-start.5
  8.8 0.0 copy-start.6
  8.8 0.0 copy-start.7
  8.8 0.0 copy-start.8
  8.8 5.2 %inner.1.adv_in = f32[2,8192,128]{2,1,0:T(8,128)S(1)} custom-call(bf16[32,32,8,256]{3,2,1,0:T(8,128)(2,1)} %s_ref.1, f32[32,8,32]{2,1,0:T(8,128)} %bitcast.8, f32[32,8,32]{2,1,0:T(8,128)} %bitcast.10), custom_call_target="tpu_custom_call" | custom-call | flops 10000000 | bytes 16777216 | tf_op jit(solution)/shard_map/inner/pallas_call | solution.py:442
  14.0 0.1 pad_add_fusion.place_ref
  14.1 0.0 collective-permute-done.west_ref
  14.1 0.0 collective-permute-done.1.east_ref
  14.1 0.0 collective-permute-done.2.south_ref
  14.1 0.0 collective-permute-done.3.north_ref
  14.1 0.0 copy-done
  14.1 0.0 copy-done.1
  14.1 0.0 copy-done.2
  14.1 0.0 copy-done.3
  14.1 0.0 copy-done.4
  14.2 0.0 copy-done.5
  14.2 0.0 copy-done.6
  14.2 0.0 copy-done.7
  14.2 0.0 copy-done.8
  14.2 8.2 %cloud.1 = (f32[2,8192,128]{2,1,0:T(8,128)S(1)}, bf16[576,256]{1,0:T(8,128)(2,1)S(1)}) custom-call(s32[2]{0:T(128)S(1)} %pad_add_fusion.place_ref, s32[16,64]{1,0:T(8,128)S(1)} %bitcast.12, s32[8,8,1,64]{3,2,1,0:T(1,128)S(1)} %copy-done.7, f32[2,8192,128]{2,1,0:T(8,128)S(1)} %inner.1.adv_in, ...), custom_call_target="tpu_custom_call", output_to_operand_aliasing={{0}: (3, {})} | custom-call | tf_op jit(solution)/shard_map/cloud/pallas_call | solution.py:462
  22.4 1.3 %collective-permute-start.8 = (bf16[576,256]{1,0:T(8,128)(2,1)S(1)}, bf16[576,256]{1,0:T(8,128)(2,1)S(1)}, u32[]{:S(2)}, u32[]{:S(2)}) collective-permute-start(bf16[576,256]{1,0:T(8,128)(2,1)S(1)} %get-tuple-element.21), channel_id=1, source_target_pairs={{3,0},{7,4},{11,8},{15,12},{19,16},{23,20},{27,24},{31,28},{35,32}... | collective-permute-start | bytes 884744 | tf_op jit(solution)/shard_map/ppermute | solution.py:547
  23.7 0.7 %collective-permute-start.7 = (bf16[560,256]{1,0:T(8,128)(2,1)S(1)}, bf16[560,256]{1,0:T(8,128)(2,1)S(1)}, u32[]{:S(2)}, u32[]{:S(2)}) collective-permute-start(bf16[560,256]{1,0:T(8,128)(2,1)S(1)} %slice.7.own_ref), channel_id=1, source_target_pairs={{3,2},{2,1},{7,6},{6,5},{11,10},{10,9},{15,14},{14,13},{19,18},{18... | collective-permute-start | bytes 860168 | tf_op jit(solution)/shard_map/ppermute | solution.py:546
  24.4 3.3 %settle.1 = (f32[2,8192,128]{2,1,0:T(8,128)}, bf16[544,256]{1,0:T(8,128)(2,1)S(1)}) custom-call(f32[2,8192,128]{2,1,0:T(8,128)S(1)} %get-tuple-element.19.adv, f32[8,256]{1,0:T(8,128)S(1)} %copy-done.6), custom_call_target="tpu_custom_call" | custom-call | tf_op jit(solution)/shard_map/settle/pallas_call | solution.py:484
  27.8 1.3 %collective-permute-start.5 = (bf16[544,256]{1,0:T(8,128)(2,1)S(1)}, bf16[544,256]{1,0:T(8,128)(2,1)S(1)}, u32[]{:S(2)}, u32[]{:S(2)}) collective-permute-start(bf16[544,256]{1,0:T(8,128)(2,1)S(1)} %get-tuple-element.20), channel_id=1, source_target_pairs={{3,0},{7,4},{11,8},{15,12},{19,16},{23,20},{27,24},{31,28},{35,32}... | collective-permute-start | bytes 835592 | tf_op jit(solution)/shard_map/ppermute | solution.py:547
  29.1 0.7 %collective-permute-start.4 = (bf16[528,256]{1,0:T(8,128)(2,1)S(1)}, bf16[528,256]{1,0:T(8,128)(2,1)S(1)}, u32[]{:S(2)}, u32[]{:S(2)}) collective-permute-start(bf16[528,256]{1,0:T(8,128)(2,1)S(1)} %slice.6.own_ref), channel_id=1, source_target_pairs={{3,2},{2,1},{7,6},{6,5},{11,10},{10,9},{15,14},{14,13},{19,18},{18... | collective-permute-start | bytes 811016 | tf_op jit(solution)/shard_map/ppermute | solution.py:546
  29.8 0.0 collective-permute-done.7.a_ref
  29.8 4.5 %collective-permute-done.8.b_ref = bf16[576,256]{1,0:T(8,128)(2,1)S(1)} collective-permute-done((bf16[576,256]{1,0:T(8,128)(2,1)S(1)}, bf16[576,256]{1,0:T(8,128)(2,1)S(1)}, u32[]{:S(2)}, u32[]{:S(2)}) %collective-permute-start.8) | collective-permute-done | bytes 294944 | tf_op jit(solution)/shard_map/ppermute | solution.py:547
  34.3 2.8 %collective-permute-start.9 = (bf16[560,256]{1,0:T(8,128)(2,1)S(1)}, bf16[560,256]{1,0:T(8,128)(2,1)S(1)}, u32[]{:S(2)}, u32[]{:S(2)}) collective-permute-start(bf16[560,256]{1,0:T(8,128)(2,1)S(1)} %combine.3), channel_id=1, source_target_pairs={{1,0},{0,1},{5,4},{4,5},{9,8},{8,9},{13,12},{12,13},{17,16},{16,17... | collective-permute-start | bytes 860168 | tf_op jit(solution)/shard_map/ppermute | solution.py:555
  37.0 0.0 collective-permute-done.4.a_ref
  37.0 2.9 %collective-permute-done.5.b_ref = bf16[544,256]{1,0:T(8,128)(2,1)S(1)} collective-permute-done((bf16[544,256]{1,0:T(8,128)(2,1)S(1)}, bf16[544,256]{1,0:T(8,128)(2,1)S(1)}, u32[]{:S(2)}, u32[]{:S(2)}) %collective-permute-start.5) | collective-permute-done | bytes 278560 | tf_op jit(solution)/shard_map/ppermute | solution.py:547
  40.0 2.7 %collective-permute-start.6 = (bf16[528,256]{1,0:T(8,128)(2,1)S(1)}, bf16[528,256]{1,0:T(8,128)(2,1)S(1)}, u32[]{:S(2)}, u32[]{:S(2)}) collective-permute-start(bf16[528,256]{1,0:T(8,128)(2,1)S(1)} %combine.2), channel_id=1, source_target_pairs={{1,0},{0,1},{5,4},{4,5},{9,8},{8,9},{13,12},{12,13},{17,16},{16,17... | collective-permute-start | bytes 811016 | tf_op jit(solution)/shard_map/ppermute | solution.py:555
  42.7 0.6 %collective-permute-done.9.d_ref = bf16[560,256]{1,0:T(8,128)(2,1)S(1)} collective-permute-done((bf16[560,256]{1,0:T(8,128)(2,1)S(1)}, bf16[560,256]{1,0:T(8,128)(2,1)S(1)}, u32[]{:S(2)}, u32[]{:S(2)}) %collective-permute-start.9) | collective-permute-done | bytes 286752 | tf_op jit(solution)/shard_map/ppermute | solution.py:555
  43.3 4.6 %finish_front.1 = (bf16[32,32,8,256]{3,2,1,0:T(8,128)(2,1)}, f32[2,4096,128]{2,1,0:T(8,128)S(1)}) custom-call(s32[1]{0:T(128)} %bitcast.zid_ref, f32[8,256]{1,0:T(8,128)S(1)} %copy-done.6, bf16[560,256]{1,0:T(8,128)(2,1)S(1)} %collective-permute-done.7.a_ref, bf16[576,256]{1,0:T(8,128)(2,1)S(1)} %collective-permute-done.8.b_ref, ...), custom_call_target="tpu_custom_call" | custom-call | tf_op jit(solution)/shard_map/finish_front/pallas_call | solution.py:413
  47.9 1.3 %collective-permute-done.6.d_ref = bf16[528,256]{1,0:T(8,128)(2,1)S(1)} collective-permute-done((bf16[528,256]{1,0:T(8,128)(2,1)S(1)}, bf16[528,256]{1,0:T(8,128)(2,1)S(1)}, u32[]{:S(2)}, u32[]{:S(2)}) %collective-permute-start.6) | collective-permute-done | bytes 270368 | tf_op jit(solution)/shard_map/ppermute | solution.py:555
  49.3 1.9 %finish_back.1 = bf16[32,32,8,256]{3,2,1,0:T(8,128)(2,1)} custom-call(s32[1]{0:T(128)} %bitcast.zid_ref, f32[8,256]{1,0:T(8,128)S(1)} %copy-done.6, bf16[528,256]{1,0:T(8,128)(2,1)S(1)} %collective-permute-done.4.a_ref, bf16[544,256]{1,0:T(8,128)(2,1)S(1)} %collective-permute-done.5.b_ref, ...), custom_call_target="tpu_custom_call", output_to_operand_aliasing={{}: (6, {})} | custom-call | tf_op jit(solution)/shard_map/finish_back/pallas_call | solution.py:428
  (4 shorter events, 0.1 us)
Async XLA Ops:
  1.1 13.0 %collective-permute-start = (bf16[1,32,8,256]{3,2,1,0:T(8,128)(2,1)S(1)}, bf16[1,32,8,256]{3,2,1,0:T(8,128)(2,1)S(1)}, u32[]{:S(2)}, u32[]{:S(2)}) collective-permute-start(bf16[1,32,8,256]{3,2,1,0:T(8,128)(2,1)S(1)} %get-tuple-element.15), channel_id=1, source_target_pairs={{0,32},{32,64},{64,96},{96,128},{128,160},{160,192},{192,224},{224... | collective-permute-start | bytes 393224 | tf_op jit(solution)/shard_map/ppermute | solution.py:517
  1.2 12.9 %collective-permute-start.1 = (bf16[1,32,8,256]{3,2,1,0:T(8,128)(2,1)S(1)}, bf16[1,32,8,256]{3,2,1,0:T(8,128)(2,1)S(1)}, u32[]{:S(2)}, u32[]{:S(2)}) collective-permute-start(bf16[1,32,8,256]{3,2,1,0:T(8,128)(2,1)S(1)} %get-tuple-element.16), channel_id=1, source_target_pairs={{32,0},{64,32},{96,64},{128,96},{160,128},{192,160},{224,192},{0,2... | collective-permute-start | bytes 393224 | tf_op jit(solution)/shard_map/ppermute | solution.py:518
  2.9 11.2 %collective-permute-start.2 = (bf16[32,1,8,256]{3,2,1,0:T(8,128)(2,1)S(1)}, bf16[32,1,8,256]{3,2,1,0:T(8,128)(2,1)S(1)}, u32[]{:S(2)}, u32[]{:S(2)}) collective-permute-start(bf16[32,1,8,256]{3,2,1,0:T(8,128)(2,1)S(1)} %get-tuple-element.17), channel_id=1, source_target_pairs={{0,4},{4,8},{8,12},{12,16},{16,20},{20,24},{24,28},{28,0},{1,5},{5... | collective-permute-start | bytes 393224 | tf_op jit(solution)/shard_map/ppermute | solution.py:515
  4.8 9.3 %collective-permute-start.3 = (bf16[32,1,8,256]{3,2,1,0:T(8,128)(2,1)S(1)}, bf16[32,1,8,256]{3,2,1,0:T(8,128)(2,1)S(1)}, u32[]{:S(2)}, u32[]{:S(2)}) collective-permute-start(bf16[32,1,8,256]{3,2,1,0:T(8,128)(2,1)S(1)} %get-tuple-element.18), channel_id=1, source_target_pairs={{4,0},{8,4},{12,8},{16,12},{20,16},{24,20},{28,24},{0,28},{5,1},{9... | collective-permute-start | bytes 393224 | tf_op jit(solution)/shard_map/ppermute | solution.py:516
  8.8 5.4 %copy-start = (bf16[256,2048]{1,0:T(8,128)(2,1)S(1)}, bf16[256,2048]{1,0:T(8,128)(2,1)}, u32[]{:S(2)}) copy-start(bf16[256,2048]{1,0:T(8,128)(2,1)} %pi_ref.1) | copy-start | bytes 3145732
  8.8 5.4 %copy-start.1 = (f32[32,32,8]{1,2,0:T(8,128)S(1)}, f32[32,32,8]{1,2,0:T(8,128)}, u32[]{:S(2)}) copy-start(f32[32,32,8]{1,2,0:T(8,128)} %param.11) | copy-start | bytes 98308
  8.8 5.4 %copy-start.2 = (f32[32,32,8]{1,2,0:T(8,128)S(1)}, f32[32,32,8]{1,2,0:T(8,128)}, u32[]{:S(2)}) copy-start(f32[32,32,8]{1,2,0:T(8,128)} %param.12) | copy-start | bytes 98308
  8.8 5.4 %copy-start.3 = (bf16[1024,256]{1,0:T(8,128)(2,1)S(1)}, bf16[1024,256]{1,0:T(8,128)(2,1)}, u32[]{:S(2)}) copy-start(bf16[1024,256]{1,0:T(8,128)(2,1)} %po_ref.1) | copy-start | bytes 1572868
  8.8 5.4 %copy-start.4 = (bf16[256,256]{1,0:T(8,128)(2,1)S(1)}, bf16[256,256]{1,0:T(8,128)(2,1)}, u32[]{:S(2)}) copy-start(bf16[256,256]{1,0:T(8,128)(2,1)} %lk_ref.1) | copy-start | bytes 393220
  8.8 5.4 %copy-start.5 = (bf16[256,256]{1,0:T(8,128)(2,1)S(1)}, bf16[256,256]{1,0:T(8,128)(2,1)}, u32[]{:S(2)}) copy-start(bf16[256,256]{1,0:T(8,128)(2,1)} %fr_ref.1) | copy-start | bytes 393220
  8.8 5.4 %copy-start.6 = (f32[8,256]{1,0:T(8,128)S(1)}, f32[8,256]{1,0:T(8,128)}, u32[]{:S(2)}) copy-start(f32[8,256]{1,0:T(8,128)} %fall_ref.7) | copy-start | bytes 24580
  8.8 5.4 %copy-start.7 = (s32[8,8,1,64]{3,2,1,0:T(1,128)S(1)}, s32[8,8,1,64]{3,2,1,0:T(1,128)}, u32[]{:S(2)}) copy-start(s32[8,8,1,64]{3,2,1,0:T(1,128)} %target_any.1) | copy-start | bytes 49156
  8.8 5.4 %copy-start.8 = (s32[1,1,1,64,16]{3,4,2,1,0:T(8,128)S(1)}, s32[1,1,1,64,16]{3,4,2,1,0:T(8,128)}, u32[]{:S(2)}) copy-start(s32[1,1,1,64,16]{3,4,2,1,0:T(8,128)} %param.14) | copy-start | bytes 12292
  22.4 11.8 %collective-permute-start.8 = (bf16[576,256]{1,0:T(8,128)(2,1)S(1)}, bf16[576,256]{1,0:T(8,128)(2,1)S(1)}, u32[]{:S(2)}, u32[]{:S(2)}) collective-permute-start(bf16[576,256]{1,0:T(8,128)(2,1)S(1)} %get-tuple-element.21), channel_id=1, source_target_pairs={{3,0},{7,4},{11,8},{15,12},{19,16},{23,20},{27,24},{31,28},{35,32}... | collective-permute-start | bytes 884744 | tf_op jit(solution)/shard_map/ppermute | solution.py:547
  23.7 6.1 %collective-permute-start.7 = (bf16[560,256]{1,0:T(8,128)(2,1)S(1)}, bf16[560,256]{1,0:T(8,128)(2,1)S(1)}, u32[]{:S(2)}, u32[]{:S(2)}) collective-permute-start(bf16[560,256]{1,0:T(8,128)(2,1)S(1)} %slice.7.own_ref), channel_id=1, source_target_pairs={{3,2},{2,1},{7,6},{6,5},{11,10},{10,9},{15,14},{14,13},{19,18},{18... | collective-permute-start | bytes 860168 | tf_op jit(solution)/shard_map/ppermute | solution.py:546
  27.8 12.2 %collective-permute-start.5 = (bf16[544,256]{1,0:T(8,128)(2,1)S(1)}, bf16[544,256]{1,0:T(8,128)(2,1)S(1)}, u32[]{:S(2)}, u32[]{:S(2)}) collective-permute-start(bf16[544,256]{1,0:T(8,128)(2,1)S(1)} %get-tuple-element.20), channel_id=1, source_target_pairs={{3,0},{7,4},{11,8},{15,12},{19,16},{23,20},{27,24},{31,28},{35,32}... | collective-permute-start | bytes 835592 | tf_op jit(solution)/shard_map/ppermute | solution.py:547
  29.1 8.0 %collective-permute-start.4 = (bf16[528,256]{1,0:T(8,128)(2,1)S(1)}, bf16[528,256]{1,0:T(8,128)(2,1)S(1)}, u32[]{:S(2)}, u32[]{:S(2)}) collective-permute-start(bf16[528,256]{1,0:T(8,128)(2,1)S(1)} %slice.6.own_ref), channel_id=1, source_target_pairs={{3,2},{2,1},{7,6},{6,5},{11,10},{10,9},{15,14},{14,13},{19,18},{18... | collective-permute-start | bytes 811016 | tf_op jit(solution)/shard_map/ppermute | solution.py:546
  34.3 9.1 %collective-permute-start.9 = (bf16[560,256]{1,0:T(8,128)(2,1)S(1)}, bf16[560,256]{1,0:T(8,128)(2,1)S(1)}, u32[]{:S(2)}, u32[]{:S(2)}) collective-permute-start(bf16[560,256]{1,0:T(8,128)(2,1)S(1)} %combine.3), channel_id=1, source_target_pairs={{1,0},{0,1},{5,4},{4,5},{9,8},{8,9},{13,12},{12,13},{17,16},{16,17... | collective-permute-start | bytes 860168 | tf_op jit(solution)/shard_map/ppermute | solution.py:555
  40.0 9.3 %collective-permute-start.6 = (bf16[528,256]{1,0:T(8,128)(2,1)S(1)}, bf16[528,256]{1,0:T(8,128)(2,1)S(1)}, u32[]{:S(2)}, u32[]{:S(2)}) collective-permute-start(bf16[528,256]{1,0:T(8,128)(2,1)S(1)} %combine.2), channel_id=1, source_target_pairs={{1,0},{0,1},{5,4},{4,5},{9,8},{8,9},{13,12},{12,13},{17,16},{16,17... | collective-permute-start | bytes 811016 | tf_op jit(solution)/shard_map/ppermute | solution.py:555

commit v5 on v4

--- a/solution.py
+++ b/solution.py
@@ -10,7 +10,7 @@
 F32 = jnp.float32
 BF16 = jnp.bfloat16
 LANES = 128
-GROUP = 4
+GROUP = 8
 GAIN_ROWS = 16
 MIB = 2**20
 VMEM = pl.BlockSpec(memory_space=pltpu.VMEM)
@@ -556,7 +556,7 @@
     front, back = ready
     shape = spectrum.shape
     out, rest = finish_front(zid, fall_rate, *front, local, shape, first, 4)
-    out = finish_back(zid, fall_rate, *back, rest, out, columns - first, 4)
+    out = finish_back(zid, fall_rate, *back, rest, out, columns - first, 8)
     return out
 
 

time: 51.4 us -> 51.7 us (level); the launches traced: 51.2 us -> 50.9 us
  transfers between devices with their start and end apart: 10 -> 10, of which waited for: 4 -> 4; matrix products, arithmetic and copies ran while one was open for 0% -> 0% of each run, Pallas kernels for 26% -> 25%
where the time goes in v5:
time: 51.7 us; the launch traced here: 50.9 us
  Pallas kernels  24.1 us (47%)
  starting transfers between devices  17 us (33%)
  waiting for transfers between devices  9.31 us (18%)
    pallas_call x1, Pallas kernels, cloud(): pl.pallas_call(cloud_kernel, out_shape=(pltpu.VMEM(adv.shape, F32), pltpu...  8.19 us
    ppermute x2, waiting for transfers between devices, begin(): b = lax.ppermute(flux, 'gz', [(3, 0)])  7.38 us
    ppermute x2, starting transfers between devices, body(): lax.ppermute(combine(zid, flux, a, b, n), 'gz', [(1, 0), (0, 1)])  5.49 us
    pallas_call x1, Pallas kernels, inner(): pl.pallas_call(inner_kernel, out_shape=pltpu.VMEM((nb // LANES, nx * ny *...  4.92 us
    pallas_call x1, Pallas kernels, finish_front(): pl.pallas_call(finish_front_kernel, out_shape=(jax.ShapeDtypeStruct(shape...  4.6 us
    ppermute x1, starting transfers between devices, body(): north = lax.ppermute(low_y, 'gy', [(b, a) for a, b in up_y])  3.94 us
    pallas_call x1, Pallas kernels, settle(): pl.pallas_call(settle_kernel, out_shape=(pltpu.HBM(adv.shape, F32), pltpu...  3.34 us
    ppermute x2, starting transfers between devices, begin(): b = lax.ppermute(flux, 'gz', [(3, 0)])  2.58 us
  transfers between devices with their start and end apart: 10, of which 4 were waited for; matrix products, arithmetic and copies ran while one was open for 0% of the time, Pallas kernels for 25%

profile of v5, /device:TPU:2, one launch (start us, length us, event | category | flops | bytes accessed | tf_op | source)
XLA Modules:
  0.0 50.9 jit_solution(18411859027201554197)
XLA Ops:
  0.0 1.1 %edges.1 = (bf16[1,32,8,256]{3,2,1,0:T(8,128)(2,1)S(1)}, bf16[1,32,8,256]{3,2,1,0:T(8,128)(2,1)S(1)}, bf16[32,1,8,256]{3,2,1,0:T(8,128)(2,1)S(1)}, bf16[32,1,8,256]{3,2,1,0:T(8,128)(2,1)S(1)}) custom-call(bf16[32,32,8,256]{3,2,1,0:T(8,128)(2,1)} %s_ref.1), custom_call_target="tpu_custom_call" | custom-call | tf_op jit(solution)/shard_map/edges/pallas_call | solution.py:45
  1.1 0.0 collective-permute-start
  1.2 1.7 %collective-permute-start.1 = (bf16[1,32,8,256]{3,2,1,0:T(8,128)(2,1)S(1)}, bf16[1,32,8,256]{3,2,1,0:T(8,128)(2,1)S(1)}, u32[]{:S(2)}, u32[]{:S(2)}) collective-permute-start(bf16[1,32,8,256]{3,2,1,0:T(8,128)(2,1)S(1)} %get-tuple-element.16), channel_id=1, source_target_pairs={{32,0},{64,32},{96,64},{128,96},{160,128},{192,160},{224,192},{0,2... | collective-permute-start | bytes 393224 | tf_op jit(solution)/shard_map/ppermute | solution.py:518
  2.9 1.9 %collective-permute-start.2 = (bf16[32,1,8,256]{3,2,1,0:T(8,128)(2,1)S(1)}, bf16[32,1,8,256]{3,2,1,0:T(8,128)(2,1)S(1)}, u32[]{:S(2)}, u32[]{:S(2)}) collective-permute-start(bf16[32,1,8,256]{3,2,1,0:T(8,128)(2,1)S(1)} %get-tuple-element.17), channel_id=1, source_target_pairs={{0,4},{4,8},{8,12},{12,16},{16,20},{20,24},{24,28},{28,0},{1,5},{5... | collective-permute-start | bytes 393224 | tf_op jit(solution)/shard_map/ppermute | solution.py:515
  4.8 3.9 %collective-permute-start.3 = (bf16[32,1,8,256]{3,2,1,0:T(8,128)(2,1)S(1)}, bf16[32,1,8,256]{3,2,1,0:T(8,128)(2,1)S(1)}, u32[]{:S(2)}, u32[]{:S(2)}) collective-permute-start(bf16[32,1,8,256]{3,2,1,0:T(8,128)(2,1)S(1)} %get-tuple-element.18), channel_id=1, source_target_pairs={{4,0},{8,4},{12,8},{16,12},{20,16},{24,20},{28,24},{0,28},{5,1},{9... | collective-permute-start | bytes 393224 | tf_op jit(solution)/shard_map/ppermute | solution.py:516
  8.8 0.0 copy-start
  8.8 0.0 copy-start.1
  8.8 0.0 copy-start.2
  8.8 0.0 copy-start.3
  8.8 0.0 copy-start.4
  8.8 0.0 copy-start.5
  8.8 0.0 copy-start.6
  8.8 0.0 copy-start.7
  8.8 0.0 copy-start.8
  8.8 4.9 %inner.1.adv_in = f32[2,8192,128]{2,1,0:T(8,128)S(1)} custom-call(bf16[32,32,8,256]{3,2,1,0:T(8,128)(2,1)} %s_ref.1, f32[32,8,32]{2,1,0:T(8,128)} %bitcast.8, f32[32,8,32]{2,1,0:T(8,128)} %bitcast.10), custom_call_target="tpu_custom_call" | custom-call | flops 10000000 | bytes 16777216 | tf_op jit(solution)/shard_map/inner/pallas_call | solution.py:442
  13.8 0.1 pad_add_fusion.place_ref
  13.8 0.0 collective-permute-done.west_ref
  13.8 0.0 collective-permute-done.1.east_ref
  13.8 0.0 collective-permute-done.2.south_ref
  13.8 0.0 collective-permute-done.3.north_ref
  13.9 0.0 copy-done
  13.9 0.0 copy-done.1
  13.9 0.0 copy-done.2
  13.9 0.0 copy-done.3
  13.9 0.0 copy-done.4
  13.9 0.0 copy-done.5
  13.9 0.0 copy-done.6
  13.9 0.0 copy-done.7
  13.9 0.0 copy-done.8
  13.9 8.2 %cloud.1 = (f32[2,8192,128]{2,1,0:T(8,128)S(1)}, bf16[576,256]{1,0:T(8,128)(2,1)S(1)}) custom-call(s32[2]{0:T(128)S(1)} %pad_add_fusion.place_ref, s32[16,64]{1,0:T(8,128)S(1)} %bitcast.12, s32[8,8,1,64]{3,2,1,0:T(1,128)S(1)} %copy-done.7, f32[2,8192,128]{2,1,0:T(8,128)S(1)} %inner.1.adv_in, ...), custom_call_target="tpu_custom_call", output_to_operand_aliasing={{0}: (3, {})} | custom-call | tf_op jit(solution)/shard_map/cloud/pallas_call | solution.py:462
  22.1 1.3 %collective-permute-start.8 = (bf16[576,256]{1,0:T(8,128)(2,1)S(1)}, bf16[576,256]{1,0:T(8,128)(2,1)S(1)}, u32[]{:S(2)}, u32[]{:S(2)}) collective-permute-start(bf16[576,256]{1,0:T(8,128)(2,1)S(1)} %get-tuple-element.21), channel_id=1, source_target_pairs={{3,0},{7,4},{11,8},{15,12},{19,16},{23,20},{27,24},{31,28},{35,32}... | collective-permute-start | bytes 884744 | tf_op jit(solution)/shard_map/ppermute | solution.py:547
  23.5 0.7 %collective-permute-start.7 = (bf16[560,256]{1,0:T(8,128)(2,1)S(1)}, bf16[560,256]{1,0:T(8,128)(2,1)S(1)}, u32[]{:S(2)}, u32[]{:S(2)}) collective-permute-start(bf16[560,256]{1,0:T(8,128)(2,1)S(1)} %slice.7.own_ref), channel_id=1, source_target_pairs={{3,2},{2,1},{7,6},{6,5},{11,10},{10,9},{15,14},{14,13},{19,18},{18... | collective-permute-start | bytes 860168 | tf_op jit(solution)/shard_map/ppermute | solution.py:546
  24.2 3.3 %settle.1 = (f32[2,8192,128]{2,1,0:T(8,128)}, bf16[544,256]{1,0:T(8,128)(2,1)S(1)}) custom-call(f32[2,8192,128]{2,1,0:T(8,128)S(1)} %get-tuple-element.19.adv, f32[8,256]{1,0:T(8,128)S(1)} %copy-done.6), custom_call_target="tpu_custom_call" | custom-call | tf_op jit(solution)/shard_map/settle/pallas_call | solution.py:484
  27.5 1.3 %collective-permute-start.5 = (bf16[544,256]{1,0:T(8,128)(2,1)S(1)}, bf16[544,256]{1,0:T(8,128)(2,1)S(1)}, u32[]{:S(2)}, u32[]{:S(2)}) collective-permute-start(bf16[544,256]{1,0:T(8,128)(2,1)S(1)} %get-tuple-element.20), channel_id=1, source_target_pairs={{3,0},{7,4},{11,8},{15,12},{19,16},{23,20},{27,24},{31,28},{35,32}... | collective-permute-start | bytes 835592 | tf_op jit(solution)/shard_map/ppermute | solution.py:547
  28.8 0.7 %collective-permute-start.4 = (bf16[528,256]{1,0:T(8,128)(2,1)S(1)}, bf16[528,256]{1,0:T(8,128)(2,1)S(1)}, u32[]{:S(2)}, u32[]{:S(2)}) collective-permute-start(bf16[528,256]{1,0:T(8,128)(2,1)S(1)} %slice.6.own_ref), channel_id=1, source_target_pairs={{3,2},{2,1},{7,6},{6,5},{11,10},{10,9},{15,14},{14,13},{19,18},{18... | collective-permute-start | bytes 811016 | tf_op jit(solution)/shard_map/ppermute | solution.py:546
  29.5 0.0 collective-permute-done.7.a_ref
  29.5 4.5 %collective-permute-done.8.b_ref = bf16[576,256]{1,0:T(8,128)(2,1)S(1)} collective-permute-done((bf16[576,256]{1,0:T(8,128)(2,1)S(1)}, bf16[576,256]{1,0:T(8,128)(2,1)S(1)}, u32[]{:S(2)}, u32[]{:S(2)}) %collective-permute-start.8) | collective-permute-done | bytes 294944 | tf_op jit(solution)/shard_map/ppermute | solution.py:547
  34.0 2.8 %collective-permute-start.9 = (bf16[560,256]{1,0:T(8,128)(2,1)S(1)}, bf16[560,256]{1,0:T(8,128)(2,1)S(1)}, u32[]{:S(2)}, u32[]{:S(2)}) collective-permute-start(bf16[560,256]{1,0:T(8,128)(2,1)S(1)} %combine.3), channel_id=1, source_target_pairs={{1,0},{0,1},{5,4},{4,5},{9,8},{8,9},{13,12},{12,13},{17,16},{16,17... | collective-permute-start | bytes 860168 | tf_op jit(solution)/shard_map/ppermute | solution.py:555
  36.8 0.0 collective-permute-done.4.a_ref
  36.8 2.9 %collective-permute-done.5.b_ref = bf16[544,256]{1,0:T(8,128)(2,1)S(1)} collective-permute-done((bf16[544,256]{1,0:T(8,128)(2,1)S(1)}, bf16[544,256]{1,0:T(8,128)(2,1)S(1)}, u32[]{:S(2)}, u32[]{:S(2)}) %collective-permute-start.5) | collective-permute-done | bytes 278560 | tf_op jit(solution)/shard_map/ppermute | solution.py:547
  39.7 2.7 %collective-permute-start.6 = (bf16[528,256]{1,0:T(8,128)(2,1)S(1)}, bf16[528,256]{1,0:T(8,128)(2,1)S(1)}, u32[]{:S(2)}, u32[]{:S(2)}) collective-permute-start(bf16[528,256]{1,0:T(8,128)(2,1)S(1)} %combine.2), channel_id=1, source_target_pairs={{1,0},{0,1},{5,4},{4,5},{9,8},{8,9},{13,12},{12,13},{17,16},{16,17... | collective-permute-start | bytes 811016 | tf_op jit(solution)/shard_map/ppermute | solution.py:555
  42.5 0.6 %collective-permute-done.9.d_ref = bf16[560,256]{1,0:T(8,128)(2,1)S(1)} collective-permute-done((bf16[560,256]{1,0:T(8,128)(2,1)S(1)}, bf16[560,256]{1,0:T(8,128)(2,1)S(1)}, u32[]{:S(2)}, u32[]{:S(2)}) %collective-permute-start.9) | collective-permute-done | bytes 286752 | tf_op jit(solution)/shard_map/ppermute | solution.py:555
  43.1 4.6 %finish_front.1 = (bf16[32,32,8,256]{3,2,1,0:T(8,128)(2,1)}, f32[2,4096,128]{2,1,0:T(8,128)S(1)}) custom-call(s32[1]{0:T(128)} %bitcast.zid_ref, f32[8,256]{1,0:T(8,128)S(1)} %copy-done.6, bf16[560,256]{1,0:T(8,128)(2,1)S(1)} %collective-permute-done.7.a_ref, bf16[576,256]{1,0:T(8,128)(2,1)S(1)} %collective-permute-done.8.b_ref, ...), custom_call_target="tpu_custom_call" | custom-call | tf_op jit(solution)/shard_map/finish_front/pallas_call | solution.py:413
  47.7 1.3 %collective-permute-done.6.d_ref = bf16[528,256]{1,0:T(8,128)(2,1)S(1)} collective-permute-done((bf16[528,256]{1,0:T(8,128)(2,1)S(1)}, bf16[528,256]{1,0:T(8,128)(2,1)S(1)}, u32[]{:S(2)}, u32[]{:S(2)}) %collective-permute-start.6) | collective-permute-done | bytes 270368 | tf_op jit(solution)/shard_map/ppermute | solution.py:555
  49.0 1.9 %finish_back.1 = bf16[32,32,8,256]{3,2,1,0:T(8,128)(2,1)} custom-call(s32[1]{0:T(128)} %bitcast.zid_ref, f32[8,256]{1,0:T(8,128)S(1)} %copy-done.6, bf16[528,256]{1,0:T(8,128)(2,1)S(1)} %collective-permute-done.4.a_ref, bf16[544,256]{1,0:T(8,128)(2,1)S(1)} %collective-permute-done.5.b_ref, ...), custom_call_target="tpu_custom_call", output_to_operand_aliasing={{}: (6, {})} | custom-call | tf_op jit(solution)/shard_map/finish_back/pallas_call | solution.py:428
  (4 shorter events, 0.1 us)
Async XLA Ops:
  1.1 12.7 %collective-permute-start = (bf16[1,32,8,256]{3,2,1,0:T(8,128)(2,1)S(1)}, bf16[1,32,8,256]{3,2,1,0:T(8,128)(2,1)S(1)}, u32[]{:S(2)}, u32[]{:S(2)}) collective-permute-start(bf16[1,32,8,256]{3,2,1,0:T(8,128)(2,1)S(1)} %get-tuple-element.15), channel_id=1, source_target_pairs={{0,32},{32,64},{64,96},{96,128},{128,160},{160,192},{192,224},{224... | collective-permute-start | bytes 393224 | tf_op jit(solution)/shard_map/ppermute | solution.py:517
  1.2 12.7 %collective-permute-start.1 = (bf16[1,32,8,256]{3,2,1,0:T(8,128)(2,1)S(1)}, bf16[1,32,8,256]{3,2,1,0:T(8,128)(2,1)S(1)}, u32[]{:S(2)}, u32[]{:S(2)}) collective-permute-start(bf16[1,32,8,256]{3,2,1,0:T(8,128)(2,1)S(1)} %get-tuple-element.16), channel_id=1, source_target_pairs={{32,0},{64,32},{96,64},{128,96},{160,128},{192,160},{224,192},{0,2... | collective-permute-start | bytes 393224 | tf_op jit(solution)/shard_map/ppermute | solution.py:518
  2.9 10.9 %collective-permute-start.2 = (bf16[32,1,8,256]{3,2,1,0:T(8,128)(2,1)S(1)}, bf16[32,1,8,256]{3,2,1,0:T(8,128)(2,1)S(1)}, u32[]{:S(2)}, u32[]{:S(2)}) collective-permute-start(bf16[32,1,8,256]{3,2,1,0:T(8,128)(2,1)S(1)} %get-tuple-element.17), channel_id=1, source_target_pairs={{0,4},{4,8},{8,12},{12,16},{16,20},{20,24},{24,28},{28,0},{1,5},{5... | collective-permute-start | bytes 393224 | tf_op jit(solution)/shard_map/ppermute | solution.py:515
  4.8 9.0 %collective-permute-start.3 = (bf16[32,1,8,256]{3,2,1,0:T(8,128)(2,1)S(1)}, bf16[32,1,8,256]{3,2,1,0:T(8,128)(2,1)S(1)}, u32[]{:S(2)}, u32[]{:S(2)}) collective-permute-start(bf16[32,1,8,256]{3,2,1,0:T(8,128)(2,1)S(1)} %get-tuple-element.18), channel_id=1, source_target_pairs={{4,0},{8,4},{12,8},{16,12},{20,16},{24,20},{28,24},{0,28},{5,1},{9... | collective-permute-start | bytes 393224 | tf_op jit(solution)/shard_map/ppermute | solution.py:516
  8.8 5.1 %copy-start = (bf16[256,2048]{1,0:T(8,128)(2,1)S(1)}, bf16[256,2048]{1,0:T(8,128)(2,1)}, u32[]{:S(2)}) copy-start(bf16[256,2048]{1,0:T(8,128)(2,1)} %pi_ref.1) | copy-start | bytes 3145732
  8.8 5.1 %copy-start.1 = (f32[32,32,8]{1,2,0:T(8,128)S(1)}, f32[32,32,8]{1,2,0:T(8,128)}, u32[]{:S(2)}) copy-start(f32[32,32,8]{1,2,0:T(8,128)} %param.11) | copy-start | bytes 98308
  8.8 5.1 %copy-start.2 = (f32[32,32,8]{1,2,0:T(8,128)S(1)}, f32[32,32,8]{1,2,0:T(8,128)}, u32[]{:S(2)}) copy-start(f32[32,32,8]{1,2,0:T(8,128)} %param.12) | copy-start | bytes 98308
  8.8 5.1 %copy-start.3 = (bf16[1024,256]{1,0:T(8,128)(2,1)S(1)}, bf16[1024,256]{1,0:T(8,128)(2,1)}, u32[]{:S(2)}) copy-start(bf16[1024,256]{1,0:T(8,128)(2,1)} %po_ref.1) | copy-start | bytes 1572868
  8.8 5.1 %copy-start.4 = (bf16[256,256]{1,0:T(8,128)(2,1)S(1)}, bf16[256,256]{1,0:T(8,128)(2,1)}, u32[]{:S(2)}) copy-start(bf16[256,256]{1,0:T(8,128)(2,1)} %lk_ref.1) | copy-start | bytes 393220
  8.8 5.1 %copy-start.5 = (bf16[256,256]{1,0:T(8,128)(2,1)S(1)}, bf16[256,256]{1,0:T(8,128)(2,1)}, u32[]{:S(2)}) copy-start(bf16[256,256]{1,0:T(8,128)(2,1)} %fr_ref.1) | copy-start | bytes 393220
  8.8 5.1 %copy-start.6 = (f32[8,256]{1,0:T(8,128)S(1)}, f32[8,256]{1,0:T(8,128)}, u32[]{:S(2)}) copy-start(f32[8,256]{1,0:T(8,128)} %fall_ref.7) | copy-start | bytes 24580
  8.8 5.1 %copy-start.7 = (s32[8,8,1,64]{3,2,1,0:T(1,128)S(1)}, s32[8,8,1,64]{3,2,1,0:T(1,128)}, u32[]{:S(2)}) copy-start(s32[8,8,1,64]{3,2,1,0:T(1,128)} %target_any.1) | copy-start | bytes 49156
  8.8 5.1 %copy-start.8 = (s32[1,1,1,64,16]{3,4,2,1,0:T(8,128)S(1)}, s32[1,1,1,64,16]{3,4,2,1,0:T(8,128)}, u32[]{:S(2)}) copy-start(s32[1,1,1,64,16]{3,4,2,1,0:T(8,128)} %param.14) | copy-start | bytes 12292
  22.1 11.8 %collective-permute-start.8 = (bf16[576,256]{1,0:T(8,128)(2,1)S(1)}, bf16[576,256]{1,0:T(8,128)(2,1)S(1)}, u32[]{:S(2)}, u32[]{:S(2)}) collective-permute-start(bf16[576,256]{1,0:T(8,128)(2,1)S(1)} %get-tuple-element.21), channel_id=1, source_target_pairs={{3,0},{7,4},{11,8},{15,12},{19,16},{23,20},{27,24},{31,28},{35,32}... | collective-permute-start | bytes 884744 | tf_op jit(solution)/shard_map/ppermute | solution.py:547
  23.5 6.1 %collective-permute-start.7 = (bf16[560,256]{1,0:T(8,128)(2,1)S(1)}, bf16[560,256]{1,0:T(8,128)(2,1)S(1)}, u32[]{:S(2)}, u32[]{:S(2)}) collective-permute-start(bf16[560,256]{1,0:T(8,128)(2,1)S(1)} %slice.7.own_ref), channel_id=1, source_target_pairs={{3,2},{2,1},{7,6},{6,5},{11,10},{10,9},{15,14},{14,13},{19,18},{18... | collective-permute-start | bytes 860168 | tf_op jit(solution)/shard_map/ppermute | solution.py:546
  27.5 12.2 %collective-permute-start.5 = (bf16[544,256]{1,0:T(8,128)(2,1)S(1)}, bf16[544,256]{1,0:T(8,128)(2,1)S(1)}, u32[]{:S(2)}, u32[]{:S(2)}) collective-permute-start(bf16[544,256]{1,0:T(8,128)(2,1)S(1)} %get-tuple-element.20), channel_id=1, source_target_pairs={{3,0},{7,4},{11,8},{15,12},{19,16},{23,20},{27,24},{31,28},{35,32}... | collective-permute-start | bytes 835592 | tf_op jit(solution)/shard_map/ppermute | solution.py:547
  28.8 8.0 %collective-permute-start.4 = (bf16[528,256]{1,0:T(8,128)(2,1)S(1)}, bf16[528,256]{1,0:T(8,128)(2,1)S(1)}, u32[]{:S(2)}, u32[]{:S(2)}) collective-permute-start(bf16[528,256]{1,0:T(8,128)(2,1)S(1)} %slice.6.own_ref), channel_id=1, source_target_pairs={{3,2},{2,1},{7,6},{6,5},{11,10},{10,9},{15,14},{14,13},{19,18},{18... | collective-permute-start | bytes 811016 | tf_op jit(solution)/shard_map/ppermute | solution.py:546
  34.0 9.1 %collective-permute-start.9 = (bf16[560,256]{1,0:T(8,128)(2,1)S(1)}, bf16[560,256]{1,0:T(8,128)(2,1)S(1)}, u32[]{:S(2)}, u32[]{:S(2)}) collective-permute-start(bf16[560,256]{1,0:T(8,128)(2,1)S(1)} %combine.3), channel_id=1, source_target_pairs={{1,0},{0,1},{5,4},{4,5},{9,8},{8,9},{13,12},{12,13},{17,16},{16,17... | collective-permute-start | bytes 860168 | tf_op jit(solution)/shard_map/ppermute | solution.py:555
  39.7 9.3 %collective-permute-start.6 = (bf16[528,256]{1,0:T(8,128)(2,1)S(1)}, bf16[528,256]{1,0:T(8,128)(2,1)S(1)}, u32[]{:S(2)}, u32[]{:S(2)}) collective-permute-start(bf16[528,256]{1,0:T(8,128)(2,1)S(1)} %combine.2), channel_id=1, source_target_pairs={{1,0},{0,1},{5,4},{4,5},{9,8},{8,9},{13,12},{12,13},{17,16},{16,17... | collective-permute-start | bytes 811016 | tf_op jit(solution)/shard_map/ppermute | solution.py:555
